TPU v7x, 32 devices: a whole 2x2x4 slice. The times are simulated.
32 devices in a mesh: group: 8 (over z, x), row: 4 (over y, core).
Axes of the slice: x: 2, y: 2, z: 4, core: 2. Of those that a mesh axis runs over, the one named last changes fastest.
Arguments:
- video_frames: bfloat16 [32, 16, 192, 128], P('group', 'row'), may hold values from -6 to 6
- pred_owner: int32 [8], P('group'), may hold values from -1 to 6, as said below
- frame_counts: int32 [8], P('group'), may hold values from 2 to 4, as said below
- norm1_gain: float32 [128], replicated, may hold values from 0.1 to 1.9
- conv1_weight: bfloat16 [3, 3, 3, 128, 128], replicated, may hold values from -0.109375 to 0.109375
- conv1_bias: float32 [128], replicated, may hold values from -3 to 3
- norm2_gain: float32 [128], replicated, may hold values from 0.1 to 1.9
- conv2_weight: bfloat16 [3, 3, 3, 128, 256], replicated, may hold values from -0.109375 to 0.109375
- conv2_bias: float32 [256], replicated, may hold values from -3 to 3
Outputs:
- encoded: bfloat16 [16, 8, 96, 256], P('group', 'row')
Inputs may be any that keep to these rules, and one draw needn't show every extreme that they name: `pred_owner`: -1 marks a video's first group; otherwise it is the nearest earlier group of the same video, 1 to 4 groups earlier. No group is the predecessor of two groups. Group 0 has none. `frame_counts`: every count is even; a group that precedes another group holds 4 frames, only a video's last group may hold fewer.
All inputs are finite; a program needn't handle non-finite values.
Results may differ from a plain program's by a relative error of at most 0.0046.
Values may be sent and summed in bfloat16 or wider, within the bound.
No kernel may reach another device: no remote copies, remote signals or barrier semaphores. Data moves between devices by JAX's collectives and lax.ppermute only.
A program may use at most 64 MiB of HBM per device.

v0:
```python
import jax
import jax.numpy as jnp
from jax import lax
from jax.sharding import PartitionSpec as P

SPAN = 4


def shifted_2(value, axis, steps):
    count = lax.axis_size(axis)
    first, last = (max(0, -steps), min(count, count - steps))
    return lax.ppermute(value, axis, [(source, source + steps) for source in range(first, last)])


def extended_2(block, sides, width):
    for axis, dim in sides:
        count = lax.axis_size(axis)
        forward = [(i, i + 1) for i in range(count - 1)]
        backward = [(target, source) for source, target in forward]
        low = lax.ppermute(
            lax.slice_in_dim(block, block.shape[dim] - width, None, axis=dim), axis, forward
        )
        high = lax.ppermute(lax.slice_in_dim(block, 0, width, axis=dim), axis, backward)
        block = jnp.concatenate([low, block, high], axis=dim)
    return block


def prepare(values, norm_gain):
    values = values.astype(jnp.float32)
    inverse = lax.rsqrt(jnp.mean(values * values, axis=-1, keepdims=True) + 1e-06)
    return jax.nn.silu(values * inverse * norm_gain).astype(jnp.bfloat16)


def conv_steady(padded, weight, out_frames, out_rows):
    channels = padded.shape[-1]
    columns = padded.shape[2] - 2
    outputs = weight.shape[-1]
    summed = jnp.zeros((out_frames * out_rows * columns, outputs), jnp.float32)
    for step_t in range(3):
        for step_h in range(3):
            window = jnp.concatenate(
                [
                    padded[
                        step_t : step_t + out_frames,
                        step_h : step_h + out_rows,
                        step_w : step_w + columns,
                    ]
                    for step_w in range(3)
                ],
                axis=-1,
            )
            flattened = window.reshape(out_frames * out_rows * columns, 3 * channels)
            summed = summed + jnp.dot(
                flattened,
                weight[step_t, step_h].reshape(3 * channels, outputs),
                preferred_element_type=jnp.float32,
            )
    return summed.reshape(out_frames, out_rows, columns, outputs)


def conv_stride(padded, weight, out_frames, out_rows):
    channels = padded.shape[-1]
    out_cols = (padded.shape[2] - 2) // 2
    outputs = weight.shape[-1]
    summed = jnp.zeros((out_frames * out_rows * out_cols, outputs), jnp.float32)
    for step_t in range(3):
        for step_h in range(3):
            window = jnp.concatenate(
                [
                    padded[
                        step_t : step_t + 2 * out_frames : 2,
                        step_h : step_h + 2 * out_rows : 2,
                        step_w : step_w + 2 * out_cols : 2,
                    ]
                    for step_w in range(3)
                ],
                axis=-1,
            )
            flattened = window.reshape(out_frames * out_rows * out_cols, 3 * channels)
            summed = summed + jnp.dot(
                flattened,
                weight[step_t, step_h].reshape(3 * channels, outputs),
                preferred_element_type=jnp.float32,
            )
    return summed.reshape(out_frames, out_rows, out_cols, outputs)


def fetch_frames(tail_frames, distance):
    received = jnp.zeros_like(tail_frames)
    for offset in range(1, SPAN + 1):
        shifted = shifted_2(tail_frames, "group", offset)
        received = jnp.where(distance == offset, shifted, received)
    return received


def per_device(
    video_frames,
    pred_owner,
    frame_counts,
    norm1_gain,
    conv1_weight,
    conv1_bias,
    norm2_gain,
    conv2_weight,
    conv2_bias,
):
    valid_count = frame_counts[0]
    predecessor = pred_owner[0]
    position = lax.axis_index("group")
    distance = jnp.where(predecessor >= 0, position - predecessor, 0)
    frames_here = video_frames.shape[0]
    band_rows = video_frames.shape[1]
    halo_width = 1
    banded = extended_2(video_frames, (("row", 1),), halo_width)
    tail_frames = lax.dynamic_slice_in_dim(banded, valid_count - 2, 2, 0)
    extended = jnp.concatenate([fetch_frames(tail_frames, distance), banded], 0)
    hidden = prepare(extended, norm1_gain)
    out_rows = band_rows + halo_width - 1
    padded = jnp.pad(hidden, ((0, 0), (0, 0), (1, 1), (0, 0)))
    mixed = conv_steady(padded, conv1_weight, frames_here, out_rows)
    residual_rows = extended[2:, 1 : 1 + out_rows].astype(jnp.float32)
    second = prepare(residual_rows + mixed + conv1_bias, norm2_gain)
    tail_second = lax.dynamic_slice_in_dim(second, valid_count - 1, 1, 0)
    earlier = jnp.zeros_like(tail_second)
    for offset in range(1, SPAN + 1):
        shifted = shifted_2(tail_second, "group", offset)
        earlier = jnp.where(distance == offset, shifted, earlier)
    joined_second = jnp.concatenate([earlier, second], 0)
    above = shifted_2(joined_second[:, band_rows - 1 :], "row", 1)
    joined_second = jnp.concatenate([above, joined_second], 1)
    padded_second = jnp.pad(joined_second, ((0, 0), (0, 0), (1, 1), (0, 0)))
    mixed_second = (
        conv_stride(padded_second, conv2_weight, frames_here // 2, band_rows // 2) + conv2_bias
    )
    keep = jnp.arange(frames_here // 2) < valid_count // 2
    return jnp.where(keep[:, None, None, None], mixed_second, 0.0).astype(jnp.bfloat16)


def solution(mesh):
    placed = (P("group", "row", None, None), P("group"), P("group"), P(), P(), P(), P(), P(), P())
    return jax.shard_map(
        per_device,
        mesh=mesh,
        in_specs=placed,
        out_specs=P("group", "row", None, None),
        check_vma=False,
    )
```

profile of v0, /device:TPU:20, one launch (start us, length us, event | category | flops | bytes accessed | tf_op | source)
XLA Modules:
  0.0 179.0 jit_solution(13285813665323205382)
XLA Ops:
  1.1 1.9 %collective-permute-start = (bf16[4,1,192,128]{3,2,1,0:T(8,128)(2,1)S(1)}, bf16[4,1,192,128]{3,2,1,0:T(8,128)(2,1)S(1)}, u32[]{:S(2)}, u32[]{:S(2)}) collective-permute-start(bf16[4,1,192,128]{3,2,1,0:T(8,128)(2,1)S(1)} %get-tuple-element.51), channel_id=1, source_target_pairs={{0,1},{1,2},{2,3},{4,5},{5,6},{6,7},{8,9},{9,10},{10,11},{12,13},{... | collective-permute-start | bytes 589832 | tf_op jit(solution)/shard_map/ppermute | solution.py:20
  3.1 3.6 %collective-permute-start.1 = (bf16[4,1,192,128]{3,2,1,0:T(8,128)(2,1)S(1)}, bf16[4,1,192,128]{3,2,1,0:T(8,128)(2,1)S(1)}, u32[]{:S(2)}, u32[]{:S(2)}) collective-permute-start(bf16[4,1,192,128]{3,2,1,0:T(8,128)(2,1)S(1)} %get-tuple-element.50), channel_id=1, source_target_pairs={{1,0},{2,1},{3,2},{5,4},{6,5},{7,6},{9,8},{10,9},{11,10},{13,12},{... | collective-permute-start | bytes 589832 | tf_op jit(solution)/shard_map/ppermute | solution.py:23
  12.1 4.4 %collective-permute-start.3 = (bf16[2,6,192,128]{3,2,1,0:T(8,128)(2,1)}, bf16[2,6,192,128]{3,2,1,0:T(8,128)(2,1)S(1)}, u32[]{:S(2)}, u32[]{:S(2)}) collective-permute-start(bf16[2,6,192,128]{3,2,1,0:T(8,128)(2,1)} %constant_dynamic-slice_fusion.1), channel_id=1, source_target_pairs={{0,12},{4,16},{8,20},{12,24},{16,28},{1,13},{5,17},{9,21},{13,25},... | collective-permute-start | bytes 1769480 | tf_op jit(solution)/shard_map/ppermute | solution.py:12
  16.5 1.9 %collective-permute-start.4 = (bf16[2,6,192,128]{3,2,1,0:T(8,128)(2,1)}, bf16[2,6,192,128]{3,2,1,0:T(8,128)(2,1)}, u32[]{:S(2)}, u32[]{:S(2)}) collective-permute-start(bf16[2,6,192,128]{3,2,1,0:T(8,128)(2,1)} %constant_dynamic-slice_fusion.1), channel_id=1, source_target_pairs={{0,8},{4,12},{8,16},{12,20},{16,24},{20,28},{1,9},{5,13},{9,17},{1... | collective-permute-start | bytes 1769480 | tf_op jit(solution)/shard_map/ppermute | solution.py:12
  18.4 1.9 %collective-permute-start.5 = (bf16[2,6,192,128]{3,2,1,0:T(8,128)(2,1)}, bf16[2,6,192,128]{3,2,1,0:T(8,128)(2,1)}, u32[]{:S(2)}, u32[]{:S(2)}) collective-permute-start(bf16[2,6,192,128]{3,2,1,0:T(8,128)(2,1)} %constant_dynamic-slice_fusion.1), channel_id=1, source_target_pairs={{0,4},{4,8},{8,12},{12,16},{16,20},{20,24},{24,28},{1,5},{5,9},{9,... | collective-permute-start | bytes 1769480 | tf_op jit(solution)/shard_map/ppermute | solution.py:12
  21.1 8.9 %collective-permute-done.2 = bf16[2,6,192,128]{3,2,1,0:T(8,128)(2,1)S(1)} collective-permute-done((bf16[2,6,192,128]{3,2,1,0:T(8,128)(2,1)}, bf16[2,6,192,128]{3,2,1,0:T(8,128)(2,1)S(1)}, u32[]{:S(2)}, u32[]{:S(2)}) %collective-permute-start.2) | collective-permute-done | bytes 589856 | tf_op jit(solution)/shard_map/ppermute | solution.py:12
  30.1 13.6 %collective-permute-done.3 = bf16[2,6,192,128]{3,2,1,0:T(8,128)(2,1)S(1)} collective-permute-done((bf16[2,6,192,128]{3,2,1,0:T(8,128)(2,1)}, bf16[2,6,192,128]{3,2,1,0:T(8,128)(2,1)S(1)}, u32[]{:S(2)}, u32[]{:S(2)}) %collective-permute-start.3) | collective-permute-done | bytes 589856 | tf_op jit(solution)/shard_map/ppermute | solution.py:12
  43.6 21.0 %collective-permute-done.4 = bf16[2,6,192,128]{3,2,1,0:T(8,128)(2,1)} collective-permute-done((bf16[2,6,192,128]{3,2,1,0:T(8,128)(2,1)}, bf16[2,6,192,128]{3,2,1,0:T(8,128)(2,1)}, u32[]{:S(2)}, u32[]{:S(2)}) %collective-permute-start.4) | collective-permute-done | bytes 589856 | tf_op jit(solution)/shard_map/ppermute | solution.py:12
  64.7 26.2 %collective-permute-done.5 = bf16[2,6,192,128]{3,2,1,0:T(8,128)(2,1)} collective-permute-done((bf16[2,6,192,128]{3,2,1,0:T(8,128)(2,1)}, bf16[2,6,192,128]{3,2,1,0:T(8,128)(2,1)}, u32[]{:S(2)}, u32[]{:S(2)}) %collective-permute-start.5) | collective-permute-done | bytes 589856 | tf_op jit(solution)/shard_map/ppermute | solution.py:12
  93.7 3.2 %pad_slice_fusion.1 = (bf16[4,4,192,128]{3,2,1,0:T(8,128)(2,1)S(1)}, bf16[4,4,192,128]{3,2,1,0:T(8,128)(2,1)S(1)}, bf16[4,4,192,128]{3,2,1,0:T(8,128)(2,1)S(1)},...) fusion(bf16[6,6,192,128]{3,2,1,0:T(8,128)(2,1)S(1)} %fusion.7), kind=kLoop, calls=%fused_computation.69 | loop fusion | bytes 10420224 | tf_op jit(solution)/shard_map/slice | solution.py:43
  98.0 2.6 %pad_slice_fusion = (bf16[4,4,192,128]{3,2,1,0:T(8,128)(2,1)S(1)}, bf16[4,4,192,128]{3,2,1,0:T(8,128)(2,1)S(1)}, bf16[4,4,192,128]{3,2,1,0:T(8,128)(2,1)S(1)}, b...) fusion(bf16[6,6,192,128]{3,2,1,0:T(8,128)(2,1)S(1)} %fusion.7), kind=kLoop, calls=%fused_computation.68 | loop fusion | bytes 12779520 | tf_op jit(solution)/shard_map/slice | solution.py:43
  114.4 1.9 %collective-permute-start.7 = (bf16[1,4,192,128]{3,2,1,0:T(8,128)(2,1)S(1)}, bf16[1,4,192,128]{3,2,1,0:T(8,128)(2,1)S(1)}, u32[]{:S(2)}, u32[]{:S(2)}) collective-permute-start(bf16[1,4,192,128]{3,2,1,0:T(8,128)(2,1)S(1)} %constant_dynamic-slice_fusion), channel_id=1, source_target_pairs={{0,12},{4,16},{8,20},{12,24},{16,28},{1,13},{5,17},{9,21},{13,25},... | collective-permute-start | bytes 589832 | tf_op jit(solution)/shard_map/ppermute | solution.py:12
  116.4 1.9 %collective-permute-start.8 = (bf16[1,4,192,128]{3,2,1,0:T(8,128)(2,1)S(1)}, bf16[1,4,192,128]{3,2,1,0:T(8,128)(2,1)S(1)}, u32[]{:S(2)}, u32[]{:S(2)}) collective-permute-start(bf16[1,4,192,128]{3,2,1,0:T(8,128)(2,1)S(1)} %constant_dynamic-slice_fusion), channel_id=1, source_target_pairs={{0,8},{4,12},{8,16},{12,20},{16,24},{20,28},{1,9},{5,13},{9,17},{1... | collective-permute-start | bytes 589832 | tf_op jit(solution)/shard_map/ppermute | solution.py:12
  118.3 1.9 %collective-permute-start.9 = (bf16[1,4,192,128]{3,2,1,0:T(8,128)(2,1)S(1)}, bf16[1,4,192,128]{3,2,1,0:T(8,128)(2,1)S(1)}, u32[]{:S(2)}, u32[]{:S(2)}) collective-permute-start(bf16[1,4,192,128]{3,2,1,0:T(8,128)(2,1)S(1)} %constant_dynamic-slice_fusion), channel_id=1, source_target_pairs={{0,4},{4,8},{8,12},{12,16},{16,20},{20,24},{24,28},{1,5},{5,9},{9,... | collective-permute-start | bytes 589832 | tf_op jit(solution)/shard_map/ppermute | solution.py:12
  120.2 3.4 %collective-permute-done.6 = bf16[1,4,192,128]{3,2,1,0:T(8,128)(2,1)S(1)} collective-permute-done((bf16[1,4,192,128]{3,2,1,0:T(8,128)(2,1)S(1)}, bf16[1,4,192,128]{3,2,1,0:T(8,128)(2,1)S(1)}, u32[]{:S(2)}, u32[]{:S(2)}) %collective-permute-start.6) | collective-permute-done | bytes 196640 | tf_op jit(solution)/shard_map/ppermute | solution.py:12
  123.7 2.2 %collective-permute-done.7 = bf16[1,4,192,128]{3,2,1,0:T(8,128)(2,1)S(1)} collective-permute-done((bf16[1,4,192,128]{3,2,1,0:T(8,128)(2,1)S(1)}, bf16[1,4,192,128]{3,2,1,0:T(8,128)(2,1)S(1)}, u32[]{:S(2)}, u32[]{:S(2)}) %collective-permute-start.7) | collective-permute-done | bytes 196640 | tf_op jit(solution)/shard_map/ppermute | solution.py:12
  127.0 9.0 %collective-permute-done.9 = bf16[1,4,192,128]{3,2,1,0:T(8,128)(2,1)S(1)} collective-permute-done((bf16[1,4,192,128]{3,2,1,0:T(8,128)(2,1)S(1)}, bf16[1,4,192,128]{3,2,1,0:T(8,128)(2,1)S(1)}, u32[]{:S(2)}, u32[]{:S(2)}) %collective-permute-start.9) | collective-permute-done | bytes 196640 | tf_op jit(solution)/shard_map/ppermute | solution.py:12
  136.0 1.9 %collective-permute-start.10 = (bf16[5,1,192,128]{3,2,1,0:T(8,128)(2,1)S(1)}, bf16[5,1,192,128]{3,2,1,0:T(8,128)(2,1)S(1)}, u32[]{:S(2)}, u32[]{:S(2)}) collective-permute-start(bf16[5,1,192,128]{3,2,1,0:T(8,128)(2,1)S(1)} %pad_maximum_fusion.19), channel_id=1, source_target_pairs={{0,1},{1,2},{2,3},{4,5},{5,6},{6,7},{8,9},{9,10},{10,11},{12,13},{... | collective-permute-start | bytes 737288 | tf_op jit(solution)/shard_map/ppermute | solution.py:12
  138.9 4.6 %collective-permute-done.10 = bf16[5,1,192,128]{3,2,1,0:T(8,128)(2,1)S(1)} collective-permute-done((bf16[5,1,192,128]{3,2,1,0:T(8,128)(2,1)S(1)}, bf16[5,1,192,128]{3,2,1,0:T(8,128)(2,1)S(1)}, u32[]{:S(2)}, u32[]{:S(2)}) %collective-permute-start.10) | collective-permute-done | bytes 245792 | tf_op jit(solution)/shard_map/ppermute | solution.py:12
  152.3 1.4 slice.282
  153.7 1.4 slice.281
  162.9 1.6 slice.295
  164.5 1.4 slice.294
  165.9 1.4 slice.293
  (130 shorter events, 53.4 us)
Async XLA Ops:
  0.0 21.0 %copy-start.2 = (bf16[3,3,3,128,128]{4,3,2,1,0:T(8,128)(2,1)S(1)}, bf16[3,3,3,128,128]{4,3,2,1,0:T(8,128)(2,1)}, u32[]{:S(2)}) copy-start(bf16[3,3,3,128,128]{4,3,2,1,0:T(8,128)(2,1)} %param.13) | copy-start | bytes 2654212
  1.1 7.0 %collective-permute-start = (bf16[4,1,192,128]{3,2,1,0:T(8,128)(2,1)S(1)}, bf16[4,1,192,128]{3,2,1,0:T(8,128)(2,1)S(1)}, u32[]{:S(2)}, u32[]{:S(2)}) collective-permute-start(bf16[4,1,192,128]{3,2,1,0:T(8,128)(2,1)S(1)} %get-tuple-element.51), channel_id=1, source_target_pairs={{0,1},{1,2},{2,3},{4,5},{5,6},{6,7},{8,9},{9,10},{10,11},{12,13},{... | collective-permute-start | bytes 589832 | tf_op jit(solution)/shard_map/ppermute | solution.py:20
  3.1 6.8 %collective-permute-start.1 = (bf16[4,1,192,128]{3,2,1,0:T(8,128)(2,1)S(1)}, bf16[4,1,192,128]{3,2,1,0:T(8,128)(2,1)S(1)}, u32[]{:S(2)}, u32[]{:S(2)}) collective-permute-start(bf16[4,1,192,128]{3,2,1,0:T(8,128)(2,1)S(1)} %get-tuple-element.50), channel_id=1, source_target_pairs={{1,0},{2,1},{3,2},{5,4},{6,5},{7,6},{9,8},{10,9},{11,10},{13,12},{... | collective-permute-start | bytes 589832 | tf_op jit(solution)/shard_map/ppermute | solution.py:23
  10.8 19.3 %collective-permute-start.2 = (bf16[2,6,192,128]{3,2,1,0:T(8,128)(2,1)}, bf16[2,6,192,128]{3,2,1,0:T(8,128)(2,1)S(1)}, u32[]{:S(2)}, u32[]{:S(2)}) collective-permute-start(bf16[2,6,192,128]{3,2,1,0:T(8,128)(2,1)} %constant_dynamic-slice_fusion.1), channel_id=1, source_target_pairs={{0,16},{4,20},{8,24},{12,28},{1,17},{5,21},{9,25},{13,29},{2,18},{... | collective-permute-start | bytes 1769480 | tf_op jit(solution)/shard_map/ppermute | solution.py:12
  12.1 31.5 %collective-permute-start.3 = (bf16[2,6,192,128]{3,2,1,0:T(8,128)(2,1)}, bf16[2,6,192,128]{3,2,1,0:T(8,128)(2,1)S(1)}, u32[]{:S(2)}, u32[]{:S(2)}) collective-permute-start(bf16[2,6,192,128]{3,2,1,0:T(8,128)(2,1)} %constant_dynamic-slice_fusion.1), channel_id=1, source_target_pairs={{0,12},{4,16},{8,20},{12,24},{16,28},{1,13},{5,17},{9,21},{13,25},... | collective-permute-start | bytes 1769480 | tf_op jit(solution)/shard_map/ppermute | solution.py:12
  16.5 48.2 %collective-permute-start.4 = (bf16[2,6,192,128]{3,2,1,0:T(8,128)(2,1)}, bf16[2,6,192,128]{3,2,1,0:T(8,128)(2,1)}, u32[]{:S(2)}, u32[]{:S(2)}) collective-permute-start(bf16[2,6,192,128]{3,2,1,0:T(8,128)(2,1)} %constant_dynamic-slice_fusion.1), channel_id=1, source_target_pairs={{0,8},{4,12},{8,16},{12,20},{16,24},{20,28},{1,9},{5,13},{9,17},{1... | collective-permute-start | bytes 1769480 | tf_op jit(solution)/shard_map/ppermute | solution.py:12
  18.4 72.4 %collective-permute-start.5 = (bf16[2,6,192,128]{3,2,1,0:T(8,128)(2,1)}, bf16[2,6,192,128]{3,2,1,0:T(8,128)(2,1)}, u32[]{:S(2)}, u32[]{:S(2)}) collective-permute-start(bf16[2,6,192,128]{3,2,1,0:T(8,128)(2,1)} %constant_dynamic-slice_fusion.1), channel_id=1, source_target_pairs={{0,4},{4,8},{8,12},{12,16},{16,20},{20,24},{24,28},{1,5},{5,9},{9,... | collective-permute-start | bytes 1769480 | tf_op jit(solution)/shard_map/ppermute | solution.py:12
  21.1 71.2 %copy-start.24 = (f32[128]{0:T(128)S(1)}, f32[128]{0:T(128)}, u32[]{:S(2)}) copy-start(f32[128]{0:T(128)} %param.12) | copy-start | bytes 1540
  110.6 1.1 copy-start
  112.4 25.5 %copy-start.1 = (bf16[3,3,3,128,256]{4,3,2,1,0:T(8,128)(2,1)S(1)}, bf16[3,3,3,128,256]{4,3,2,1,0:T(8,128)(2,1)}, u32[]{:S(2)}) copy-start(bf16[3,3,3,128,256]{4,3,2,1,0:T(8,128)(2,1)} %param.16) | copy-start | bytes 5308420
  113.1 10.6 %collective-permute-start.6 = (bf16[1,4,192,128]{3,2,1,0:T(8,128)(2,1)S(1)}, bf16[1,4,192,128]{3,2,1,0:T(8,128)(2,1)S(1)}, u32[]{:S(2)}, u32[]{:S(2)}) collective-permute-start(bf16[1,4,192,128]{3,2,1,0:T(8,128)(2,1)S(1)} %constant_dynamic-slice_fusion), channel_id=1, source_target_pairs={{0,16},{4,20},{8,24},{12,28},{1,17},{5,21},{9,25},{13,29},{2,18},{... | collective-permute-start | bytes 589832 | tf_op jit(solution)/shard_map/ppermute | solution.py:12
  114.4 11.5 %collective-permute-start.7 = (bf16[1,4,192,128]{3,2,1,0:T(8,128)(2,1)S(1)}, bf16[1,4,192,128]{3,2,1,0:T(8,128)(2,1)S(1)}, u32[]{:S(2)}, u32[]{:S(2)}) collective-permute-start(bf16[1,4,192,128]{3,2,1,0:T(8,128)(2,1)S(1)} %constant_dynamic-slice_fusion), channel_id=1, source_target_pairs={{0,12},{4,16},{8,20},{12,24},{16,28},{1,13},{5,17},{9,21},{13,25},... | collective-permute-start | bytes 589832 | tf_op jit(solution)/shard_map/ppermute | solution.py:12
  116.4 10.6 %collective-permute-start.8 = (bf16[1,4,192,128]{3,2,1,0:T(8,128)(2,1)S(1)}, bf16[1,4,192,128]{3,2,1,0:T(8,128)(2,1)S(1)}, u32[]{:S(2)}, u32[]{:S(2)}) collective-permute-start(bf16[1,4,192,128]{3,2,1,0:T(8,128)(2,1)S(1)} %constant_dynamic-slice_fusion), channel_id=1, source_target_pairs={{0,8},{4,12},{8,16},{12,20},{16,24},{20,28},{1,9},{5,13},{9,17},{1... | collective-permute-start | bytes 589832 | tf_op jit(solution)/shard_map/ppermute | solution.py:12
  118.3 17.6 %collective-permute-start.9 = (bf16[1,4,192,128]{3,2,1,0:T(8,128)(2,1)S(1)}, bf16[1,4,192,128]{3,2,1,0:T(8,128)(2,1)S(1)}, u32[]{:S(2)}, u32[]{:S(2)}) collective-permute-start(bf16[1,4,192,128]{3,2,1,0:T(8,128)(2,1)S(1)} %constant_dynamic-slice_fusion), channel_id=1, source_target_pairs={{0,4},{4,8},{8,12},{12,16},{16,20},{20,24},{24,28},{1,5},{5,9},{9,... | collective-permute-start | bytes 589832 | tf_op jit(solution)/shard_map/ppermute | solution.py:12
  136.0 7.5 %collective-permute-start.10 = (bf16[5,1,192,128]{3,2,1,0:T(8,128)(2,1)S(1)}, bf16[5,1,192,128]{3,2,1,0:T(8,128)(2,1)S(1)}, u32[]{:S(2)}, u32[]{:S(2)}) collective-permute-start(bf16[5,1,192,128]{3,2,1,0:T(8,128)(2,1)S(1)} %pad_maximum_fusion.19), channel_id=1, source_target_pairs={{0,1},{1,2},{2,3},{4,5},{5,6},{6,7},{8,9},{9,10},{10,11},{12,13},{... | collective-permute-start | bytes 737288 | tf_op jit(solution)/shard_map/ppermute | solution.py:12
  151.8 22.3 %copy-start.6 = (bf16[1,1,3,128,256]{4,3,2,1,0:T(8,128)(2,1)S(1)}, bf16[1,1,3,128,256]{4,3,2,1,0:T(8,128)(2,1)}, u32[]{:S(2)}) copy-start(bf16[1,1,3,128,256]{4,3,2,1,0:T(8,128)(2,1)} %get-tuple-element.12) | copy-start | bytes 589828
  161.6 13.8 %copy-start.5 = (bf16[1,1,3,128,256]{4,3,2,1,0:T(8,128)(2,1)S(1)}, bf16[1,1,3,128,256]{4,3,2,1,0:T(8,128)(2,1)}, u32[]{:S(2)}) copy-start(bf16[1,1,3,128,256]{4,3,2,1,0:T(8,128)(2,1)} %get-tuple-element.11) | copy-start | bytes 589828
  171.6 4.2 %copy-start.4 = (bf16[1,1,3,128,256]{4,3,2,1,0:T(8,128)(2,1)S(1)}, bf16[1,1,3,128,256]{4,3,2,1,0:T(8,128)(2,1)}, u32[]{:S(2)}) copy-start(bf16[1,1,3,128,256]{4,3,2,1,0:T(8,128)(2,1)} %get-tuple-element.10) | copy-start | bytes 589828
  173.0 2.8 %copy-start.19 = (bf16[2,2,96,128]{3,2,1,0:T(8,128)(2,1)S(1)}, bf16[2,2,96,128]{3,2,1,0:T(8,128)(2,1)}, u32[]{:S(2)}) copy-start(bf16[2,2,96,128]{3,2,1,0:T(8,128)(2,1)} %slice.282) | copy-start | bytes 294916
  173.0 2.8 %copy-start.20 = (bf16[2,2,96,128]{3,2,1,0:T(8,128)(2,1)S(1)}, bf16[2,2,96,128]{3,2,1,0:T(8,128)(2,1)}, u32[]{:S(2)}) copy-start(bf16[2,2,96,128]{3,2,1,0:T(8,128)(2,1)} %slice.281) | copy-start | bytes 294916
  174.1 2.1 %copy-start.16 = (bf16[2,2,96,128]{3,2,1,0:T(8,128)(2,1)S(1)}, bf16[2,2,96,128]{3,2,1,0:T(8,128)(2,1)}, u32[]{:S(2)}) copy-start(bf16[2,2,96,128]{3,2,1,0:T(8,128)(2,1)} %slice.287) | copy-start | bytes 294916
  174.1 2.1 %copy-start.17 = (bf16[2,2,96,128]{3,2,1,0:T(8,128)(2,1)S(1)}, bf16[2,2,96,128]{3,2,1,0:T(8,128)(2,1)}, u32[]{:S(2)}) copy-start(bf16[2,2,96,128]{3,2,1,0:T(8,128)(2,1)} %slice.286) | copy-start | bytes 294916
  174.1 2.1 %copy-start.18 = (bf16[2,2,96,128]{3,2,1,0:T(8,128)(2,1)S(1)}, bf16[2,2,96,128]{3,2,1,0:T(8,128)(2,1)}, u32[]{:S(2)}) copy-start(bf16[2,2,96,128]{3,2,1,0:T(8,128)(2,1)} %slice.285) | copy-start | bytes 294916
  174.4 1.8 %copy-start.3 = (bf16[1,1,3,128,256]{4,3,2,1,0:T(8,128)(2,1)S(1)}, bf16[1,1,3,128,256]{4,3,2,1,0:T(8,128)(2,1)}, u32[]{:S(2)}) copy-start(bf16[1,1,3,128,256]{4,3,2,1,0:T(8,128)(2,1)} %get-tuple-element.9) | copy-start | bytes 589828
  (12 other events, 12.1 us)
where the time goes:
time: 180 us; the launch traced here: 179 us
  waiting for transfers between devices  91.3 us (51%)
  local copies, waits for them, and re-layouts  40.7 us (23%)
  starting transfers between devices  24.1 us (13%)
  other arithmetic  11.1 us (6%)
  matrix products  9.58 us (5%)
  between operations  2.21 us (1%)
    ppermute x9, waiting for transfers between devices, shifted_2(): lax.ppermute(value, axis, [(source, source + steps) for source in range(f...  90 us
    slice x27, local copies, waits for them, and re-layouts, conv_stride(): padded[step_t:step_t + 2 * out_frames:2, step_h:step_h + 2 * out_rows:2,...  29 us
    ppermute x9, starting transfers between devices, shifted_2(): lax.ppermute(value, axis, [(source, source + steps) for source in range(f...  18.5 us
    dot_general x9, matrix products, conv_steady(): jnp.dot(flattened, weight[step_t, step_h].reshape(3 * channels, outputs),...  7.29 us
    slice x3, local copies, waits for them, and re-layouts, conv_steady(): padded[step_t:step_t + out_frames, step_h:step_h + out_rows, step_w:step_...  6.92 us
    ppermute x1, starting transfers between devices, extended_2(): lax.ppermute(lax.slice_in_dim(block, 0, width, axis=dim), axis, backward)  3.64 us
  transfers between devices with their start and end apart: 11, of which 11 were waited for; matrix products, arithmetic and copies ran while one was open for 1% of the time, Pallas kernels for 0%

commit v1 on v0

v1 whole, which is shorter than its diff:
```python
import functools

import jax
import jax.numpy as jnp
from jax import lax
from jax.experimental import pallas as pl
from jax.experimental.pallas import tpu as pltpu
from jax.sharding import PartitionSpec as P

ABOVE = 2
VMEM = pltpu.VMEM
SMEM = pltpu.SMEM
F32 = jnp.float32
BF16 = jnp.bfloat16


def shifted(value, axis, steps):
    count = lax.axis_size(axis)
    first, last = (max(0, -steps), min(count, count - steps))
    return lax.ppermute(value, axis, [(source, source + steps) for source in range(first, last)])


def swapped(value, axis, offset):
    count = lax.axis_size(axis)
    pairs = []
    for low in range(offset, count - 1, 2):
        pairs += [(low, low + 1), (low + 1, low)]
    return lax.ppermute(value, axis, pairs)


def pixel_silu(values, gain):
    inverse = lax.rsqrt(jnp.mean(values * values, axis=-1, keepdims=True) + 1e-06)
    half = values * inverse * (0.5 * gain)
    return half + half * jnp.tanh(half)


def column_window(row):
    width = row.shape[0]
    column = lax.broadcasted_iota(jnp.int32, row.shape, 0)
    left = jnp.where(column == 0, 0.0, pltpu.roll(row, 1, 0))
    right = jnp.where(column == width - 1, 0.0, pltpu.roll(row, width - 1, 0))
    return jnp.concatenate([left.astype(BF16), row.astype(BF16), right.astype(BF16)], axis=-1)


def fill_hidden(read, gain, window_ref, frame, rows):
    for row in range(rows):
        window_ref[frame, row] = column_window(pixel_silu(read(row), gain))


def conv1_rows(window_ref, frame, rows, weight):
    width, depth = window_ref.shape[2], window_ref.shape[3]
    total = None
    for tap in range(3):
        part = jnp.dot(
            window_ref[frame, tap : tap + rows].reshape(rows * width, depth),
            weight(tap),
            preferred_element_type=F32,
        )
        total = part if total is None else total + part
    return total


def fill_second(values, gain, first_row, stage_ref, strided_ref, slot):
    rows, half = strided_ref.shape[1], strided_ref.shape[2]
    width, channels = 2 * half, stage_ref.shape[2]
    for row in range(rows):
        ready = pixel_silu(values(row), gain).astype(BF16).astype(F32)
        if row == 0:
            ready = jnp.where(first_row, 0.0, ready)
        stage_ref[row, 0:8] = jnp.zeros((8, channels), F32)
        stage_ref[row, 8 : 8 + width] = ready
        strided_ref[slot, row] = jnp.concatenate(
            [stage_ref[row, pl.ds(7 + tap, half, stride=2), :].astype(BF16) for tap in range(3)],
            axis=-1,
        )


def conv2_frame(strided_ref, slot, weight_ref, step):
    total = None
    for tap in range(3):
        window = jnp.concatenate([strided_ref[slot, tap], strided_ref[slot, tap + 2]], axis=0)
        part = jnp.dot(window, weight_ref[step, tap], preferred_element_type=F32)
        total = part if total is None else total + part
    return total


def pick_rows(even, first, second):
    return jnp.where(even, first, second)


def row_reader(video_ref, frame, pair_ref, cross_ref, even):
    def read(row):
        if row < ABOVE:
            return jnp.where(even, cross_ref[frame, row].astype(F32), pair_ref[frame, row].astype(F32))
        if row < ABOVE + 4:
            return video_ref[frame, row - ABOVE].astype(F32)
        return jnp.where(even, pair_ref[frame, 0].astype(F32), cross_ref[frame, 0].astype(F32))

    return read


def send_kernel(
    flag_ref, video_ref, pair_ref, cross_ref, gain1_ref, weight1_ref, bias1_ref, gain2_ref,
    weight2_ref, prior_ref, tail_ref, strided_out_ref, window_ref, stage_ref, total_ref,
):
    even, first_row = flag_ref[0] == 1, flag_ref[1] == 1
    width = video_ref.shape[2]
    channels = video_ref.shape[3]
    readers = [row_reader(video_ref, f, pair_ref, cross_ref, even) for f in range(4)]
    for slot, frame in enumerate((1, 2, 3)):
        fill_hidden(readers[frame], gain1_ref[...], window_ref, slot, 7)
    both = conv1_rows(
        window_ref, 1, 5,
        lambda tap: jnp.concatenate([weight1_ref[1, tap], weight1_ref[0, tap]], axis=-1),
    )
    prior_ref[...] = both[:, channels:].astype(BF16).reshape(prior_ref.shape)
    total_ref[...] = (
        both[:, :channels]
        + conv1_rows(window_ref, 0, 5, lambda tap: weight1_ref[0, tap])
        + conv1_rows(window_ref, 2, 5, lambda tap: weight1_ref[2, tap])
    ).reshape(total_ref.shape)
    fill_second(
        lambda row: total_ref[row] + readers[3](row + 1) + bias1_ref[...],
        gain2_ref[...], first_row, stage_ref, strided_out_ref, 0,
    )
    tail_ref[...] = conv2_frame(strided_out_ref, 0, weight2_ref, 0).astype(BF16).reshape(tail_ref.shape)


def own_kernel(
    flag_ref, video_ref, pair_ref, cross_ref, gain1_ref, weight1_ref, bias1_ref, gain2_ref,
    weight2_ref, bias2_ref, strided3_ref, first_ref, next_ref, late_ref,
    window_ref, stage_ref, strided_ref, total_ref,
):
    even, first_row = flag_ref[0] == 1, flag_ref[1] == 1
    width = video_ref.shape[2]
    channels = video_ref.shape[3]
    readers = [row_reader(video_ref, f, pair_ref, cross_ref, even) for f in range(4)]
    for frame in range(3):
        fill_hidden(readers[frame], gain1_ref[...], window_ref, frame, 7)
    both = conv1_rows(
        window_ref, 0, 5,
        lambda tap: jnp.concatenate([weight1_ref[0, tap], weight1_ref[1, tap]], axis=-1),
    ) + conv1_rows(
        window_ref, 1, 5,
        lambda tap: jnp.concatenate([weight1_ref[1, tap], weight1_ref[2, tap]], axis=-1),
    )
    next_ref[...] = both[:, channels:].reshape(next_ref.shape)
    total_ref[...] = (
        both[:, :channels] + conv1_rows(window_ref, 2, 5, lambda tap: weight1_ref[2, tap])
    ).reshape(total_ref.shape)
    first_ref[...] = conv1_rows(window_ref, 0, 5, lambda tap: weight1_ref[2, tap]).reshape(first_ref.shape)
    for row in range(5):
        next_ref[row] += readers[1](row + 1) + bias1_ref[...]
        first_ref[row] += readers[0](row + 1) + bias1_ref[...]
    fill_second(
        lambda row: total_ref[row] + readers[2](row + 1) + bias1_ref[...],
        gain2_ref[...], first_row, stage_ref, strided_ref, 0,
    )
    late_ref[...] = (
        conv2_frame(strided_ref, 0, weight2_ref, 1)
        + conv2_frame(strided3_ref, 0, weight2_ref, 2)
        + bias2_ref[...]
    )


def next_kernel(
    flag_ref, prior_ref, pair_ref, cross_ref, gain1_ref, weight1_ref, gain2_ref,
    weight2_ref, bias2_ref, first_ref, next_ref, late_ref, second_out_ref, first_out_ref, early_ref,
    window_ref, stage_ref, strided_ref, total_ref,
):
    even, first_row, keep = flag_ref[0] == 1, flag_ref[1] == 1, flag_ref[2] == 1
    channels = prior_ref.shape[3]
    fill_hidden(
        row_reader(prior_ref, 0, pair_ref, cross_ref, even), gain1_ref[...], window_ref, 0, 7
    )
    both = conv1_rows(
        window_ref, 0, 5,
        lambda tap: jnp.concatenate([weight1_ref[0, tap], weight1_ref[1, tap]], axis=-1),
    )
    total_ref[...] = both[:, :channels].reshape(total_ref.shape)
    first_out_ref[...] = first_ref[...] + both[:, channels:].reshape(first_ref.shape)
    fill_second(
        lambda row: total_ref[row] + next_ref[row],
        gain2_ref[...], first_row, stage_ref, strided_ref, 0,
    )
    late = late_ref[...] + conv2_frame(strided_ref, 0, weight2_ref, 0)
    second_out_ref[...] = jnp.where(keep, late, 0.0).astype(BF16).reshape(second_out_ref.shape)
    early_ref[...] = conv2_frame(strided_ref, 0, weight2_ref, 2) + bias2_ref[...]


def last_kernel(
    flag_ref, prior_a_ref, prior_b_ref, prior_c_ref, tail_a_ref, tail_b_ref, tail_c_ref,
    gain2_ref, weight2_ref, first_ref, early_ref, done_ref, out_ref, stage_ref, strided_ref,
):
    first_row, distance = flag_ref[1] == 1, flag_ref[3]

    def chosen(two, four, odd):
        value = jnp.where(distance == 2, two.astype(F32), odd.astype(F32))
        value = jnp.where(distance == 4, four.astype(F32), value)
        return jnp.where(distance == 0, 0.0, value)

    fill_second(
        lambda row: first_ref[row] + chosen(prior_a_ref[row], prior_b_ref[row], prior_c_ref[row]),
        gain2_ref[...], first_row, stage_ref, strided_ref, 0,
    )
    early = early_ref[...] + conv2_frame(strided_ref, 0, weight2_ref, 0)
    shape = tail_a_ref.shape
    tail = chosen(tail_a_ref[...], tail_b_ref[...], tail_c_ref[...])
    out_ref[0] = (early.reshape(shape) + tail).astype(BF16)
    out_ref[1] = done_ref[...]


def whole(shape):
    return pl.BlockSpec(shape, lambda i: (0,) * len(shape))


def call(kernel, operands, outs, scratch, blocks=None, flops=0):
    specs = [pl.BlockSpec(memory_space=SMEM)]
    for index, operand in enumerate(operands[1:]):
        block = (blocks or {}).get(index + 1)
        specs.append(block if block is not None else whole(operand.shape))
    moved = sum(o.size * o.dtype.itemsize for o in list(operands) + list(outs))
    return pl.pallas_call(
        kernel,
        grid=(1,),
        out_shape=outs,
        in_specs=specs,
        out_specs=[whole(o.shape) for o in outs],
        scratch_shapes=scratch,
        compiler_params=pltpu.CompilerParams(vmem_limit_bytes=40 * 1024 * 1024),
        cost_estimate=pl.CostEstimate(flops=flops, bytes_accessed=moved, transcendentals=0),
    )(*operands)


def row_halo(frames, even, rows):
    low = lax.slice_in_dim(frames, rows - ABOVE, rows, axis=1)
    high = lax.slice_in_dim(frames, 0, ABOVE, axis=1)
    pair = swapped(jnp.where(even, low, high), "row", 0)
    cross = swapped(jnp.where(even, high, low), "row", 1)
    return pair, cross


def per_device(
    video_frames, pred_owner, frame_counts, norm1_gain, conv1_weight, conv1_bias, norm2_gain,
    conv2_weight, conv2_bias,
):
    frames, rows, width, channels = video_frames.shape
    wide = conv2_weight.shape[-1]
    half = width // 2
    position = lax.axis_index("group")
    band = lax.axis_index("row")
    distance = jnp.where(pred_owner >= 0, position - pred_owner, 0)
    even = band % 2 == 0
    even_group = position % 2 == 0
    keep = frame_counts >= frames
    flags = jnp.concatenate(
        [jnp.stack([even, band == 0]).astype(jnp.int32), keep.astype(jnp.int32), distance]
    )
    gain1, bias1 = norm1_gain[None], conv1_bias[None]
    gain2, bias2 = norm2_gain[None], conv2_bias[None]
    weight1 = conv1_weight.reshape(3, 3, 3 * channels, channels)
    weight2 = conv2_weight.reshape(3, 3, 3 * channels, wide)

    wanted = swapped(distance, "group", 0)[0]

    def for_partner(own, near, far):
        one = jnp.where(even_group, own, near)
        three = jnp.where(even_group, near, far)
        return jnp.where(wanted == 1, one, three)

    pair, cross = row_halo(video_frames, even, rows)
    own_a = lax.slice_in_dim(video_frames, frames - 1, frames, axis=0)
    near_a = shifted(own_a, "group", 2)
    far_a = shifted(near_a, "group", 2)
    odd_a = swapped(for_partner(own_a, near_a, far_a), "group", 0)

    def window(count, rows_of):
        return VMEM((count, rows_of, width, 3 * channels), BF16)

    stage = VMEM((rows + 1, width + 16, channels), F32)
    strided = VMEM((1, rows + 1, half, 3 * channels), BF16)
    total = VMEM((rows + 1, width, channels), F32)
    band_out = jax.ShapeDtypeStruct((rows + 1, width, channels), BF16)
    band_f32 = jax.ShapeDtypeStruct((rows + 1, width, channels), F32)
    code_out = jax.ShapeDtypeStruct((rows // 2, half, wide), BF16)
    code_f32 = jax.ShapeDtypeStruct((rows // 2 * half, wide), F32)
    one_tap = 2 * (rows + 1) * width * 9 * channels * channels
    one_code = 2 * (rows // 2) * half * 9 * channels * wide
    step2 = pl.BlockSpec((1, 3, 3 * channels, wide), lambda i: (0, 0, 0, 0))
    step2_mid = pl.BlockSpec((1, 3, 3 * channels, wide), lambda i: (1, 0, 0, 0))

    own_b, own_e, strided3 = call(
        send_kernel,
        [flags, video_frames, pair, cross, gain1, weight1, bias1, gain2, weight2],
        [band_out, code_out, jax.ShapeDtypeStruct(strided.shape, BF16)],
        [window(3, rows + 3), stage, total],
        {8: step2},
        flops=4 * one_tap + one_code,
    )
    near_b = shifted(own_b, "group", 2)
    near_e = shifted(own_e, "group", 2)
    first, following, late = call(
        own_kernel,
        [flags, video_frames, pair, cross, gain1, weight1, bias1, gain2, weight2, bias2, strided3],
        [band_f32, band_f32, code_f32],
        [window(3, rows + 3), stage, strided, total],
        flops=6 * one_tap + 2 * one_code,
    )
    far_b = shifted(near_b, "group", 2)
    far_e = shifted(near_e, "group", 2)
    gap = distance[0]
    prior = jnp.where(gap == 2, near_a, jnp.where(gap == 4, far_a, odd_a))
    prior = jnp.where(gap == 0, jnp.zeros_like(prior), prior)
    prior_pair, prior_cross = row_halo(prior, even, rows)
    done, first, early = call(
        next_kernel,
        [flags, prior, prior_pair, prior_cross, gain1, weight1, gain2, weight2, bias2, first,
         following, late],
        [code_out, band_f32, code_f32],
        [window(1, rows + 3), stage, strided, total],
        flops=2 * one_tap + 2 * one_code,
    )
    odd_b = swapped(for_partner(own_b, near_b, far_b), "group", 0)
    odd_e = swapped(for_partner(own_e, near_e, far_e), "group", 0)
    return call(
        last_kernel,
        [flags, near_b, far_b, odd_b, near_e, far_e, odd_e, gain2, weight2, first, early, done],
        [jax.ShapeDtypeStruct((frames // 2, rows // 2, half, wide), BF16)],
        [stage, strided],
        {8: step2_mid},
        flops=one_code,
    )[0]


def solution(mesh):
    placed = (P("group", "row", None, None), P("group"), P("group"), P(), P(), P(), P(), P(), P())
    return jax.shard_map(
        per_device,
        mesh=mesh,
        in_specs=placed,
        out_specs=P("group", "row", None, None),
        check_vma=False,
    )
```

time: 180 us -> 60.5 us (0.34)
  the two profiles are of different devices: /device:TPU:20 before, /device:TPU:0 now
where the time goes in v1:
time: 60.5 us; the launch traced here: 60.1 us
  starting transfers between devices  32.8 us (54%)
  Pallas kernels  12.9 us (21%)
  waiting for transfers between devices  6.81 us (11%)
  local copies, waits for them, and re-layouts  2.96 us (5%)
  other arithmetic  2.38 us (4%)
  between operations  2.2 us (4%)
    ppermute x6, starting transfers between devices, shifted(): lax.ppermute(value, axis, [(source, source + steps) for source in range(f...  25.7 us
    pallas_call x4, Pallas kernels, call(): pl.pallas_call(kernel, grid=(1,), out_shape=outs, in_specs=specs, out_spe...  12.9 us
    ppermute x8, starting transfers between devices, swapped(): return lax.ppermute(value, axis, pairs)  7.06 us
    ppermute x6, waiting for transfers between devices, shifted(): lax.ppermute(value, axis, [(source, source + steps) for source in range(f...  6.79 us
    select_n x2, other arithmetic, row_halo(): cross = swapped(jnp.where(even, high, low), 'row', 1)  2.07 us
    slice x1, local copies, waits for them, and re-layouts, per_device(): own_a = lax.slice_in_dim(video_frames, frames - 1, frames, axis=0)  1.77 us
  transfers between devices with their start and end apart: 14, of which 3 were waited for; matrix products, arithmetic and copies ran while one was open for 4% of the time, Pallas kernels for 19%

profile of v1, /device:TPU:0, one launch (start us, length us, event | category | flops | bytes accessed | tf_op | source)
XLA Modules:
  0.0 60.1 jit_solution(11891407084770278937)
XLA Ops:
  0.0 1.8 %slice.17 = bf16[1,4,192,128]{3,2,1,0:T(8,128)(2,1)} slice(bf16[4,4,192,128]{3,2,1,0:T(8,128)(2,1)} %video_ref.3), slice={[3:4], [0:4], [0:192], [0:128]} | slice | bytes 393216 | tf_op jit(solution)/shard_map/slice | solution.py:272
  1.8 4.9 %collective-permute-start.9 = (bf16[1,4,192,128]{3,2,1,0:T(8,128)(2,1)}, bf16[1,4,192,128]{3,2,1,0:T(8,128)(2,1)S(1)}, u32[]{:S(2)}, u32[]{:S(2)}) collective-permute-start(bf16[1,4,192,128]{3,2,1,0:T(8,128)(2,1)} %slice.17), channel_id=1, source_target_pairs={{0,8},{4,12},{8,16},{12,20},{16,24},{20,28},{1,9},{5,13},{9,17},{1... | collective-permute-start | bytes 589832 | tf_op jit(solution)/shard_map/ppermute | solution.py:20
  6.7 2.1 %broadcast_select_fusion = (bf16[4,2,192,128]{3,2,1,0:T(8,128)(2,1)}, bf16[4,2,192,128]{3,2,1,0:T(8,128)(2,1)}) fusion(pred[]{:T(512)} %eq.38, bf16[4,4,192,128]{3,2,1,0:T(8,128)(2,1)} %video_ref.3), kind=kLoop, calls=%fused_computation | loop fusion | flops 393216 | bytes 1572865 | tf_op jit(solution)/shard_map/jit(_where)/select_n | solution.py:239
  8.8 0.7 %collective-permute-start.1 = (bf16[4,2,192,128]{3,2,1,0:T(8,128)(2,1)}, bf16[4,2,192,128]{3,2,1,0:T(8,128)(2,1)S(1)}, u32[]{:S(2)}, u32[]{:S(2)}) collective-permute-start(bf16[4,2,192,128]{3,2,1,0:T(8,128)(2,1)} %get-tuple-element.23), channel_id=1, source_target_pairs={{1,2},{2,1},{5,6},{6,5},{9,10},{10,9},{13,14},{14,13},{17,18},{18,... | collective-permute-start | bytes 1179656 | tf_op jit(solution)/shard_map/ppermute | solution.py:28
  10.1 2.9 %collective-permute-start.4 = (s32[1]{0:T(128)}, s32[1]{0:T(128)}, u32[]{:S(2)}, u32[]{:S(2)}) collective-permute-start(s32[1]{0:T(128)} %select_n.112), channel_id=1, source_target_pairs={{0,4},{4,0},{8,12},{12,8},{16,20},{20,16},{24,28},{28,24},{1,5},{5... | collective-permute-start | bytes 20 | tf_op jit(solution)/shard_map/ppermute | solution.py:28
  13.0 4.1 %collective-permute-start.10 = (bf16[1,4,192,128]{3,2,1,0:T(8,128)(2,1)S(1)}, bf16[1,4,192,128]{3,2,1,0:T(8,128)(2,1)}, u32[]{:S(2)}, u32[]{:S(2)}) collective-permute-start(bf16[1,4,192,128]{3,2,1,0:T(8,128)(2,1)S(1)} %collective-permute-done.9), channel_id=1, source_target_pairs={{0,8},{4,12},{8,16},{12,20},{16,24},{20,28},{1,9},{5,13},{9,17},{1... | collective-permute-start | bytes 589832 | tf_op jit(solution)/shard_map/ppermute | solution.py:20
  17.1 0.1 add_convert_fusion
  17.9 0.1 pad_add_fusion.flag_ref
  18.6 2.1 %collective-permute-done.10 = bf16[1,4,192,128]{3,2,1,0:T(8,128)(2,1)} collective-permute-done((bf16[1,4,192,128]{3,2,1,0:T(8,128)(2,1)S(1)}, bf16[1,4,192,128]{3,2,1,0:T(8,128)(2,1)}, u32[]{:S(2)}, u32[]{:S(2)}) %collective-permute-start.10) | collective-permute-done | bytes 196640 | tf_op jit(solution)/shard_map/ppermute | solution.py:20
  20.8 1.5 %collective-permute-start.11 = (bf16[1,4,192,128]{3,2,1,0:T(8,128)(2,1)S(1)}, bf16[1,4,192,128]{3,2,1,0:T(8,128)(2,1)S(1)}, u32[]{:S(2)}, u32[]{:S(2)}) collective-permute-start(bf16[1,4,192,128]{3,2,1,0:T(8,128)(2,1)S(1)} %select_select_fusion.2), channel_id=1, source_target_pairs={{0,4},{4,0},{8,12},{12,8},{16,20},{20,16},{24,28},{28,24},{1,5},{5... | collective-permute-start | bytes 589832 | tf_op jit(solution)/shard_map/ppermute | solution.py:28
  22.3 1.2 %copy-done.2 = bf16[3,3,3,128,128]{4,3,2,1,0:T(8,128)(2,1)S(1)} copy-done((bf16[3,3,3,128,128]{4,3,2,1,0:T(8,128)(2,1)S(1)}, bf16[3,3,3,128,128]{4,3,2,1,0:T(8,128)(2,1)}, u32[]{:S(2)}) %copy-start.2) | copy-done | bytes 884760
  23.5 3.7 %shard_map.91 = (bf16[5,192,128]{2,1,0:T(8,128)(2,1)S(1)}, bf16[2,96,256]{2,1,0:T(8,128)(2,1)S(1)}, bf16[1,5,96,384]{3,2,1,0:T(8,128)(2,1)S(1)}) custom-call(s32[4]{0:T(128)S(1)} %pad_add_fusion.flag_ref, bf16[4,4,192,128]{3,2,1,0:T(8,128)(2,1)S(1)} %copy-done.1, bf16[4,2,192,128]{3,2,1,0:T(8,128)(2,1)S(1)} %collective-permute-done.pair_ref, ...), custom_call_target="tpu_custom_call" | custom-call | flops 1245708288 | bytes 4941328 | tf_op jit(solution)/shard_map/pallas_call | solution.py:223
  27.2 4.5 %collective-permute-start.6 = (bf16[2,96,256]{2,1,0:T(8,128)(2,1)S(1)}, bf16[2,96,256]{2,1,0:T(8,128)(2,1)S(1)}, u32[]{:S(2)}, u32[]{:S(2)}) collective-permute-start(bf16[2,96,256]{2,1,0:T(8,128)(2,1)S(1)} %get-tuple-element.15), channel_id=1, source_target_pairs={{0,8},{4,12},{8,16},{12,20},{16,24},{20,28},{1,9},{5,13},{9,17},{1... | collective-permute-start | bytes 294920 | tf_op jit(solution)/shard_map/ppermute | solution.py:20
  31.7 3.5 %collective-permute-start.2 = (bf16[5,192,128]{2,1,0:T(8,128)(2,1)S(1)}, bf16[5,192,128]{2,1,0:T(8,128)(2,1)S(1)}, u32[]{:S(2)}, u32[]{:S(2)}) collective-permute-start(bf16[5,192,128]{2,1,0:T(8,128)(2,1)S(1)} %get-tuple-element.14), channel_id=1, source_target_pairs={{0,8},{4,12},{8,16},{12,20},{16,24},{20,28},{1,9},{5,13},{9,17},{1... | collective-permute-start | bytes 737288 | tf_op jit(solution)/shard_map/ppermute | solution.py:20
  35.2 4.3 %collective-permute-start.7 = (bf16[2,96,256]{2,1,0:T(8,128)(2,1)S(1)}, bf16[2,96,256]{2,1,0:T(8,128)(2,1)S(1)}, u32[]{:S(2)}, u32[]{:S(2)}) collective-permute-start(bf16[2,96,256]{2,1,0:T(8,128)(2,1)S(1)} %collective-permute-done.6.tail_a_ref), channel_id=1, source_target_pairs={{0,8},{4,12},{8,16},{12,20},{16,24},{20,28},{1,9},{5,13},{9,17},{1... | collective-permute-start | bytes 294920 | tf_op jit(solution)/shard_map/ppermute | solution.py:20
  39.5 1.9 %collective-permute-done.2.prior_a_ref = bf16[5,192,128]{2,1,0:T(8,128)(2,1)S(1)} collective-permute-done((bf16[5,192,128]{2,1,0:T(8,128)(2,1)S(1)}, bf16[5,192,128]{2,1,0:T(8,128)(2,1)S(1)}, u32[]{:S(2)}, u32[]{:S(2)}) %collective-permute-start.2) | collective-permute-done | bytes 245792 | tf_op jit(solution)/shard_map/ppermute | solution.py:20
  41.4 4.4 %collective-permute-start.3 = (bf16[5,192,128]{2,1,0:T(8,128)(2,1)S(1)}, bf16[5,192,128]{2,1,0:T(8,128)(2,1)S(1)}, u32[]{:S(2)}, u32[]{:S(2)}) collective-permute-start(bf16[5,192,128]{2,1,0:T(8,128)(2,1)S(1)} %collective-permute-done.2.prior_a_ref), channel_id=1, source_target_pairs={{0,8},{4,12},{8,16},{12,20},{16,24},{20,28},{1,9},{5,13},{9,17},{1... | collective-permute-start | bytes 737288 | tf_op jit(solution)/shard_map/ppermute | solution.py:20
  45.9 0.7 %collective-permute-start.13 = (bf16[1,2,192,128]{3,2,1,0:T(8,128)(2,1)S(1)}, bf16[1,2,192,128]{3,2,1,0:T(8,128)(2,1)S(1)}, u32[]{:S(2)}, u32[]{:S(2)}) collective-permute-start(bf16[1,2,192,128]{3,2,1,0:T(8,128)(2,1)S(1)} %get-tuple-element.25), channel_id=1, source_target_pairs={{1,2},{2,1},{5,6},{6,5},{9,10},{10,9},{13,14},{14,13},{17,18},{18,... | collective-permute-start | bytes 294920 | tf_op jit(solution)/shard_map/ppermute | solution.py:28
  46.6 0.6 %collective-permute-start.8 = (bf16[2,96,256]{2,1,0:T(8,128)(2,1)S(1)}, bf16[2,96,256]{2,1,0:T(8,128)(2,1)S(1)}, u32[]{:S(2)}, u32[]{:S(2)}) collective-permute-start(bf16[2,96,256]{2,1,0:T(8,128)(2,1)S(1)} %select_select_fusion.3), channel_id=1, source_target_pairs={{0,4},{4,0},{8,12},{12,8},{16,20},{20,16},{24,28},{28,24},{1,5},{5... | collective-permute-start | bytes 294920 | tf_op jit(solution)/shard_map/ppermute | solution.py:28
  47.3 2.8 %collective-permute-done.3.prior_b_ref = bf16[5,192,128]{2,1,0:T(8,128)(2,1)S(1)} collective-permute-done((bf16[5,192,128]{2,1,0:T(8,128)(2,1)S(1)}, bf16[5,192,128]{2,1,0:T(8,128)(2,1)S(1)}, u32[]{:S(2)}, u32[]{:S(2)}) %collective-permute-start.3) | collective-permute-done | bytes 245792 | tf_op jit(solution)/shard_map/ppermute | solution.py:20
  50.1 0.6 %collective-permute-start.5 = (bf16[5,192,128]{2,1,0:T(8,128)(2,1)S(1)}, bf16[5,192,128]{2,1,0:T(8,128)(2,1)S(1)}, u32[]{:S(2)}, u32[]{:S(2)}) collective-permute-start(bf16[5,192,128]{2,1,0:T(8,128)(2,1)S(1)} %select_select_fusion), channel_id=1, source_target_pairs={{0,4},{4,0},{8,12},{12,8},{16,20},{20,16},{24,28},{28,24},{1,5},{5... | collective-permute-start | bytes 737288 | tf_op jit(solution)/shard_map/ppermute | solution.py:28
  50.7 4.8 %shard_map.92 = (f32[5,192,128]{2,1,0:T(8,128)S(1)}, f32[5,192,128]{2,1,0:T(8,128)S(1)}, f32[192,256]{1,0:T(8,128)S(1)}) custom-call(s32[4]{0:T(128)S(1)} %pad_add_fusion.flag_ref, bf16[4,4,192,128]{3,2,1,0:T(8,128)(2,1)S(1)} %copy-done.1, bf16[4,2,192,128]{3,2,1,0:T(8,128)(2,1)S(1)} %collective-permute-done.pair_ref, ...), custom_call_target="tpu_custom_call" | custom-call | flops 1925185536 | bytes 5777936 | tf_op jit(solution)/shard_map/pallas_call | solution.py:223
  55.6 2.7 %shard_map.93 = (bf16[2,96,256]{2,1,0:T(8,128)(2,1)S(1)}, f32[5,192,128]{2,1,0:T(8,128)S(1)}, f32[192,256]{1,0:T(8,128)S(1)}) custom-call(s32[4]{0:T(128)S(1)} %pad_add_fusion.flag_ref, bf16[1,4,192,128]{3,2,1,0:T(8,128)(2,1)S(1)} %select_select_fusion.1.prior_ref, bf16[1,2,192,128]{3,2,1,0:T(8,128)(2,1)S(1)} %collective-permute-done.12.pair_ref, ...), custom_call_target="tpu_custom_call" | custom-call | flops 792723456 | bytes 5015568 | tf_op jit(solution)/shard_map/pallas_call | solution.py:223
  58.3 1.8 %shard_map.94 = bf16[2,2,96,256]{3,2,1,0:T(8,128)(2,1)} custom-call(s32[4]{0:T(128)S(1)} %pad_add_fusion.flag_ref, bf16[5,192,128]{2,1,0:T(8,128)(2,1)S(1)} %collective-permute-done.2.prior_a_ref, bf16[5,192,128]{2,1,0:T(8,128)(2,1)S(1)} %collective-permute-done.3.prior_b_ref, bf16[5,192,128]{2,1,0:T(8,128)(2,1)S(1)} %collective-permute-done.5.prior_c_ref, ...), custom_call_target="tpu_custom_call" | custom-call | flops 113246208 | bytes 3785232 | tf_op jit(solution)/shard_map/pallas_call | solution.py:223
  (31 shorter events, 0.3 us)
Async XLA Ops:
  0.0 20.7 %copy-start.1 = (bf16[4,4,192,128]{3,2,1,0:T(8,128)(2,1)S(1)}, bf16[4,4,192,128]{3,2,1,0:T(8,128)(2,1)}, u32[]{:S(2)}) copy-start(bf16[4,4,192,128]{3,2,1,0:T(8,128)(2,1)} %video_ref.3) | copy-start | bytes 2359300
  0.0 22.3 %copy-start.3 = (f32[128]{0:T(128)S(1)}, f32[128]{0:T(128)}, u32[]{:S(2)}) copy-start(f32[128]{0:T(128)} %param.15) | copy-start | bytes 1540
  0.0 22.3 %copy-start = (bf16[3,3,3,128,256]{4,3,2,1,0:T(8,128)(2,1)S(1)}, bf16[3,3,3,128,256]{4,3,2,1,0:T(8,128)(2,1)}, u32[]{:S(2)}) copy-start(bf16[3,3,3,128,256]{4,3,2,1,0:T(8,128)(2,1)} %param.16) | copy-start | bytes 5308420
  0.0 22.3 %copy-start.5 = (f32[128]{0:T(128)S(1)}, f32[128]{0:T(128)}, u32[]{:S(2)}) copy-start(f32[128]{0:T(128)} %param.12) | copy-start | bytes 1540
  0.0 22.3 %copy-start.6 = (f32[128]{0:T(128)S(1)}, f32[128]{0:T(128)}, u32[]{:S(2)}) copy-start(f32[128]{0:T(128)} %param.14) | copy-start | bytes 1540
  1.8 11.2 %collective-permute-start.9 = (bf16[1,4,192,128]{3,2,1,0:T(8,128)(2,1)}, bf16[1,4,192,128]{3,2,1,0:T(8,128)(2,1)S(1)}, u32[]{:S(2)}, u32[]{:S(2)}) collective-permute-start(bf16[1,4,192,128]{3,2,1,0:T(8,128)(2,1)} %slice.17), channel_id=1, source_target_pairs={{0,8},{4,12},{8,16},{12,20},{16,24},{20,28},{1,9},{5,13},{9,17},{1... | collective-permute-start | bytes 589832 | tf_op jit(solution)/shard_map/ppermute | solution.py:20
  8.8 13.5 %collective-permute-start = (bf16[4,2,192,128]{3,2,1,0:T(8,128)(2,1)}, bf16[4,2,192,128]{3,2,1,0:T(8,128)(2,1)S(1)}, u32[]{:S(2)}, u32[]{:S(2)}) collective-permute-start(bf16[4,2,192,128]{3,2,1,0:T(8,128)(2,1)} %get-tuple-element.24), channel_id=1, source_target_pairs={{0,1},{1,0},{2,3},{3,2},{4,5},{5,4},{6,7},{7,6},{8,9},{9,8},{10,11... | collective-permute-start | bytes 1179656 | tf_op jit(solution)/shard_map/ppermute | solution.py:28
  8.8 13.5 %collective-permute-start.1 = (bf16[4,2,192,128]{3,2,1,0:T(8,128)(2,1)}, bf16[4,2,192,128]{3,2,1,0:T(8,128)(2,1)S(1)}, u32[]{:S(2)}, u32[]{:S(2)}) collective-permute-start(bf16[4,2,192,128]{3,2,1,0:T(8,128)(2,1)} %get-tuple-element.23), channel_id=1, source_target_pairs={{1,2},{2,1},{5,6},{6,5},{9,10},{10,9},{13,14},{14,13},{17,18},{18,... | collective-permute-start | bytes 1179656 | tf_op jit(solution)/shard_map/ppermute | solution.py:28
  10.1 7.8 %collective-permute-start.4 = (s32[1]{0:T(128)}, s32[1]{0:T(128)}, u32[]{:S(2)}, u32[]{:S(2)}) collective-permute-start(s32[1]{0:T(128)} %select_n.112), channel_id=1, source_target_pairs={{0,4},{4,0},{8,12},{12,8},{16,20},{20,16},{24,28},{28,24},{1,5},{5... | collective-permute-start | bytes 20 | tf_op jit(solution)/shard_map/ppermute | solution.py:28
  13.0 7.7 %collective-permute-start.10 = (bf16[1,4,192,128]{3,2,1,0:T(8,128)(2,1)S(1)}, bf16[1,4,192,128]{3,2,1,0:T(8,128)(2,1)}, u32[]{:S(2)}, u32[]{:S(2)}) collective-permute-start(bf16[1,4,192,128]{3,2,1,0:T(8,128)(2,1)S(1)} %collective-permute-done.9), channel_id=1, source_target_pairs={{0,8},{4,12},{8,16},{12,20},{16,24},{20,28},{1,9},{5,13},{9,17},{1... | collective-permute-start | bytes 589832 | tf_op jit(solution)/shard_map/ppermute | solution.py:20
  20.8 18.7 %collective-permute-start.11 = (bf16[1,4,192,128]{3,2,1,0:T(8,128)(2,1)S(1)}, bf16[1,4,192,128]{3,2,1,0:T(8,128)(2,1)S(1)}, u32[]{:S(2)}, u32[]{:S(2)}) collective-permute-start(bf16[1,4,192,128]{3,2,1,0:T(8,128)(2,1)S(1)} %select_select_fusion.2), channel_id=1, source_target_pairs={{0,4},{4,0},{8,12},{12,8},{16,20},{20,16},{24,28},{28,24},{1,5},{5... | collective-permute-start | bytes 589832 | tf_op jit(solution)/shard_map/ppermute | solution.py:28
  22.3 1.2 %copy-start.2 = (bf16[3,3,3,128,128]{4,3,2,1,0:T(8,128)(2,1)S(1)}, bf16[3,3,3,128,128]{4,3,2,1,0:T(8,128)(2,1)}, u32[]{:S(2)}) copy-start(bf16[3,3,3,128,128]{4,3,2,1,0:T(8,128)(2,1)} %param.13) | copy-start | bytes 2654212
  27.2 23.6 %copy-start.4 = (f32[256]{0:T(256)S(1)}, f32[256]{0:T(256)}, u32[]{:S(2)}) copy-start(f32[256]{0:T(256)} %param.17) | copy-start | bytes 3076
  27.2 8.0 %collective-permute-start.6 = (bf16[2,96,256]{2,1,0:T(8,128)(2,1)S(1)}, bf16[2,96,256]{2,1,0:T(8,128)(2,1)S(1)}, u32[]{:S(2)}, u32[]{:S(2)}) collective-permute-start(bf16[2,96,256]{2,1,0:T(8,128)(2,1)S(1)} %get-tuple-element.15), channel_id=1, source_target_pairs={{0,8},{4,12},{8,16},{12,20},{16,24},{20,28},{1,9},{5,13},{9,17},{1... | collective-permute-start | bytes 294920 | tf_op jit(solution)/shard_map/ppermute | solution.py:20
  31.7 9.8 %collective-permute-start.2 = (bf16[5,192,128]{2,1,0:T(8,128)(2,1)S(1)}, bf16[5,192,128]{2,1,0:T(8,128)(2,1)S(1)}, u32[]{:S(2)}, u32[]{:S(2)}) collective-permute-start(bf16[5,192,128]{2,1,0:T(8,128)(2,1)S(1)} %get-tuple-element.14), channel_id=1, source_target_pairs={{0,8},{4,12},{8,16},{12,20},{16,24},{20,28},{1,9},{5,13},{9,17},{1... | collective-permute-start | bytes 737288 | tf_op jit(solution)/shard_map/ppermute | solution.py:20
  35.2 11.4 %collective-permute-start.7 = (bf16[2,96,256]{2,1,0:T(8,128)(2,1)S(1)}, bf16[2,96,256]{2,1,0:T(8,128)(2,1)S(1)}, u32[]{:S(2)}, u32[]{:S(2)}) collective-permute-start(bf16[2,96,256]{2,1,0:T(8,128)(2,1)S(1)} %collective-permute-done.6.tail_a_ref), channel_id=1, source_target_pairs={{0,8},{4,12},{8,16},{12,20},{16,24},{20,28},{1,9},{5,13},{9,17},{1... | collective-permute-start | bytes 294920 | tf_op jit(solution)/shard_map/ppermute | solution.py:20
  41.4 8.6 %collective-permute-start.3 = (bf16[5,192,128]{2,1,0:T(8,128)(2,1)S(1)}, bf16[5,192,128]{2,1,0:T(8,128)(2,1)S(1)}, u32[]{:S(2)}, u32[]{:S(2)}) collective-permute-start(bf16[5,192,128]{2,1,0:T(8,128)(2,1)S(1)} %collective-permute-done.2.prior_a_ref), channel_id=1, source_target_pairs={{0,8},{4,12},{8,16},{12,20},{16,24},{20,28},{1,9},{5,13},{9,17},{1... | collective-permute-start | bytes 737288 | tf_op jit(solution)/shard_map/ppermute | solution.py:20
  45.9 9.7 %collective-permute-start.12 = (bf16[1,2,192,128]{3,2,1,0:T(8,128)(2,1)S(1)}, bf16[1,2,192,128]{3,2,1,0:T(8,128)(2,1)S(1)}, u32[]{:S(2)}, u32[]{:S(2)}) collective-permute-start(bf16[1,2,192,128]{3,2,1,0:T(8,128)(2,1)S(1)} %get-tuple-element.26), channel_id=1, source_target_pairs={{0,1},{1,0},{2,3},{3,2},{4,5},{5,4},{6,7},{7,6},{8,9},{9,8},{10,11... | collective-permute-start | bytes 294920 | tf_op jit(solution)/shard_map/ppermute | solution.py:28
  45.9 9.6 %collective-permute-start.13 = (bf16[1,2,192,128]{3,2,1,0:T(8,128)(2,1)S(1)}, bf16[1,2,192,128]{3,2,1,0:T(8,128)(2,1)S(1)}, u32[]{:S(2)}, u32[]{:S(2)}) collective-permute-start(bf16[1,2,192,128]{3,2,1,0:T(8,128)(2,1)S(1)} %get-tuple-element.25), channel_id=1, source_target_pairs={{1,2},{2,1},{5,6},{6,5},{9,10},{10,9},{13,14},{14,13},{17,18},{18,... | collective-permute-start | bytes 294920 | tf_op jit(solution)/shard_map/ppermute | solution.py:28
  46.6 11.6 %collective-permute-start.8 = (bf16[2,96,256]{2,1,0:T(8,128)(2,1)S(1)}, bf16[2,96,256]{2,1,0:T(8,128)(2,1)S(1)}, u32[]{:S(2)}, u32[]{:S(2)}) collective-permute-start(bf16[2,96,256]{2,1,0:T(8,128)(2,1)S(1)} %select_select_fusion.3), channel_id=1, source_target_pairs={{0,4},{4,0},{8,12},{12,8},{16,20},{20,16},{24,28},{28,24},{1,5},{5... | collective-permute-start | bytes 294920 | tf_op jit(solution)/shard_map/ppermute | solution.py:28
  50.1 8.2 %collective-permute-start.5 = (bf16[5,192,128]{2,1,0:T(8,128)(2,1)S(1)}, bf16[5,192,128]{2,1,0:T(8,128)(2,1)S(1)}, u32[]{:S(2)}, u32[]{:S(2)}) collective-permute-start(bf16[5,192,128]{2,1,0:T(8,128)(2,1)S(1)} %select_select_fusion), channel_id=1, source_target_pairs={{0,4},{4,0},{8,12},{12,8},{16,20},{20,16},{24,28},{28,24},{1,5},{5... | collective-permute-start | bytes 737288 | tf_op jit(solution)/shard_map/ppermute | solution.py:28

commit v2 on v1

--- a/solution.py
+++ b/solution.py
@@ -14,17 +14,17 @@
 BF16 = jnp.bfloat16
 
 
-def shifted(value, axis, steps):
+def rotated(value, axis, steps):
     count = lax.axis_size(axis)
-    first, last = (max(0, -steps), min(count, count - steps))
-    return lax.ppermute(value, axis, [(source, source + steps) for source in range(first, last)])
+    return lax.ppermute(value, axis, [(source, (source + steps) % count) for source in range(count)])
 
 
 def swapped(value, axis, offset):
     count = lax.axis_size(axis)
     pairs = []
-    for low in range(offset, count - 1, 2):
-        pairs += [(low, low + 1), (low + 1, low)]
+    for low in range(offset, count, 2):
+        high = (low + 1) % count
+        pairs += [(low, high), (high, low)]
     return lax.ppermute(value, axis, pairs)
 
 
@@ -84,17 +84,19 @@
     return total
 
 
-def pick_rows(even, first, second):
-    return jnp.where(even, first, second)
-
-
-def row_reader(video_ref, frame, pair_ref, cross_ref, even):
+def row_reader(flag_ref, video_ref, frame, pair_ref, cross_ref):
+    even, top, bottom = flag_ref[0] == 1, flag_ref[1] == 1, flag_ref[4] == 1
+    rows = video_ref.shape[1]
+
     def read(row):
+        if ABOVE <= row < ABOVE + rows:
+            return video_ref[frame, row - ABOVE].astype(F32)
         if row < ABOVE:
-            return jnp.where(even, cross_ref[frame, row].astype(F32), pair_ref[frame, row].astype(F32))
-        if row < ABOVE + 4:
-            return video_ref[frame, row - ABOVE].astype(F32)
-        return jnp.where(even, pair_ref[frame, 0].astype(F32), cross_ref[frame, 0].astype(F32))
+            first, second, outside = cross_ref[frame, row], pair_ref[frame, row], top
+        else:
+            first, second, outside = pair_ref[frame, 0], cross_ref[frame, 0], bottom
+        value = jnp.where(even, first.astype(F32), second.astype(F32))
+        return jnp.where(outside, 0.0, value)
 
     return read
 
@@ -103,10 +105,9 @@
     flag_ref, video_ref, pair_ref, cross_ref, gain1_ref, weight1_ref, bias1_ref, gain2_ref,
     weight2_ref, prior_ref, tail_ref, strided_out_ref, window_ref, stage_ref, total_ref,
 ):
-    even, first_row = flag_ref[0] == 1, flag_ref[1] == 1
-    width = video_ref.shape[2]
+    first_row = flag_ref[1] == 1
     channels = video_ref.shape[3]
-    readers = [row_reader(video_ref, f, pair_ref, cross_ref, even) for f in range(4)]
+    readers = [row_reader(flag_ref, video_ref, f, pair_ref, cross_ref) for f in range(4)]
     for slot, frame in enumerate((1, 2, 3)):
         fill_hidden(readers[frame], gain1_ref[...], window_ref, slot, 7)
     both = conv1_rows(
@@ -131,10 +132,9 @@
     weight2_ref, bias2_ref, strided3_ref, first_ref, next_ref, late_ref,
     window_ref, stage_ref, strided_ref, total_ref,
 ):
-    even, first_row = flag_ref[0] == 1, flag_ref[1] == 1
-    width = video_ref.shape[2]
+    first_row = flag_ref[1] == 1
     channels = video_ref.shape[3]
-    readers = [row_reader(video_ref, f, pair_ref, cross_ref, even) for f in range(4)]
+    readers = [row_reader(flag_ref, video_ref, f, pair_ref, cross_ref) for f in range(4)]
     for frame in range(3):
         fill_hidden(readers[frame], gain1_ref[...], window_ref, frame, 7)
     both = conv1_rows(
@@ -168,10 +168,10 @@
     weight2_ref, bias2_ref, first_ref, next_ref, late_ref, second_out_ref, first_out_ref, early_ref,
     window_ref, stage_ref, strided_ref, total_ref,
 ):
-    even, first_row, keep = flag_ref[0] == 1, flag_ref[1] == 1, flag_ref[2] == 1
+    first_row, keep = flag_ref[1] == 1, flag_ref[2] == 1
     channels = prior_ref.shape[3]
     fill_hidden(
-        row_reader(prior_ref, 0, pair_ref, cross_ref, even), gain1_ref[...], window_ref, 0, 7
+        row_reader(flag_ref, prior_ref, 0, pair_ref, cross_ref), gain1_ref[...], window_ref, 0, 7
     )
     both = conv1_rows(
         window_ref, 0, 5,
@@ -208,6 +208,17 @@
     tail = chosen(tail_a_ref[...], tail_b_ref[...], tail_c_ref[...])
     out_ref[0] = (early.reshape(shape) + tail).astype(BF16)
     out_ref[1] = done_ref[...]
+
+
+def pack_kernel(flag_ref, video_ref, own_ref, pair_ref, cross_ref):
+    even = flag_ref[0] == 1
+    frames, rows = video_ref.shape[:2]
+    own_ref[0] = video_ref[frames - 1]
+    for frame in range(frames):
+        for row in range(ABOVE):
+            high, low = video_ref[frame, row], video_ref[frame, rows - ABOVE + row]
+            pair_ref[frame, row] = jnp.where(even, low, high)
+            cross_ref[frame, row] = jnp.where(even, high, low)
 
 
 def whole(shape):
@@ -254,7 +265,12 @@
     even_group = position % 2 == 0
     keep = frame_counts >= frames
     flags = jnp.concatenate(
-        [jnp.stack([even, band == 0]).astype(jnp.int32), keep.astype(jnp.int32), distance]
+        [
+            jnp.stack([even, band == 0]).astype(jnp.int32),
+            keep.astype(jnp.int32),
+            distance,
+            (band == lax.axis_size("row") - 1).astype(jnp.int32)[None],
+        ]
     )
     gain1, bias1 = norm1_gain[None], conv1_bias[None]
     gain2, bias2 = norm2_gain[None], conv2_bias[None]
@@ -268,10 +284,16 @@
         three = jnp.where(even_group, near, far)
         return jnp.where(wanted == 1, one, three)
 
-    pair, cross = row_halo(video_frames, even, rows)
-    own_a = lax.slice_in_dim(video_frames, frames - 1, frames, axis=0)
-    near_a = shifted(own_a, "group", 2)
-    far_a = shifted(near_a, "group", 2)
+    edge = jax.ShapeDtypeStruct((frames, ABOVE, width, channels), BF16)
+    own_a, pair, cross = call(
+        pack_kernel,
+        [flags, video_frames],
+        [jax.ShapeDtypeStruct((1, rows, width, channels), BF16), edge, edge],
+        [],
+    )
+    pair, cross = swapped(pair, "row", 0), swapped(cross, "row", 1)
+    near_a = rotated(own_a, "group", 2)
+    far_a = rotated(near_a, "group", 2)
     odd_a = swapped(for_partner(own_a, near_a, far_a), "group", 0)
 
     def window(count, rows_of):
@@ -297,8 +319,8 @@
         {8: step2},
         flops=4 * one_tap + one_code,
     )
-    near_b = shifted(own_b, "group", 2)
-    near_e = shifted(own_e, "group", 2)
+    near_b = rotated(own_b, "group", 2)
+    near_e = rotated(own_e, "group", 2)
     first, following, late = call(
         own_kernel,
         [flags, video_frames, pair, cross, gain1, weight1, bias1, gain2, weight2, bias2, strided3],
@@ -306,8 +328,9 @@
         [window(3, rows + 3), stage, strided, total],
         flops=6 * one_tap + 2 * one_code,
     )
-    far_b = shifted(near_b, "group", 2)
-    far_e = shifted(near_e, "group", 2)
+    near_b, near_e, first = lax.optimization_barrier((near_b, near_e, first))
+    far_b = rotated(near_b, "group", 2)
+    far_e = rotated(near_e, "group", 2)
     gap = distance[0]
     prior = jnp.where(gap == 2, near_a, jnp.where(gap == 4, far_a, odd_a))
     prior = jnp.where(gap == 0, jnp.zeros_like(prior), prior)

time: 60.5 us -> 57.6 us (0.952)
  starting transfers between devices: 32.8 us -> 16.5 us
  waiting for transfers between devices: 6.81 us -> 17.8 us
  local copies, waits for them, and re-layouts: 2.96 us -> 6.88 us
  other arithmetic: 2.38 us -> 0.32 us
  Pallas kernels: 12.9 us -> 13.7 us
    ppermute x6, starting transfers between devices: 25.7 us -> 5.78 us  [rotated(): lax.ppermute(value, axis, [(source, (source + steps) % count) for source...]
    ppermute x6, waiting for transfers between devices: 6.79 us -> 15.1 us  [rotated(): lax.ppermute(value, axis, [(source, (source + steps) % count) for source...]
    unnamed x14 -> x18, local copies, waits for them, and re-layouts: 1.19 us -> 6.88 us
    ppermute x8, starting transfers between devices: 7.06 us -> 10.8 us  [swapped(): return lax.ppermute(value, axis, pairs)]
    ppermute x8, waiting for transfers between devices: 0.02 us -> 2.74 us  [swapped(): return lax.ppermute(value, axis, pairs)]
    select_n x2 -> x1, other arithmetic: 2.07 us -> 0.02 us  [row_halo(): cross = swapped(jnp.where(even, high, low), 'row', 1)]
    slice x1 -> x0, local copies, waits for them, and re-layouts: 1.77 us -> none  [per_device(): own_a = lax.slice_in_dim(video_frames, frames - 1, frames, axis=0)]
    pallas_call x4 -> x5, Pallas kernels: 12.9 us -> 13.7 us  [call(): pl.pallas_call(kernel, grid=(1,), out_shape=outs, in_specs=specs, out_spe...]
  transfers between devices with their start and end apart: 14 -> 14, of which waited for: 3 -> 5; matrix products, arithmetic and copies ran while one was open for 4% -> 0% of each run, Pallas kernels for 19% -> 20%
where the time goes in v2:
time: 57.6 us; the launch traced here: 57.2 us
  waiting for transfers between devices  17.8 us (31%)
  starting transfers between devices  16.5 us (29%)
  Pallas kernels  13.7 us (24%)
  local copies, waits for them, and re-layouts  6.88 us (12%)
  between operations  2.03 us (4%)
    ppermute x6, waiting for transfers between devices, rotated(): lax.ppermute(value, axis, [(source, (source + steps) % count) for source...  15.1 us
    pallas_call x5, Pallas kernels, call(): pl.pallas_call(kernel, grid=(1,), out_shape=outs, in_specs=specs, out_spe...  13.7 us
    ppermute x8, starting transfers between devices, swapped(): return lax.ppermute(value, axis, pairs)  10.8 us
    unnamed x18, local copies, waits for them, and re-layouts  6.88 us
    ppermute x6, starting transfers between devices, rotated(): lax.ppermute(value, axis, [(source, (source + steps) % count) for source...  5.78 us
    ppermute x8, waiting for transfers between devices, swapped(): return lax.ppermute(value, axis, pairs)  2.74 us
  transfers between devices with their start and end apart: 14, of which 5 were waited for; matrix products, arithmetic and copies ran while one was open for 0% of the time, Pallas kernels for 20%

profile of v2, /device:TPU:0, one launch (start us, length us, event | category | flops | bytes accessed | tf_op | source)
XLA Modules:
  0.0 57.2 jit_solution(8001041819509243673)
XLA Ops:
  1.5 1.1 %copy-done.3 = bf16[4,4,192,128]{3,2,1,0:T(8,128)(2,1)S(1)} copy-done((bf16[4,4,192,128]{3,2,1,0:T(8,128)(2,1)S(1)}, bf16[4,4,192,128]{3,2,1,0:T(8,128)(2,1)}, u32[]{:S(2)}) %copy-start.3) | copy-done | bytes 786456
  2.6 0.7 %shard_map.91 = (bf16[1,4,192,128]{3,2,1,0:T(8,128)(2,1)S(1)}, bf16[4,2,192,128]{3,2,1,0:T(8,128)(2,1)S(1)}, bf16[4,2,192,128]{3,2,1,0:T(8,128)(2,1)S(1)}) custom-call(s32[5]{0:T(128)S(1)} %pad_add_fusion.flag_ref, bf16[4,4,192,128]{3,2,1,0:T(8,128)(2,1)S(1)} %copy-done.3), custom_call_target="tpu_custom_call" | custom-call | bytes 1769492 | tf_op jit(solution)/shard_map/pallas_call | solution.py:234
  3.8 2.6 %collective-permute-start.1 = (bf16[4,2,192,128]{3,2,1,0:T(8,128)(2,1)S(1)}, bf16[4,2,192,128]{3,2,1,0:T(8,128)(2,1)S(1)}, u32[]{:S(2)}, u32[]{:S(2)}) collective-permute-start(bf16[4,2,192,128]{3,2,1,0:T(8,128)(2,1)S(1)} %get-tuple-element.21), channel_id=1, source_target_pairs={{1,2},{2,1},{3,0},{0,3},{5,6},{6,5},{7,4},{4,7},{9,10},{10,9},{11,... | collective-permute-start | bytes 1179656 | tf_op jit(solution)/shard_map/ppermute | solution.py:28
  6.5 1.6 %collective-permute-start.9 = (bf16[1,4,192,128]{3,2,1,0:T(8,128)(2,1)S(1)}, bf16[1,4,192,128]{3,2,1,0:T(8,128)(2,1)S(1)}, u32[]{:S(2)}, u32[]{:S(2)}) collective-permute-start(bf16[1,4,192,128]{3,2,1,0:T(8,128)(2,1)S(1)} %get-tuple-element.28), channel_id=1, source_target_pairs={{0,8},{4,12},{8,16},{12,20},{16,24},{20,28},{24,0},{28,4},{1,9},{5... | collective-permute-start | bytes 589832 | tf_op jit(solution)/shard_map/ppermute | solution.py:19
  8.0 7.2 %collective-permute-done.9 = bf16[1,4,192,128]{3,2,1,0:T(8,128)(2,1)S(1)} collective-permute-done((bf16[1,4,192,128]{3,2,1,0:T(8,128)(2,1)S(1)}, bf16[1,4,192,128]{3,2,1,0:T(8,128)(2,1)S(1)}, u32[]{:S(2)}, u32[]{:S(2)}) %collective-permute-start.9) | collective-permute-done | bytes 196640 | tf_op jit(solution)/shard_map/ppermute | solution.py:19
  15.2 2.8 %collective-permute-start.5 = (s32[1]{0:T(128)}, s32[1]{0:T(128)}, u32[]{:S(2)}, u32[]{:S(2)}) collective-permute-start(s32[1]{0:T(128)} %select_n.100), channel_id=1, source_target_pairs={{0,4},{4,0},{8,12},{12,8},{16,20},{20,16},{24,28},{28,24},{1,5},{5... | collective-permute-start | bytes 20 | tf_op jit(solution)/shard_map/ppermute | solution.py:28
  18.0 0.7 %collective-permute-done.5 = s32[1]{0:T(128)} collective-permute-done((s32[1]{0:T(128)}, s32[1]{0:T(128)}, u32[]{:S(2)}, u32[]{:S(2)}) %collective-permute-start.5) | collective-permute-done | bytes 36 | tf_op jit(solution)/shard_map/ppermute | solution.py:28
  19.3 1.5 %copy-done = bf16[3,3,3,128,256]{4,3,2,1,0:T(8,128)(2,1)S(1)} copy-done((bf16[3,3,3,128,256]{4,3,2,1,0:T(8,128)(2,1)S(1)}, bf16[3,3,3,128,256]{4,3,2,1,0:T(8,128)(2,1)}, u32[]{:S(2)}) %copy-start) | copy-done | bytes 1769496
  20.8 1.2 %copy-done.2 = bf16[3,3,3,128,128]{4,3,2,1,0:T(8,128)(2,1)S(1)} copy-done((bf16[3,3,3,128,128]{4,3,2,1,0:T(8,128)(2,1)S(1)}, bf16[3,3,3,128,128]{4,3,2,1,0:T(8,128)(2,1)}, u32[]{:S(2)}) %copy-start.2) | copy-done | bytes 884760
  22.0 1.1 %copy-done.4 = bf16[4,4,192,128]{3,2,1,0:T(8,128)(2,1)S(1)} copy-done((bf16[4,4,192,128]{3,2,1,0:T(8,128)(2,1)S(1)}, bf16[4,4,192,128]{3,2,1,0:T(8,128)(2,1)}, u32[]{:S(2)}) %copy-start.4) | copy-done | bytes 786456
  23.8 0.7 %copy-done.7 = f32[128]{0:T(128)S(1)} copy-done((f32[128]{0:T(128)S(1)}, f32[128]{0:T(128)}, u32[]{:S(2)}) %copy-start.7) | copy-done | bytes 536
  25.1 3.7 %shard_map.92 = (bf16[5,192,128]{2,1,0:T(8,128)(2,1)S(1)}, bf16[2,96,256]{2,1,0:T(8,128)(2,1)S(1)}, bf16[1,5,96,384]{3,2,1,0:T(8,128)(2,1)S(1)}) custom-call(s32[5]{0:T(128)S(1)} %pad_add_fusion.flag_ref, bf16[4,4,192,128]{3,2,1,0:T(8,128)(2,1)S(1)} %copy-done.4, bf16[4,2,192,128]{3,2,1,0:T(8,128)(2,1)S(1)} %collective-permute-done.pair_ref, ...), custom_call_target="tpu_custom_call" | custom-call | flops 1245708288 | bytes 4941332 | tf_op jit(solution)/shard_map/pallas_call | solution.py:234
  28.8 1.3 %collective-permute-start.2 = (bf16[5,192,128]{2,1,0:T(8,128)(2,1)S(1)}, bf16[5,192,128]{2,1,0:T(8,128)(2,1)S(1)}, u32[]{:S(2)}, u32[]{:S(2)}) collective-permute-start(bf16[5,192,128]{2,1,0:T(8,128)(2,1)S(1)} %get-tuple-element.22), channel_id=1, source_target_pairs={{0,8},{4,12},{8,16},{12,20},{16,24},{20,28},{24,0},{28,4},{1,9},{5... | collective-permute-start | bytes 737288 | tf_op jit(solution)/shard_map/ppermute | solution.py:19
  30.2 1.6 %collective-permute-start.11 = (bf16[1,4,192,128]{3,2,1,0:T(8,128)(2,1)S(1)}, bf16[1,4,192,128]{3,2,1,0:T(8,128)(2,1)S(1)}, u32[]{:S(2)}, u32[]{:S(2)}) collective-permute-start(bf16[1,4,192,128]{3,2,1,0:T(8,128)(2,1)S(1)} %select_select_fusion.2), channel_id=1, source_target_pairs={{0,4},{4,0},{8,12},{12,8},{16,20},{20,16},{24,28},{28,24},{1,5},{5... | collective-permute-start | bytes 589832 | tf_op jit(solution)/shard_map/ppermute | solution.py:28
  31.7 1.6 %collective-permute-start.3 = (bf16[2,96,256]{2,1,0:T(8,128)(2,1)S(1)}, bf16[2,96,256]{2,1,0:T(8,128)(2,1)S(1)}, u32[]{:S(2)}, u32[]{:S(2)}) collective-permute-start(bf16[2,96,256]{2,1,0:T(8,128)(2,1)S(1)} %get-tuple-element.23), channel_id=1, source_target_pairs={{0,8},{4,12},{8,16},{12,20},{16,24},{20,28},{24,0},{28,4},{1,9},{5... | collective-permute-start | bytes 294920 | tf_op jit(solution)/shard_map/ppermute | solution.py:19
  33.3 4.8 %shard_map.93 = (f32[5,192,128]{2,1,0:T(8,128)S(1)}, f32[5,192,128]{2,1,0:T(8,128)S(1)}, f32[192,256]{1,0:T(8,128)S(1)}) custom-call(s32[5]{0:T(128)S(1)} %pad_add_fusion.flag_ref, bf16[4,4,192,128]{3,2,1,0:T(8,128)(2,1)S(1)} %copy-done.4, bf16[4,2,192,128]{3,2,1,0:T(8,128)(2,1)S(1)} %collective-permute-done.pair_ref, ...), custom_call_target="tpu_custom_call" | custom-call | flops 1925185536 | bytes 5777940 | tf_op jit(solution)/shard_map/pallas_call | solution.py:234
  38.2 0.9 %collective-permute-done.3.tail_a_ref = bf16[2,96,256]{2,1,0:T(8,128)(2,1)S(1)} collective-permute-done((bf16[2,96,256]{2,1,0:T(8,128)(2,1)S(1)}, bf16[2,96,256]{2,1,0:T(8,128)(2,1)S(1)}, u32[]{:S(2)}, u32[]{:S(2)}) %collective-permute-start.3) | collective-permute-done | bytes 98336 | tf_op jit(solution)/shard_map/ppermute | solution.py:19
  39.1 1.2 %collective-permute-start.4 = (bf16[5,192,128]{2,1,0:T(8,128)(2,1)S(1)}, bf16[5,192,128]{2,1,0:T(8,128)(2,1)S(1)}, u32[]{:S(2)}, u32[]{:S(2)}) collective-permute-start(bf16[5,192,128]{2,1,0:T(8,128)(2,1)S(1)} %collective-permute-done.2.prior_a_ref), channel_id=1, source_target_pairs={{0,8},{4,12},{8,16},{12,20},{16,24},{20,28},{24,0},{28,4},{1,9},{5... | collective-permute-start | bytes 737288 | tf_op jit(solution)/shard_map/ppermute | solution.py:19
  41.1 7.0 %collective-permute-done.4.prior_b_ref = bf16[5,192,128]{2,1,0:T(8,128)(2,1)S(1)} collective-permute-done((bf16[5,192,128]{2,1,0:T(8,128)(2,1)S(1)}, bf16[5,192,128]{2,1,0:T(8,128)(2,1)S(1)}, u32[]{:S(2)}, u32[]{:S(2)}) %collective-permute-start.4) | collective-permute-done | bytes 245792 | tf_op jit(solution)/shard_map/ppermute | solution.py:19
  48.2 1.6 %collective-permute-start.6 = (bf16[5,192,128]{2,1,0:T(8,128)(2,1)S(1)}, bf16[5,192,128]{2,1,0:T(8,128)(2,1)S(1)}, u32[]{:S(2)}, u32[]{:S(2)}) collective-permute-start(bf16[5,192,128]{2,1,0:T(8,128)(2,1)S(1)} %select_select_fusion), channel_id=1, source_target_pairs={{0,4},{4,0},{8,12},{12,8},{16,20},{20,16},{24,28},{28,24},{1,5},{5... | collective-permute-start | bytes 737288 | tf_op jit(solution)/shard_map/ppermute | solution.py:28
  49.7 1.0 %collective-permute-start.8 = (bf16[2,96,256]{2,1,0:T(8,128)(2,1)S(1)}, bf16[2,96,256]{2,1,0:T(8,128)(2,1)S(1)}, u32[]{:S(2)}, u32[]{:S(2)}) collective-permute-start(bf16[2,96,256]{2,1,0:T(8,128)(2,1)S(1)} %select_select_fusion.3), channel_id=1, source_target_pairs={{0,4},{4,0},{8,12},{12,8},{16,20},{20,16},{24,28},{28,24},{1,5},{5... | collective-permute-start | bytes 294920 | tf_op jit(solution)/shard_map/ppermute | solution.py:28
  50.8 2.7 %shard_map.94 = (bf16[2,96,256]{2,1,0:T(8,128)(2,1)S(1)}, f32[5,192,128]{2,1,0:T(8,128)S(1)}, f32[192,256]{1,0:T(8,128)S(1)}) custom-call(s32[5]{0:T(128)S(1)} %pad_add_fusion.flag_ref, bf16[1,4,192,128]{3,2,1,0:T(8,128)(2,1)S(1)} %select_select_fusion.1.prior_ref, bf16[1,2,192,128]{3,2,1,0:T(8,128)(2,1)S(1)} %collective-permute-done.12.pair_ref, ...), custom_call_target="tpu_custom_call" | custom-call | flops 792723456 | bytes 5015572 | tf_op jit(solution)/shard_map/pallas_call | solution.py:234
  53.5 2.0 %collective-permute-done.8.tail_c_ref = bf16[2,96,256]{2,1,0:T(8,128)(2,1)S(1)} collective-permute-done((bf16[2,96,256]{2,1,0:T(8,128)(2,1)S(1)}, bf16[2,96,256]{2,1,0:T(8,128)(2,1)S(1)}, u32[]{:S(2)}, u32[]{:S(2)}) %collective-permute-start.8) | collective-permute-done | bytes 98336 | tf_op jit(solution)/shard_map/ppermute | solution.py:28
  55.5 1.8 %shard_map.95 = bf16[2,2,96,256]{3,2,1,0:T(8,128)(2,1)} custom-call(s32[5]{0:T(128)S(1)} %pad_add_fusion.flag_ref, bf16[5,192,128]{2,1,0:T(8,128)(2,1)S(1)} %collective-permute-done.2.prior_a_ref, bf16[5,192,128]{2,1,0:T(8,128)(2,1)S(1)} %collective-permute-done.4.prior_b_ref, bf16[5,192,128]{2,1,0:T(8,128)(2,1)S(1)} %collective-permute-done.6.prior_c_ref, ...), custom_call_target="tpu_custom_call" | custom-call | flops 113246208 | bytes 3785236 | tf_op jit(solution)/shard_map/pallas_call | solution.py:234
  (34 shorter events, 2.9 us)
Async XLA Ops:
  1.5 1.1 %copy-start.3 = (bf16[4,4,192,128]{3,2,1,0:T(8,128)(2,1)S(1)}, bf16[4,4,192,128]{3,2,1,0:T(8,128)(2,1)}, u32[]{:S(2)}) copy-start(bf16[4,4,192,128]{3,2,1,0:T(8,128)(2,1)} %video_ref.5) | copy-start | bytes 2359300
  3.3 16.0 %collective-permute-start = (bf16[4,2,192,128]{3,2,1,0:T(8,128)(2,1)S(1)}, bf16[4,2,192,128]{3,2,1,0:T(8,128)(2,1)S(1)}, u32[]{:S(2)}, u32[]{:S(2)}) collective-permute-start(bf16[4,2,192,128]{3,2,1,0:T(8,128)(2,1)S(1)} %get-tuple-element.20), channel_id=1, source_target_pairs={{0,1},{1,0},{2,3},{3,2},{4,5},{5,4},{6,7},{7,6},{8,9},{9,8},{10,11... | collective-permute-start | bytes 1179656 | tf_op jit(solution)/shard_map/ppermute | solution.py:28
  3.8 15.5 %collective-permute-start.1 = (bf16[4,2,192,128]{3,2,1,0:T(8,128)(2,1)S(1)}, bf16[4,2,192,128]{3,2,1,0:T(8,128)(2,1)S(1)}, u32[]{:S(2)}, u32[]{:S(2)}) collective-permute-start(bf16[4,2,192,128]{3,2,1,0:T(8,128)(2,1)S(1)} %get-tuple-element.21), channel_id=1, source_target_pairs={{1,2},{2,1},{3,0},{0,3},{5,6},{6,5},{7,4},{4,7},{9,10},{10,9},{11,... | collective-permute-start | bytes 1179656 | tf_op jit(solution)/shard_map/ppermute | solution.py:28
  6.5 8.7 %collective-permute-start.9 = (bf16[1,4,192,128]{3,2,1,0:T(8,128)(2,1)S(1)}, bf16[1,4,192,128]{3,2,1,0:T(8,128)(2,1)S(1)}, u32[]{:S(2)}, u32[]{:S(2)}) collective-permute-start(bf16[1,4,192,128]{3,2,1,0:T(8,128)(2,1)S(1)} %get-tuple-element.28), channel_id=1, source_target_pairs={{0,8},{4,12},{8,16},{12,20},{16,24},{20,28},{24,0},{28,4},{1,9},{5... | collective-permute-start | bytes 589832 | tf_op jit(solution)/shard_map/ppermute | solution.py:19
  15.2 14.9 %collective-permute-start.10 = (bf16[1,4,192,128]{3,2,1,0:T(8,128)(2,1)S(1)}, bf16[1,4,192,128]{3,2,1,0:T(8,128)(2,1)S(1)}, u32[]{:S(2)}, u32[]{:S(2)}) collective-permute-start(bf16[1,4,192,128]{3,2,1,0:T(8,128)(2,1)S(1)} %collective-permute-done.9), channel_id=1, source_target_pairs={{0,8},{4,12},{8,16},{12,20},{16,24},{20,28},{24,0},{28,4},{1,9},{5... | collective-permute-start | bytes 589832 | tf_op jit(solution)/shard_map/ppermute | solution.py:19
  15.2 3.5 %collective-permute-start.5 = (s32[1]{0:T(128)}, s32[1]{0:T(128)}, u32[]{:S(2)}, u32[]{:S(2)}) collective-permute-start(s32[1]{0:T(128)} %select_n.100), channel_id=1, source_target_pairs={{0,4},{4,0},{8,12},{12,8},{16,20},{20,16},{24,28},{28,24},{1,5},{5... | collective-permute-start | bytes 20 | tf_op jit(solution)/shard_map/ppermute | solution.py:28
  19.3 1.5 %copy-start = (bf16[3,3,3,128,256]{4,3,2,1,0:T(8,128)(2,1)S(1)}, bf16[3,3,3,128,256]{4,3,2,1,0:T(8,128)(2,1)}, u32[]{:S(2)}) copy-start(bf16[3,3,3,128,256]{4,3,2,1,0:T(8,128)(2,1)} %param.16) | copy-start | bytes 5308420
  20.8 1.2 %copy-start.2 = (bf16[3,3,3,128,128]{4,3,2,1,0:T(8,128)(2,1)S(1)}, bf16[3,3,3,128,128]{4,3,2,1,0:T(8,128)(2,1)}, u32[]{:S(2)}) copy-start(bf16[3,3,3,128,128]{4,3,2,1,0:T(8,128)(2,1)} %param.13) | copy-start | bytes 2654212
  22.0 1.1 %copy-start.4 = (bf16[4,4,192,128]{3,2,1,0:T(8,128)(2,1)S(1)}, bf16[4,4,192,128]{3,2,1,0:T(8,128)(2,1)}, u32[]{:S(2)}) copy-start(bf16[4,4,192,128]{3,2,1,0:T(8,128)(2,1)} %video_ref.5) | copy-start | bytes 2359300
  23.1 0.7 %copy-start.5 = (f32[128]{0:T(128)S(1)}, f32[128]{0:T(128)}, u32[]{:S(2)}) copy-start(f32[128]{0:T(128)} %param.15) | copy-start | bytes 1540
  23.8 0.7 %copy-start.7 = (f32[128]{0:T(128)S(1)}, f32[128]{0:T(128)}, u32[]{:S(2)}) copy-start(f32[128]{0:T(128)} %param.12) | copy-start | bytes 1540
  24.4 0.7 %copy-start.8 = (f32[128]{0:T(128)S(1)}, f32[128]{0:T(128)}, u32[]{:S(2)}) copy-start(f32[128]{0:T(128)} %param.14) | copy-start | bytes 1540
  25.1 8.2 %copy-start.6 = (f32[256]{0:T(256)S(1)}, f32[256]{0:T(256)}, u32[]{:S(2)}) copy-start(f32[256]{0:T(256)} %param.17) | copy-start | bytes 3076
  28.8 10.3 %collective-permute-start.2 = (bf16[5,192,128]{2,1,0:T(8,128)(2,1)S(1)}, bf16[5,192,128]{2,1,0:T(8,128)(2,1)S(1)}, u32[]{:S(2)}, u32[]{:S(2)}) collective-permute-start(bf16[5,192,128]{2,1,0:T(8,128)(2,1)S(1)} %get-tuple-element.22), channel_id=1, source_target_pairs={{0,8},{4,12},{8,16},{12,20},{16,24},{20,28},{24,0},{28,4},{1,9},{5... | collective-permute-start | bytes 737288 | tf_op jit(solution)/shard_map/ppermute | solution.py:19
  30.2 10.2 %collective-permute-start.11 = (bf16[1,4,192,128]{3,2,1,0:T(8,128)(2,1)S(1)}, bf16[1,4,192,128]{3,2,1,0:T(8,128)(2,1)S(1)}, u32[]{:S(2)}, u32[]{:S(2)}) collective-permute-start(bf16[1,4,192,128]{3,2,1,0:T(8,128)(2,1)S(1)} %select_select_fusion.2), channel_id=1, source_target_pairs={{0,4},{4,0},{8,12},{12,8},{16,20},{20,16},{24,28},{28,24},{1,5},{5... | collective-permute-start | bytes 589832 | tf_op jit(solution)/shard_map/ppermute | solution.py:28
  31.7 7.4 %collective-permute-start.3 = (bf16[2,96,256]{2,1,0:T(8,128)(2,1)S(1)}, bf16[2,96,256]{2,1,0:T(8,128)(2,1)S(1)}, u32[]{:S(2)}, u32[]{:S(2)}) collective-permute-start(bf16[2,96,256]{2,1,0:T(8,128)(2,1)S(1)} %get-tuple-element.23), channel_id=1, source_target_pairs={{0,8},{4,12},{8,16},{12,20},{16,24},{20,28},{24,0},{28,4},{1,9},{5... | collective-permute-start | bytes 294920 | tf_op jit(solution)/shard_map/ppermute | solution.py:19
  38.2 12.6 %copy-start.1 = (bf16[3,3,3,128,256]{4,3,2,1,0:T(8,128)(2,1)S(1)}, bf16[3,3,3,128,256]{4,3,2,1,0:T(8,128)(2,1)}, u32[]{:S(2)}) copy-start(bf16[3,3,3,128,256]{4,3,2,1,0:T(8,128)(2,1)} %param.16) | copy-start | bytes 5308420
  39.1 9.0 %collective-permute-start.4 = (bf16[5,192,128]{2,1,0:T(8,128)(2,1)S(1)}, bf16[5,192,128]{2,1,0:T(8,128)(2,1)S(1)}, u32[]{:S(2)}, u32[]{:S(2)}) collective-permute-start(bf16[5,192,128]{2,1,0:T(8,128)(2,1)S(1)} %collective-permute-done.2.prior_a_ref), channel_id=1, source_target_pairs={{0,8},{4,12},{8,16},{12,20},{16,24},{20,28},{24,0},{28,4},{1,9},{5... | collective-permute-start | bytes 737288 | tf_op jit(solution)/shard_map/ppermute | solution.py:19
  40.4 10.4 %collective-permute-start.13 = (bf16[1,2,192,128]{3,2,1,0:T(8,128)(2,1)S(1)}, bf16[1,2,192,128]{3,2,1,0:T(8,128)(2,1)S(1)}, u32[]{:S(2)}, u32[]{:S(2)}) collective-permute-start(bf16[1,2,192,128]{3,2,1,0:T(8,128)(2,1)S(1)} %get-tuple-element.35), channel_id=1, source_target_pairs={{1,2},{2,1},{3,0},{0,3},{5,6},{6,5},{7,4},{4,7},{9,10},{10,9},{11,... | collective-permute-start | bytes 294920 | tf_op jit(solution)/shard_map/ppermute | solution.py:28
  40.5 10.3 %collective-permute-start.12 = (bf16[1,2,192,128]{3,2,1,0:T(8,128)(2,1)S(1)}, bf16[1,2,192,128]{3,2,1,0:T(8,128)(2,1)S(1)}, u32[]{:S(2)}, u32[]{:S(2)}) collective-permute-start(bf16[1,2,192,128]{3,2,1,0:T(8,128)(2,1)S(1)} %get-tuple-element.36), channel_id=1, source_target_pairs={{0,1},{1,0},{2,3},{3,2},{4,5},{5,4},{6,7},{7,6},{8,9},{9,8},{10,11... | collective-permute-start | bytes 294920 | tf_op jit(solution)/shard_map/ppermute | solution.py:28
  41.1 8.6 %collective-permute-start.7 = (bf16[2,96,256]{2,1,0:T(8,128)(2,1)S(1)}, bf16[2,96,256]{2,1,0:T(8,128)(2,1)S(1)}, u32[]{:S(2)}, u32[]{:S(2)}) collective-permute-start(bf16[2,96,256]{2,1,0:T(8,128)(2,1)S(1)} %collective-permute-done.3.tail_a_ref), channel_id=1, source_target_pairs={{0,8},{4,12},{8,16},{12,20},{16,24},{20,28},{24,0},{28,4},{1,9},{5... | collective-permute-start | bytes 294920 | tf_op jit(solution)/shard_map/ppermute | solution.py:19
  48.2 7.3 %collective-permute-start.6 = (bf16[5,192,128]{2,1,0:T(8,128)(2,1)S(1)}, bf16[5,192,128]{2,1,0:T(8,128)(2,1)S(1)}, u32[]{:S(2)}, u32[]{:S(2)}) collective-permute-start(bf16[5,192,128]{2,1,0:T(8,128)(2,1)S(1)} %select_select_fusion), channel_id=1, source_target_pairs={{0,4},{4,0},{8,12},{12,8},{16,20},{20,16},{24,28},{28,24},{1,5},{5... | collective-permute-start | bytes 737288 | tf_op jit(solution)/shard_map/ppermute | solution.py:28
  49.7 5.7 %collective-permute-start.8 = (bf16[2,96,256]{2,1,0:T(8,128)(2,1)S(1)}, bf16[2,96,256]{2,1,0:T(8,128)(2,1)S(1)}, u32[]{:S(2)}, u32[]{:S(2)}) collective-permute-start(bf16[2,96,256]{2,1,0:T(8,128)(2,1)S(1)} %select_select_fusion.3), channel_id=1, source_target_pairs={{0,4},{4,0},{8,12},{12,8},{16,20},{20,16},{24,28},{28,24},{1,5},{5... | collective-permute-start | bytes 294920 | tf_op jit(solution)/shard_map/ppermute | solution.py:28

commit v3 on v1

v3 whole, which is shorter than its diff:
```python
import functools

import jax
import jax.numpy as jnp
from jax import lax
from jax.experimental import pallas as pl
from jax.experimental.pallas import tpu as pltpu
from jax.sharding import PartitionSpec as P

ABOVE = 2
EVEN, TOP, FULL, DISTANCE, BOTTOM, EVEN_GROUP = range(6)
PACK = 30_000_000_000
VMEM = pltpu.VMEM
F32 = jnp.float32
BF16 = jnp.bfloat16


def rotated(value, axis, steps):
    count = lax.axis_size(axis)
    return lax.ppermute(value, axis, [(source, (source + steps) % count) for source in range(count)])


def relayed(value):
    groups, rows = lax.axis_size("group"), lax.axis_size("row")
    pairs = []
    for group in range(groups):
        for row in range(rows):
            if group < 2:
                target = (group, row ^ 1)
            else:
                target = (group + 2 if group + 2 < groups else group + 4 - groups, row)
            pairs.append((group * rows + row, target[0] * rows + target[1]))
    return lax.ppermute(value, ("group", "row"), pairs)


def swapped(value, axis):
    return lax.ppermute(value, axis, [(place, place ^ 1) for place in range(lax.axis_size(axis))])


def crossed_within(value):
    rows = lax.axis_size("row")
    return lax.ppermute(
        value, "row", [(row, (((row + 1) ^ 1) - 1) % rows) for row in range(rows)]
    )


def crossed(value):
    groups, rows = lax.axis_size("group"), lax.axis_size("row")
    pairs = []
    for group in range(groups):
        for row in range(rows):
            outer = row in (0, rows - 1)
            target = (group ^ 1, row) if outer else (group, ((row + 1) ^ 1) - 1)
            pairs.append((group * rows + row, target[0] * rows + target[1]))
    return lax.ppermute(value, ("group", "row"), pairs)


def after(first, *values):
    return lax.optimization_barrier((first,) + values)[1:]


def pixel_silu(values, gain):
    inverse = lax.rsqrt(jnp.mean(values * values, axis=-1, keepdims=True) + 1e-06)
    half = values * inverse * (0.5 * gain)
    return half + half * jnp.tanh(half)


def column_window(row):
    width = row.shape[0]
    column = lax.broadcasted_iota(jnp.int32, row.shape, 0)
    left = jnp.where(column == 0, 0.0, pltpu.roll(row, 1, 0))
    right = jnp.where(column == width - 1, 0.0, pltpu.roll(row, width - 1, 0))
    return jnp.concatenate([left.astype(BF16), row.astype(BF16), right.astype(BF16)], axis=-1)


def holds(flag_ref, index):
    return flag_ref[index : index + 1] != 0


def fill_hidden(read, gain, window_ref, frame, rows):
    for row in rows:
        window_ref[frame, row] = column_window(pixel_silu(read(row), gain))


def conv1_rows(window_ref, frame, rows, weight):
    width, depth = window_ref.shape[2], window_ref.shape[3]
    window = jnp.concatenate(
        [window_ref[frame, tap : tap + rows].reshape(rows * width, depth) for tap in range(3)],
        axis=-1,
    )
    return jnp.dot(window, weight.reshape(3 * depth, weight.shape[2]), preferred_element_type=F32)


def fill_second(values, gain, first_row, stage_ref, strided_ref, slot):
    rows, half = strided_ref.shape[1], strided_ref.shape[2]
    width, channels = 2 * half, stage_ref.shape[2]
    for row in range(rows):
        ready = pixel_silu(values(row), gain).astype(BF16).astype(F32)
        if row == 0:
            ready = jnp.where(first_row, 0.0, ready)
        stage_ref[row, 0:8] = jnp.zeros((8, channels), F32)
        stage_ref[row, 8 : 8 + width] = ready
        strided_ref[slot, row] = jnp.concatenate(
            [stage_ref[row, pl.ds(7 + tap, half, stride=2), :].astype(BF16) for tap in range(3)],
            axis=-1,
        )


def conv2_frame(strided_ref, slot, weight_ref, step):
    total = None
    for tap in range(3):
        window = jnp.concatenate([strided_ref[slot, tap], strided_ref[slot, tap + 2]], axis=0)
        part = jnp.dot(window, weight_ref[step, tap], preferred_element_type=F32)
        total = part if total is None else total + part
    return total


def row_reader(flag_ref, video_ref, frame, pair_ref, cross_ref):
    even, top, bottom = holds(flag_ref, EVEN), holds(flag_ref, TOP), holds(flag_ref, BOTTOM)
    rows = video_ref.shape[1]

    def read(row):
        if ABOVE <= row < ABOVE + rows:
            return video_ref[frame, row - ABOVE].astype(F32)
        if row < ABOVE:
            first, second, outside = cross_ref[frame, row], pair_ref[frame, row], top
        else:
            first, second, outside = pair_ref[frame, 0], cross_ref[frame, 0], bottom
        value = jnp.where(even, first.astype(F32), second.astype(F32))
        return jnp.where(outside, 0.0, value)

    return read


def pack_kernel(flag_ref, video_ref, own_ref, pair_ref, cross_ref):
    even = holds(flag_ref, EVEN)
    frames, rows = video_ref.shape[:2]
    own_ref[...] = video_ref[frames - 2 :]
    split_edges(even, video_ref, frames, rows, pair_ref, cross_ref)


def split_edges(even, source_ref, frames, rows, pair_ref, cross_ref):
    for frame in range(frames):
        for row in range(ABOVE):
            high, low = source_ref[frame, row], source_ref[frame, rows - ABOVE + row]
            pair_ref[frame, row] = jnp.where(even, low, high)
            cross_ref[frame, row] = jnp.where(even, high, low)


def beside(weight_ref, *steps):
    return jnp.concatenate([weight_ref[step] for step in steps], axis=-1)


def own_kernel(
    flag_ref, video_ref, pair_ref, cross_ref, gain1_ref, weight1_ref, bias1_ref,
    gain2_ref, weight2_ref, bias2_ref, tail_ref, first_ref, next_ref, late_ref,
    window_ref, stage_ref, strided_ref, total_ref,
):
    first_row = holds(flag_ref, TOP)
    channels = video_ref.shape[3]
    readers = [row_reader(flag_ref, video_ref, f, pair_ref, cross_ref) for f in range(4)]
    for frame in range(4):
        fill_hidden(readers[frame], gain1_ref[...], window_ref, frame, range(7))
    zero = conv1_rows(window_ref, 0, 5, beside(weight1_ref, 0, 1))
    one = conv1_rows(window_ref, 1, 5, beside(weight1_ref, 1, 2))
    two = conv1_rows(window_ref, 2, 5, beside(weight1_ref, 2, 1))
    next_ref[...] = (zero[:, channels:] + one[:, channels:]).reshape(next_ref.shape)
    total_ref[0] = (zero[:, :channels] + one[:, :channels] + two[:, :channels]).reshape(next_ref.shape)
    total_ref[1] = (
        two[:, channels:]
        + conv1_rows(window_ref, 1, 5, weight1_ref[0])
        + conv1_rows(window_ref, 3, 5, weight1_ref[2])
    ).reshape(next_ref.shape)
    first_ref[...] = conv1_rows(window_ref, 0, 5, weight1_ref[2]).reshape(first_ref.shape)
    for row in range(5):
        next_ref[row] += readers[1](row + 1) + bias1_ref[...]
        first_ref[row] += readers[0](row + 1) + bias1_ref[...]
    for slot in range(2):
        fill_second(
            lambda row: total_ref[slot, row] + readers[2 + slot](row + 1) + bias1_ref[...],
            gain2_ref[...], first_row, stage_ref, strided_ref, slot,
        )
    late_ref[...] = (
        conv2_frame(strided_ref, 0, weight2_ref, 1)
        + conv2_frame(strided_ref, 1, weight2_ref, 2)
        + bias2_ref[...]
    )
    tail = conv2_frame(strided_ref, 1, weight2_ref, 0).astype(BF16)
    half = strided_ref.shape[2]
    for row in range(tail_ref.shape[0]):
        for part in range(2):
            tail_ref[row, part * half : (part + 1) * half] = tail[
                row * half : (row + 1) * half, part * channels : (part + 1) * channels
            ]


def chosen(distance, two, four, odd):
    value = jnp.where(distance == 2, two, odd)
    value = jnp.where(distance == 4, four, value)
    return jnp.where(distance == 0, 0.0, value)


def partner_kernel(flag_ref, wanted_ref, own_ref, near_ref, far_ref, out_ref):
    first, one = holds(flag_ref, EVEN_GROUP), wanted_ref[0:1] == 1
    for row in range(out_ref.shape[0]):
        own, near, far = own_ref[row], near_ref[row], far_ref[row]
        out_ref[row] = jnp.where(
            first, jnp.where(one, own, near), jnp.where(one, near, far)
        )


def prior_kernel(
    flag_ref, two_ref, four_ref, odd_ref, prior_ref, pair_ref, cross_ref,
):
    even, distance = holds(flag_ref, EVEN), flag_ref[DISTANCE : DISTANCE + 1]
    frames, rows = prior_ref.shape[:2]
    for frame in range(frames):
        for row in range(rows):
            at = frame * rows + row
            prior_ref[frame, row] = chosen(distance, two_ref[at], four_ref[at], odd_ref[at])
    split_edges(even, prior_ref, frames, rows, pair_ref, cross_ref)


def inner_kernel(
    flag_ref, prior_ref, gain1_ref, weight1_ref, first_ref, next_ref, first_out_ref, next_out_ref,
    window_ref,
):
    del flag_ref
    rows, width, channels = prior_ref.shape[1:]
    for frame in range(2):
        fill_hidden(
            lambda row: prior_ref[frame, row].astype(F32), gain1_ref[...], window_ref, frame, range(rows)
        )
    first_out_ref[...] = first_ref[...]
    next_out_ref[...] = next_ref[...]
    for tap in range(3):
        low = max(0, ABOVE - tap)
        count = min(rows + 1, rows + ABOVE - tap) - low
        start = low + tap - ABOVE
        shape = (count, width, channels)

        def part(frame, weight):
            window = window_ref[frame, start : start + count]
            return jnp.dot(
                window.reshape(count * width, window.shape[2]), weight, preferred_element_type=F32
            )

        both = part(1, beside(weight1_ref.at[:, tap], 0, 1))
        next_out_ref[low : low + count] += both[:, :channels].reshape(shape)
        first_out_ref[low : low + count] += (
            both[:, channels:] + part(0, weight1_ref[0, tap])
        ).reshape(shape)


def last_kernel(
    flag_ref, prior_ref, pair_ref, cross_ref, gain1_ref, weight1_ref, gain2_ref,
    weight2_ref, bias2_ref, first_ref, next_ref, late_ref, two_ref, four_ref, odd_ref, out_ref,
    window_ref, stage_ref, strided_ref, total_ref,
):
    first_row, keep, distance = holds(flag_ref, TOP), holds(flag_ref, FULL), flag_ref[DISTANCE : DISTANCE + 1]
    rows, width, channels = prior_ref.shape[1:]
    outer = (0, 1, rows + ABOVE)
    for frame in range(2):
        reader = row_reader(flag_ref, prior_ref, frame, pair_ref, cross_ref)
        fill_hidden(
            lambda slot: reader(outer[slot]), gain1_ref[...], window_ref, frame, range(len(outer))
        )
    total_ref[0] = next_ref[...]
    total_ref[1] = first_ref[...]
    for slot, place in enumerate(outer):
        for tap in range(3):
            target = place - tap
            if 0 <= target <= rows:
                both = jnp.dot(
                    window_ref[1, slot], beside(weight1_ref.at[:, tap], 0, 1), preferred_element_type=F32
                )
                total_ref[0, target] += both[:, :channels]
                total_ref[1, target] += both[:, channels:] + jnp.dot(
                    window_ref[0, slot], weight1_ref[0, tap], preferred_element_type=F32
                )
    for slot in range(2):
        fill_second(
            lambda row: total_ref[slot, row],
            gain2_ref[...], first_row, stage_ref, strided_ref, slot,
        )
    shape = out_ref.shape[1:]
    half = strided_ref.shape[2]
    late = late_ref[...] + conv2_frame(strided_ref, 0, weight2_ref, 0)
    out_ref[1] = jnp.where(jnp.concatenate([keep, keep], axis=-1), late, 0.0).astype(BF16).reshape(shape)
    early = conv2_frame(strided_ref, 0, weight2_ref, 2) + conv2_frame(strided_ref, 1, weight2_ref, 1)
    for row in range(shape[0]):
        tail = chosen(
            distance, two_ref[row].astype(F32), four_ref[row].astype(F32), odd_ref[row].astype(F32)
        )
        tail = jnp.concatenate([tail[:half], tail[half:]], axis=-1)
        part = early[row * half : (row + 1) * half] + bias2_ref[...]
        out_ref[0, row] = (part + tail).astype(BF16)


def call(kernel, operands, outs, scratch, flops=0):
    moved = sum(o.size * o.dtype.itemsize for o in list(operands) + list(outs))
    return pl.pallas_call(
        kernel,
        out_shape=outs,
        in_specs=[pl.BlockSpec(memory_space=VMEM)] * len(operands),
        out_specs=[pl.BlockSpec(memory_space=VMEM)] * len(outs),
        scratch_shapes=scratch,
        compiler_params=pltpu.CompilerParams(vmem_limit_bytes=14 * 1024 * 1024),
        cost_estimate=pl.CostEstimate(flops=flops, bytes_accessed=moved, transcendentals=0),
    )(*operands)


def per_device(
    video_frames, pred_owner, frame_counts, norm1_gain, conv1_weight, conv1_bias, norm2_gain,
    conv2_weight, conv2_bias,
):
    frames, rows, width, channels = video_frames.shape
    wide = conv2_weight.shape[-1]
    half = width // 2
    position = lax.axis_index("group")
    band = lax.axis_index("row")
    distance = jnp.where(pred_owner[0] >= 0, position - pred_owner[0], 0)
    marks = [
        band % 2 == 0, band == 0, frame_counts[0] >= frames, distance,
        band == lax.axis_size("row") - 1, position % 2 == 0,
    ]
    marks += [0] * (8 - len(marks))
    flags = jnp.stack([jnp.full((channels,), mark, F32) for mark in marks])

    def like(value, dtype=BF16):
        return jax.ShapeDtypeStruct(value, dtype)

    def window(count, high):
        return VMEM((count, high, width, 3 * channels), BF16)

    def for_partner(own, near, far):
        return call(partner_kernel, [flags, wanted, own, near, far], [like(own.shape)], [])[0]

    weight1 = conv1_weight.reshape(3, 3, 3 * channels, channels)
    weight2 = conv2_weight.reshape(3, 3, 3 * channels, wide)
    gain1, bias1 = norm1_gain[None], conv1_bias[None]
    gain2, bias2 = norm2_gain[None], conv2_bias[None]
    pair_of = like((2, rows, width, channels))
    flat = (2 * rows, width, channels)
    total = (rows + 1, width, channels)
    stage = VMEM((rows + 1, width + 16, channels), F32)
    strided = VMEM((2, rows + 1, half, 3 * channels), BF16)
    one_tap = 2 * (rows + 1) * width * 9 * channels * channels
    one_code = 2 * (rows // 2) * half * 9 * channels * wide

    edge = like((frames, ABOVE, width, channels))
    own, pair, cross = call(
        pack_kernel, [flags, video_frames], [pair_of, edge, edge], [], flops=PACK
    )
    wanted = swapped(jnp.full((8, channels), distance, F32), "group")
    cross = crossed(after(wanted, cross)[0])
    own = own.reshape(flat)
    near = rotated(own, "group", 2)
    pair = swapped(pair, "row")
    far = relayed(near)
    pair, cross = after(near, pair, cross)
    own_e, first, following, late = call(
        own_kernel,
        [flags, video_frames, pair, cross, gain1, weight1, bias1, gain2, weight2, bias2],
        [
            like((rows // 2, width, channels)), like(total, F32), like(total, F32),
            like((rows // 2 * half, wide), F32),
        ],
        [window(4, rows + 3), stage, strided, VMEM((2,) + total, F32)],
        flops=9 * one_tap + 3 * one_code,
    )
    chosen_own = for_partner(own, near, after(own_e, far)[0])
    odd = swapped(chosen_own, "group")
    near_e = rotated(own_e, "group", 2)
    far_e = relayed(near_e)
    odd_e = swapped(for_partner(own_e, near_e, far_e), "group")
    edge = like((2, ABOVE, width, channels))
    prior, prior_pair, prior_cross = call(
        prior_kernel, [flags, near, far, odd], [pair_of, edge, edge], []
    )
    prior_cross = crossed_within(prior_cross)
    prior_pair = swapped(prior_pair, "row")
    first, following = call(
        inner_kernel,
        [flags, prior, gain1, weight1, first, following],
        [like(total, F32), like(total, F32)],
        [window(2, rows)],
        flops=2 * one_tap,
    )
    return call(
        last_kernel,
        [flags, prior, prior_pair, prior_cross, gain1, weight1, gain2, weight2, bias2, first,
         following, late, near_e, far_e, odd_e],
        [like((frames // 2, rows // 2, half, wide))],
        [window(2, 3), stage, strided, VMEM((2,) + total, F32)],
        flops=one_tap + 3 * one_code,
    )[0]


def solution(mesh):
    placed = (P("group", "row", None, None), P("group"), P("group"), P(), P(), P(), P(), P(), P())
    return jax.shard_map(
        per_device,
        mesh=mesh,
        in_specs=placed,
        out_specs=P("group", "row", None, None),
        check_vma=False,
    )
```

time: 60.5 us -> 43.8 us (0.72)
  starting transfers between devices: 32.8 us -> 16.3 us
  waiting for transfers between devices: 6.81 us -> 14.8 us
  Pallas kernels: 12.9 us -> 9.15 us
  other arithmetic: 2.38 us -> 0 us
  local copies, waits for them, and re-layouts: 2.96 us -> 1.21 us
  between operations: 2.2 us -> 1.51 us
    ppermute x14 -> x11, starting transfers between devices: 32.8 us -> 16.3 us  [the longest x2 8.47 us: rotated(): lax.ppermute(value, axis, [(source, (source + steps) % count) for source...]
    ppermute x14 -> x11, waiting for transfers between devices: 6.81 us -> 14.8 us  [the longest x2 9.76 us: rotated(): lax.ppermute(value, axis, [(source, (source + steps) % count) for source...]
    pallas_call x4 -> x7, Pallas kernels: 12.9 us -> 9.15 us  [call(): pl.pallas_call(kernel, out_shape=outs, in_specs=[pl.BlockSpec(memory_spac...]
    select_n x6 -> x0, other arithmetic: 2.22 us -> none  [the longest x2 2.07 us: row_halo(): cross = swapped(jnp.where(even, high, low), 'row', 1)]
    slice x1 -> x0, local copies, waits for them, and re-layouts: 1.77 us -> none  [per_device(): own_a = lax.slice_in_dim(video_frames, frames - 1, frames, axis=0)]
  transfers between devices with their start and end apart: 14 -> 11, of which waited for: 3 -> 7; matrix products, arithmetic and copies ran while one was open for 4% -> 0% of each run, Pallas kernels for 19% -> 15%
where the time goes in v3:
time: 43.8 us; the launch traced here: 43 us
  starting transfers between devices  16.3 us (37%)
  waiting for transfers between devices  14.8 us (34%)
  Pallas kernels  9.15 us (21%)
  between operations  1.51 us (3%)
  local copies, waits for them, and re-layouts  1.21 us (3%)
    ppermute x2, waiting for transfers between devices, rotated(): lax.ppermute(value, axis, [(source, (source + steps) % count) for source...  9.76 us
    pallas_call x7, Pallas kernels, call(): pl.pallas_call(kernel, out_shape=outs, in_specs=[pl.BlockSpec(memory_spac...  9.15 us
    ppermute x2, starting transfers between devices, rotated(): lax.ppermute(value, axis, [(source, (source + steps) % count) for source...  8.47 us
    ppermute x5, starting transfers between devices, swapped(): lax.ppermute(value, axis, [(place, place ^ 1) for place in range(lax.axis...  4.68 us
    ppermute x5, waiting for transfers between devices, swapped(): lax.ppermute(value, axis, [(place, place ^ 1) for place in range(lax.axis...  4.64 us
    ppermute x1, starting transfers between devices, crossed_within(): lax.ppermute(value, 'row', [(row, ((row + 1 ^ 1) - 1) % rows) for row in...  1.64 us
    ppermute x1, starting transfers between devices, crossed(): return lax.ppermute(value, ('group', 'row'), pairs)  1.49 us
    unnamed x16, local copies, waits for them, and re-layouts  1.16 us
  transfers between devices with their start and end apart: 11, of which 7 were waited for; matrix products, arithmetic and copies ran while one was open for 0% of the time, Pallas kernels for 15%

profile of v3, /device:TPU:0, one launch (start us, length us, event | category | flops | bytes accessed | tf_op | source)
XLA Modules:
  0.0 43.0 jit_solution(18156478094649483394)
XLA Ops:
  1.4 1.1 %copy-done.5 = bf16[4,4,192,128]{3,2,1,0:T(8,128)(2,1)S(1)} copy-done((bf16[4,4,192,128]{3,2,1,0:T(8,128)(2,1)S(1)}, bf16[4,4,192,128]{3,2,1,0:T(8,128)(2,1)}, u32[]{:S(2)}) %copy-start.5) | copy-done | bytes 786456
  2.6 0.0 copy-start.4
  2.6 0.0 copy-start.7
  2.6 0.2 shard_map.91
  2.8 3.1 %collective-permute-start = (bf16[8,192,128]{2,1,0:T(8,128)(2,1)S(1)}, bf16[8,192,128]{2,1,0:T(8,128)(2,1)S(1)}, u32[]{:S(2)}, u32[]{:S(2)}) collective-permute-start(bf16[8,192,128]{2,1,0:T(8,128)(2,1)S(1)} %bitcast.16), channel_id=1, source_target_pairs={{0,8},{4,12},{8,16},{12,20},{16,24},{20,28},{24,0},{28,4},{1,9},{5... | collective-permute-start | bytes 1179656 | tf_op jit(solution)/shard_map/ppermute | solution.py:20
  5.8 1.5 %collective-permute-start.2 = (f32[8,128]{1,0:T(8,128)S(1)}, f32[8,128]{1,0:T(8,128)S(1)}, u32[]{:S(2)}, u32[]{:S(2)}) collective-permute-start(f32[8,128]{1,0:T(8,128)S(1)} %broadcast_in_dim.15), channel_id=1, source_target_pairs={{0,4},{4,0},{8,12},{12,8},{16,20},{20,16},{24,28},{28,24},{1,5},{5... | collective-permute-start | bytes 12296 | tf_op jit(solution)/shard_map/ppermute | solution.py:37
  7.3 2.1 %collective-permute-done.2.wanted_ref = f32[8,128]{1,0:T(8,128)S(1)} collective-permute-done((f32[8,128]{1,0:T(8,128)S(1)}, f32[8,128]{1,0:T(8,128)S(1)}, u32[]{:S(2)}, u32[]{:S(2)}) %collective-permute-start.2) | collective-permute-done | bytes 4128 | tf_op jit(solution)/shard_map/ppermute | solution.py:37
  9.5 1.5 %collective-permute-start.4 = (bf16[4,2,192,128]{3,2,1,0:T(8,128)(2,1)S(1)}, bf16[4,2,192,128]{3,2,1,0:T(8,128)(2,1)S(1)}, u32[]{:S(2)}, u32[]{:S(2)}) collective-permute-start(bf16[4,2,192,128]{3,2,1,0:T(8,128)(2,1)S(1)} %get-tuple-element.24), channel_id=1, source_target_pairs={{0,4},{1,2},{2,1},{3,7},{4,0},{5,6},{6,5},{7,3},{8,12},{9,10},{10,... | collective-permute-start | bytes 1179656 | tf_op jit(solution)/shard_map/ppermute | solution.py:55
  10.9 6.0 %collective-permute-done.near_ref.two_ref = bf16[8,192,128]{2,1,0:T(8,128)(2,1)S(1)} collective-permute-done((bf16[8,192,128]{2,1,0:T(8,128)(2,1)S(1)}, bf16[8,192,128]{2,1,0:T(8,128)(2,1)S(1)}, u32[]{:S(2)}, u32[]{:S(2)}) %collective-permute-start) | collective-permute-done | bytes 393248 | tf_op jit(solution)/shard_map/ppermute | solution.py:20
  17.0 0.2 collective-permute-done.4.cross_ref
  17.3 4.9 %shard_map.92 = (bf16[2,192,128]{2,1,0:T(8,128)(2,1)S(1)}, f32[5,192,128]{2,1,0:T(8,128)S(1)}, f32[5,192,128]{2,1,0:T(8,128)S(1)}, f32[192,256]{1,0:T(8,128)S(1)}) custom-call(f32[8,128]{1,0:T(8,128)S(1)} %stack.7.flag_ref, bf16[4,4,192,128]{3,2,1,0:T(8,128)(2,1)S(1)} %copy-done.6, bf16[4,2,192,128]{3,2,1,0:T(8,128)(2,1)S(1)} %collective-permute-done.3.pair_ref, ...), custom_call_target="tpu_custom_call" | custom-call | flops 2887778304 | bytes 5511680 | tf_op jit(solution)/shard_map/pallas_call | solution.py:302
  22.2 0.1 shard_map.93
  22.3 1.6 %collective-permute-start.5 = (bf16[8,192,128]{2,1,0:T(8,128)(2,1)S(1)}, bf16[8,192,128]{2,1,0:T(8,128)(2,1)S(1)}, u32[]{:S(2)}, u32[]{:S(2)}) collective-permute-start(bf16[8,192,128]{2,1,0:T(8,128)(2,1)S(1)} %shard_map.93), channel_id=1, source_target_pairs={{0,4},{4,0},{8,12},{12,8},{16,20},{20,16},{24,28},{28,24},{1,5},{5... | collective-permute-start | bytes 1179656 | tf_op jit(solution)/shard_map/ppermute | solution.py:37
  23.9 5.4 %collective-permute-start.8 = (bf16[2,192,128]{2,1,0:T(8,128)(2,1)S(1)}, bf16[2,192,128]{2,1,0:T(8,128)(2,1)S(1)}, u32[]{:S(2)}, u32[]{:S(2)}) collective-permute-start(bf16[2,192,128]{2,1,0:T(8,128)(2,1)S(1)} %get-tuple-element.27.own_ref), channel_id=1, source_target_pairs={{0,8},{4,12},{8,16},{12,20},{16,24},{20,28},{24,0},{28,4},{1,9},{5... | collective-permute-start | bytes 294920 | tf_op jit(solution)/shard_map/ppermute | solution.py:20
  29.3 3.7 %collective-permute-done.8.near_ref.two_ref = bf16[2,192,128]{2,1,0:T(8,128)(2,1)S(1)} collective-permute-done((bf16[2,192,128]{2,1,0:T(8,128)(2,1)S(1)}, bf16[2,192,128]{2,1,0:T(8,128)(2,1)S(1)}, u32[]{:S(2)}, u32[]{:S(2)}) %collective-permute-start.8) | collective-permute-done | bytes 98336 | tf_op jit(solution)/shard_map/ppermute | solution.py:20
  33.0 0.7 %collective-permute-done.5.odd_ref = bf16[8,192,128]{2,1,0:T(8,128)(2,1)S(1)} collective-permute-done((bf16[8,192,128]{2,1,0:T(8,128)(2,1)S(1)}, bf16[8,192,128]{2,1,0:T(8,128)(2,1)S(1)}, u32[]{:S(2)}, u32[]{:S(2)}) %collective-permute-start.5) | collective-permute-done | bytes 393248 | tf_op jit(solution)/shard_map/ppermute | solution.py:37
  33.7 0.2 shard_map.94
  33.9 0.1 collective-permute-start.6
  34.0 1.6 %collective-permute-start.7 = (bf16[2,2,192,128]{3,2,1,0:T(8,128)(2,1)S(1)}, bf16[2,2,192,128]{3,2,1,0:T(8,128)(2,1)S(1)}, u32[]{:S(2)}, u32[]{:S(2)}) collective-permute-start(bf16[2,2,192,128]{3,2,1,0:T(8,128)(2,1)S(1)} %get-tuple-element.31), channel_id=1, source_target_pairs={{0,3},{1,2},{2,1},{3,0},{4,7},{5,6},{6,5},{7,4},{8,11},{9,10},{10,... | collective-permute-start | bytes 589832 | tf_op jit(solution)/shard_map/ppermute | solution.py:42
  35.7 1.6 %collective-permute-start.10 = (bf16[2,192,128]{2,1,0:T(8,128)(2,1)S(1)}, bf16[2,192,128]{2,1,0:T(8,128)(2,1)S(1)}, u32[]{:S(2)}, u32[]{:S(2)}) collective-permute-start(bf16[2,192,128]{2,1,0:T(8,128)(2,1)S(1)} %shard_map.96), channel_id=1, source_target_pairs={{0,4},{4,0},{8,12},{12,8},{16,20},{20,16},{24,28},{28,24},{1,5},{5... | collective-permute-start | bytes 294920 | tf_op jit(solution)/shard_map/ppermute | solution.py:37
  37.3 1.4 %shard_map.95 = (f32[5,192,128]{2,1,0:T(8,128)S(1)}, f32[5,192,128]{2,1,0:T(8,128)S(1)}) custom-call(f32[8,128]{1,0:T(8,128)S(1)} %stack.7.flag_ref, bf16[2,4,192,128]{3,2,1,0:T(8,128)(2,1)S(1)} %get-tuple-element.29.prior_ref, f32[1,128]{1,0:T(1,128)S(1)} %bitcast.19, bf16[3,3,384,128]{3,2,1,0:T(8,128)(2,1)S(1)} %bitcast.12, ...), custom_call_target="tpu_custom_call" | custom-call | flops 566231040 | bytes 3248640 | tf_op jit(solution)/shard_map/pallas_call | solution.py:302
  38.7 1.8 %collective-permute-done.10.odd_ref = bf16[2,192,128]{2,1,0:T(8,128)(2,1)S(1)} collective-permute-done((bf16[2,192,128]{2,1,0:T(8,128)(2,1)S(1)}, bf16[2,192,128]{2,1,0:T(8,128)(2,1)S(1)}, u32[]{:S(2)}, u32[]{:S(2)}) %collective-permute-start.10) | collective-permute-done | bytes 98336 | tf_op jit(solution)/shard_map/ppermute | solution.py:37
  40.5 0.2 collective-permute-done.7.cross_ref
  40.7 2.3 %shard_map.97 = bf16[2,2,96,256]{3,2,1,0:T(8,128)(2,1)} custom-call(f32[8,128]{1,0:T(8,128)S(1)} %stack.7.flag_ref, bf16[2,4,192,128]{3,2,1,0:T(8,128)(2,1)S(1)} %get-tuple-element.29.prior_ref, bf16[2,2,192,128]{3,2,1,0:T(8,128)(2,1)S(1)} %collective-permute-done.6.pair_ref, bf16[2,2,192,128]{3,2,1,0:T(8,128)(2,1)S(1)} %collective-permute-done.7.cross_ref, ...), custom_call_target="tpu_custom_call" | custom-call | flops 622854144 | bytes 5117952 | tf_op jit(solution)/shard_map/pallas_call | solution.py:302
  (30 shorter events, 0.1 us)
Async XLA Ops:
  1.4 1.1 %copy-start.5 = (bf16[4,4,192,128]{3,2,1,0:T(8,128)(2,1)S(1)}, bf16[4,4,192,128]{3,2,1,0:T(8,128)(2,1)}, u32[]{:S(2)}) copy-start(bf16[4,4,192,128]{3,2,1,0:T(8,128)(2,1)} %video_ref.3) | copy-start | bytes 2359300
  2.6 14.7 %copy-start = (bf16[3,3,3,128,128]{4,3,2,1,0:T(8,128)(2,1)S(1)}, bf16[3,3,3,128,128]{4,3,2,1,0:T(8,128)(2,1)}, u32[]{:S(2)}) copy-start(bf16[3,3,3,128,128]{4,3,2,1,0:T(8,128)(2,1)} %param.13) | copy-start | bytes 2654212
  2.6 14.7 %copy-start.1 = (bf16[3,3,3,128,256]{4,3,2,1,0:T(8,128)(2,1)S(1)}, bf16[3,3,3,128,256]{4,3,2,1,0:T(8,128)(2,1)}, u32[]{:S(2)}) copy-start(bf16[3,3,3,128,256]{4,3,2,1,0:T(8,128)(2,1)} %param.16) | copy-start | bytes 5308420
  2.6 14.7 %copy-start.2 = (f32[128]{0:T(128)S(1)}, f32[128]{0:T(128)}, u32[]{:S(2)}) copy-start(f32[128]{0:T(128)} %param.12) | copy-start | bytes 1540
  2.6 14.7 %copy-start.3 = (f32[256]{0:T(256)S(1)}, f32[256]{0:T(256)}, u32[]{:S(2)}) copy-start(f32[256]{0:T(256)} %param.17) | copy-start | bytes 3076
  2.6 14.7 %copy-start.4 = (f32[128]{0:T(128)S(1)}, f32[128]{0:T(128)}, u32[]{:S(2)}) copy-start(f32[128]{0:T(128)} %param.15) | copy-start | bytes 1540
  2.6 14.7 %copy-start.6 = (bf16[4,4,192,128]{3,2,1,0:T(8,128)(2,1)S(1)}, bf16[4,4,192,128]{3,2,1,0:T(8,128)(2,1)}, u32[]{:S(2)}) copy-start(bf16[4,4,192,128]{3,2,1,0:T(8,128)(2,1)} %video_ref.3) | copy-start | bytes 2359300
  2.6 14.7 %copy-start.7 = (f32[128]{0:T(128)S(1)}, f32[128]{0:T(128)}, u32[]{:S(2)}) copy-start(f32[128]{0:T(128)} %param.14) | copy-start | bytes 1540
  2.8 14.2 %collective-permute-start = (bf16[8,192,128]{2,1,0:T(8,128)(2,1)S(1)}, bf16[8,192,128]{2,1,0:T(8,128)(2,1)S(1)}, u32[]{:S(2)}, u32[]{:S(2)}) collective-permute-start(bf16[8,192,128]{2,1,0:T(8,128)(2,1)S(1)} %bitcast.16), channel_id=1, source_target_pairs={{0,8},{4,12},{8,16},{12,20},{16,24},{20,28},{24,0},{28,4},{1,9},{5... | collective-permute-start | bytes 1179656 | tf_op jit(solution)/shard_map/ppermute | solution.py:20
  5.8 3.6 %collective-permute-start.2 = (f32[8,128]{1,0:T(8,128)S(1)}, f32[8,128]{1,0:T(8,128)S(1)}, u32[]{:S(2)}, u32[]{:S(2)}) collective-permute-start(f32[8,128]{1,0:T(8,128)S(1)} %broadcast_in_dim.15), channel_id=1, source_target_pairs={{0,4},{4,0},{8,12},{12,8},{16,20},{20,16},{24,28},{28,24},{1,5},{5... | collective-permute-start | bytes 12296 | tf_op jit(solution)/shard_map/ppermute | solution.py:37
  7.3 9.7 %collective-permute-start.3 = (bf16[4,2,192,128]{3,2,1,0:T(8,128)(2,1)S(1)}, bf16[4,2,192,128]{3,2,1,0:T(8,128)(2,1)S(1)}, u32[]{:S(2)}, u32[]{:S(2)}) collective-permute-start(bf16[4,2,192,128]{3,2,1,0:T(8,128)(2,1)S(1)} %get-tuple-element.22), channel_id=1, source_target_pairs={{0,1},{1,0},{2,3},{3,2},{4,5},{5,4},{6,7},{7,6},{8,9},{9,8},{10,11... | collective-permute-start | bytes 1179656 | tf_op jit(solution)/shard_map/ppermute | solution.py:37
  9.5 7.8 %collective-permute-start.4 = (bf16[4,2,192,128]{3,2,1,0:T(8,128)(2,1)S(1)}, bf16[4,2,192,128]{3,2,1,0:T(8,128)(2,1)S(1)}, u32[]{:S(2)}, u32[]{:S(2)}) collective-permute-start(bf16[4,2,192,128]{3,2,1,0:T(8,128)(2,1)S(1)} %get-tuple-element.24), channel_id=1, source_target_pairs={{0,4},{1,2},{2,1},{3,7},{4,0},{5,6},{6,5},{7,3},{8,12},{9,10},{10,... | collective-permute-start | bytes 1179656 | tf_op jit(solution)/shard_map/ppermute | solution.py:55
  17.0 5.2 %collective-permute-start.1 = (bf16[8,192,128]{2,1,0:T(8,128)(2,1)S(1)}, bf16[8,192,128]{2,1,0:T(8,128)(2,1)S(1)}, u32[]{:S(2)}, u32[]{:S(2)}) collective-permute-start(bf16[8,192,128]{2,1,0:T(8,128)(2,1)S(1)} %collective-permute-done.near_ref.two_ref), channel_id=1, source_target_pairs={{0,1},{1,0},{2,3},{3,2},{4,5},{5,4},{6,7},{7,6},{8,16},{9,17},{10,... | collective-permute-start | bytes 1179656 | tf_op jit(solution)/shard_map/ppermute | solution.py:33
  22.3 11.4 %collective-permute-start.5 = (bf16[8,192,128]{2,1,0:T(8,128)(2,1)S(1)}, bf16[8,192,128]{2,1,0:T(8,128)(2,1)S(1)}, u32[]{:S(2)}, u32[]{:S(2)}) collective-permute-start(bf16[8,192,128]{2,1,0:T(8,128)(2,1)S(1)} %shard_map.93), channel_id=1, source_target_pairs={{0,4},{4,0},{8,12},{12,8},{16,20},{20,16},{24,28},{28,24},{1,5},{5... | collective-permute-start | bytes 1179656 | tf_op jit(solution)/shard_map/ppermute | solution.py:37
  23.9 9.1 %collective-permute-start.8 = (bf16[2,192,128]{2,1,0:T(8,128)(2,1)S(1)}, bf16[2,192,128]{2,1,0:T(8,128)(2,1)S(1)}, u32[]{:S(2)}, u32[]{:S(2)}) collective-permute-start(bf16[2,192,128]{2,1,0:T(8,128)(2,1)S(1)} %get-tuple-element.27.own_ref), channel_id=1, source_target_pairs={{0,8},{4,12},{8,16},{12,20},{16,24},{20,28},{24,0},{28,4},{1,9},{5... | collective-permute-start | bytes 294920 | tf_op jit(solution)/shard_map/ppermute | solution.py:20
  33.0 2.6 %collective-permute-start.9 = (bf16[2,192,128]{2,1,0:T(8,128)(2,1)S(1)}, bf16[2,192,128]{2,1,0:T(8,128)(2,1)S(1)}, u32[]{:S(2)}, u32[]{:S(2)}) collective-permute-start(bf16[2,192,128]{2,1,0:T(8,128)(2,1)S(1)} %collective-permute-done.8.near_ref.two_ref), channel_id=1, source_target_pairs={{0,1},{1,0},{2,3},{3,2},{4,5},{5,4},{6,7},{7,6},{8,16},{9,17},{10,... | collective-permute-start | bytes 294920 | tf_op jit(solution)/shard_map/ppermute | solution.py:33
  33.9 6.6 %collective-permute-start.6 = (bf16[2,2,192,128]{3,2,1,0:T(8,128)(2,1)S(1)}, bf16[2,2,192,128]{3,2,1,0:T(8,128)(2,1)S(1)}, u32[]{:S(2)}, u32[]{:S(2)}) collective-permute-start(bf16[2,2,192,128]{3,2,1,0:T(8,128)(2,1)S(1)} %get-tuple-element.30), channel_id=1, source_target_pairs={{0,1},{1,0},{2,3},{3,2},{4,5},{5,4},{6,7},{7,6},{8,9},{9,8},{10,11... | collective-permute-start | bytes 589832 | tf_op jit(solution)/shard_map/ppermute | solution.py:37
  34.0 6.7 %collective-permute-start.7 = (bf16[2,2,192,128]{3,2,1,0:T(8,128)(2,1)S(1)}, bf16[2,2,192,128]{3,2,1,0:T(8,128)(2,1)S(1)}, u32[]{:S(2)}, u32[]{:S(2)}) collective-permute-start(bf16[2,2,192,128]{3,2,1,0:T(8,128)(2,1)S(1)} %get-tuple-element.31), channel_id=1, source_target_pairs={{0,3},{1,2},{2,1},{3,0},{4,7},{5,6},{6,5},{7,4},{8,11},{9,10},{10,... | collective-permute-start | bytes 589832 | tf_op jit(solution)/shard_map/ppermute | solution.py:42
  35.7 4.8 %collective-permute-start.10 = (bf16[2,192,128]{2,1,0:T(8,128)(2,1)S(1)}, bf16[2,192,128]{2,1,0:T(8,128)(2,1)S(1)}, u32[]{:S(2)}, u32[]{:S(2)}) collective-permute-start(bf16[2,192,128]{2,1,0:T(8,128)(2,1)S(1)} %shard_map.96), channel_id=1, source_target_pairs={{0,4},{4,0},{8,12},{12,8},{16,20},{20,16},{24,28},{28,24},{1,5},{5... | collective-permute-start | bytes 294920 | tf_op jit(solution)/shard_map/ppermute | solution.py:37

commit v4 on v3

--- a/solution.py
+++ b/solution.py
@@ -10,6 +10,7 @@
 ABOVE = 2
 EVEN, TOP, FULL, DISTANCE, BOTTOM, EVEN_GROUP = range(6)
 PACK = 30_000_000_000
+WHILE_SWAPPED = 4_000_000_000
 VMEM = pltpu.VMEM
 F32 = jnp.float32
 BF16 = jnp.bfloat16
@@ -37,11 +38,21 @@
     return lax.ppermute(value, axis, [(place, place ^ 1) for place in range(lax.axis_size(axis))])
 
 
-def crossed_within(value):
-    rows = lax.axis_size("row")
-    return lax.ppermute(
-        value, "row", [(row, (((row + 1) ^ 1) - 1) % rows) for row in range(rows)]
-    )
+def crossed_late(value):
+    groups, rows = lax.axis_size("group"), lax.axis_size("row")
+    planes = groups // 2
+    pairs = []
+    for group in range(groups):
+        plane = group // 2
+        for row in range(rows):
+            if 0 < row < rows - 1:
+                target = (group, ((row + 1) ^ 1) - 1)
+            elif 0 < plane < planes - 1 and planes % 2 == 0:
+                target = (2 * (((plane + 1) ^ 1) - 1) + group % 2, row)
+            else:
+                target = (group, rows - 1 - row)
+            pairs.append((group * rows + row, target[0] * rows + target[1]))
+    return lax.ppermute(value, ("group", "row"), pairs)
 
 
 def crossed(value):
@@ -91,10 +102,10 @@
     return jnp.dot(window, weight.reshape(3 * depth, weight.shape[2]), preferred_element_type=F32)
 
 
-def fill_second(values, gain, first_row, stage_ref, strided_ref, slot):
-    rows, half = strided_ref.shape[1], strided_ref.shape[2]
+def fill_second(values, gain, first_row, stage_ref, strided_ref, slot, rows):
+    half = strided_ref.shape[2]
     width, channels = 2 * half, stage_ref.shape[2]
-    for row in range(rows):
+    for row in rows:
         ready = pixel_silu(values(row), gain).astype(BF16).astype(F32)
         if row == 0:
             ready = jnp.where(first_row, 0.0, ready)
@@ -106,13 +117,17 @@
         )
 
 
-def conv2_frame(strided_ref, slot, weight_ref, step):
-    total = None
-    for tap in range(3):
-        window = jnp.concatenate([strided_ref[slot, tap], strided_ref[slot, tap + 2]], axis=0)
-        part = jnp.dot(window, weight_ref[step, tap], preferred_element_type=F32)
-        total = part if total is None else total + part
-    return total
+def conv2_frame(weight_ref, *parts):
+    windows, weights = [], []
+    for strided_ref, slot, step in parts:
+        for tap in range(3):
+            windows.append(
+                jnp.concatenate([strided_ref[slot, tap], strided_ref[slot, tap + 2]], axis=0)
+            )
+            weights.append(weight_ref[step, tap])
+    return jnp.dot(
+        jnp.concatenate(windows, axis=-1), jnp.concatenate(weights, axis=0), preferred_element_type=F32
+    )
 
 
 def row_reader(flag_ref, video_ref, frame, pair_ref, cross_ref):
@@ -151,47 +166,58 @@
     return jnp.concatenate([weight_ref[step] for step in steps], axis=-1)
 
 
-def own_kernel(
+def send_kernel(
     flag_ref, video_ref, pair_ref, cross_ref, gain1_ref, weight1_ref, bias1_ref,
-    gain2_ref, weight2_ref, bias2_ref, tail_ref, first_ref, next_ref, late_ref,
-    window_ref, stage_ref, strided_ref, total_ref,
+    gain2_ref, weight2_ref, tail_ref, strided_out_ref, window_ref, stage_ref, total_ref,
 ):
     first_row = holds(flag_ref, TOP)
     channels = video_ref.shape[3]
     readers = [row_reader(flag_ref, video_ref, f, pair_ref, cross_ref) for f in range(4)]
-    for frame in range(4):
+    for slot, frame in enumerate((1, 2, 3)):
+        fill_hidden(readers[frame], gain1_ref[...], window_ref, slot, range(7))
+    total_ref[...] = sum(
+        conv1_rows(window_ref, step, 5, weight1_ref[step]) for step in range(3)
+    ).reshape(total_ref.shape)
+    fill_second(
+        lambda row: total_ref[row] + readers[3](row + 1) + bias1_ref[...],
+        gain2_ref[...], first_row, stage_ref, strided_out_ref, 0, range(5),
+    )
+    tail = conv2_frame(weight2_ref, (strided_out_ref, 0, 0)).astype(BF16)
+    half = strided_out_ref.shape[2]
+    for row in range(tail_ref.shape[0]):
+        for part in range(2):
+            tail_ref[row, part * half : (part + 1) * half] = tail[
+                row * half : (row + 1) * half, part * channels : (part + 1) * channels
+            ]
+
+
+def own_kernel(
+    flag_ref, video_ref, pair_ref, cross_ref, gain1_ref, weight1_ref, bias1_ref,
+    gain2_ref, weight2_ref, bias2_ref, strided3_ref, first_ref, next_ref, late_ref,
+    window_ref, stage_ref, strided_ref, total_ref,
+):
+    first_row = holds(flag_ref, TOP)
+    channels = video_ref.shape[3]
+    readers = [row_reader(flag_ref, video_ref, f, pair_ref, cross_ref) for f in range(4)]
+    for frame in range(3):
         fill_hidden(readers[frame], gain1_ref[...], window_ref, frame, range(7))
-    zero = conv1_rows(window_ref, 0, 5, beside(weight1_ref, 0, 1))
-    one = conv1_rows(window_ref, 1, 5, beside(weight1_ref, 1, 2))
-    two = conv1_rows(window_ref, 2, 5, beside(weight1_ref, 2, 1))
-    next_ref[...] = (zero[:, channels:] + one[:, channels:]).reshape(next_ref.shape)
-    total_ref[0] = (zero[:, :channels] + one[:, :channels] + two[:, :channels]).reshape(next_ref.shape)
-    total_ref[1] = (
-        two[:, channels:]
-        + conv1_rows(window_ref, 1, 5, weight1_ref[0])
-        + conv1_rows(window_ref, 3, 5, weight1_ref[2])
+    both = conv1_rows(window_ref, 0, 5, beside(weight1_ref, 0, 1))
+    both += conv1_rows(window_ref, 1, 5, beside(weight1_ref, 1, 2))
+    next_ref[...] = both[:, channels:].reshape(next_ref.shape)
+    total_ref[...] = (
+        both[:, :channels] + conv1_rows(window_ref, 2, 5, weight1_ref[2])
     ).reshape(next_ref.shape)
     first_ref[...] = conv1_rows(window_ref, 0, 5, weight1_ref[2]).reshape(first_ref.shape)
     for row in range(5):
         next_ref[row] += readers[1](row + 1) + bias1_ref[...]
         first_ref[row] += readers[0](row + 1) + bias1_ref[...]
-    for slot in range(2):
-        fill_second(
-            lambda row: total_ref[slot, row] + readers[2 + slot](row + 1) + bias1_ref[...],
-            gain2_ref[...], first_row, stage_ref, strided_ref, slot,
-        )
+    fill_second(
+        lambda row: total_ref[row] + readers[2](row + 1) + bias1_ref[...],
+        gain2_ref[...], first_row, stage_ref, strided_ref, 0, range(5),
+    )
     late_ref[...] = (
-        conv2_frame(strided_ref, 0, weight2_ref, 1)
-        + conv2_frame(strided_ref, 1, weight2_ref, 2)
-        + bias2_ref[...]
-    )
-    tail = conv2_frame(strided_ref, 1, weight2_ref, 0).astype(BF16)
-    half = strided_ref.shape[2]
-    for row in range(tail_ref.shape[0]):
-        for part in range(2):
-            tail_ref[row, part * half : (part + 1) * half] = tail[
-                row * half : (row + 1) * half, part * channels : (part + 1) * channels
-            ]
+        conv2_frame(weight2_ref, (strided_ref, 0, 1), (strided3_ref, 0, 2)) + bias2_ref[...]
+    )
 
 
 def chosen(distance, two, four, odd):
@@ -222,8 +248,8 @@
 
 
 def inner_kernel(
-    flag_ref, prior_ref, gain1_ref, weight1_ref, first_ref, next_ref, first_out_ref, next_out_ref,
-    window_ref,
+    flag_ref, prior_ref, gain1_ref, weight1_ref, gain2_ref, first_ref, next_ref,
+    first_out_ref, next_out_ref, strided_out_ref, window_ref, stage_ref,
 ):
     del flag_ref
     rows, width, channels = prior_ref.shape[1:]
@@ -250,11 +276,24 @@
         first_out_ref[low : low + count] += (
             both[:, channels:] + part(0, weight1_ref[0, tap])
         ).reshape(shape)
+    for slot, total_ref in enumerate((next_out_ref, first_out_ref)):
+        fill_second(
+            lambda row: total_ref[row],
+            gain2_ref[...], None, stage_ref, strided_out_ref, slot, range(ABOVE, rows),
+        )
+
+
+def side_by_side(window_ref, frame, taps, weight):
+    return jnp.dot(
+        jnp.concatenate([window_ref[frame, slot] for slot, _ in taps], axis=-1),
+        jnp.concatenate([weight[tap] for _, tap in taps], axis=0),
+        preferred_element_type=F32,
+    )
 
 
 def last_kernel(
     flag_ref, prior_ref, pair_ref, cross_ref, gain1_ref, weight1_ref, gain2_ref,
-    weight2_ref, bias2_ref, first_ref, next_ref, late_ref, two_ref, four_ref, odd_ref, out_ref,
+    weight2_ref, bias2_ref, first_ref, next_ref, late_ref, inner_ref, two_ref, four_ref, odd_ref, out_ref,
     window_ref, stage_ref, strided_ref, total_ref,
 ):
     first_row, keep, distance = holds(flag_ref, TOP), holds(flag_ref, FULL), flag_ref[DISTANCE : DISTANCE + 1]
@@ -265,29 +304,26 @@
         fill_hidden(
             lambda slot: reader(outer[slot]), gain1_ref[...], window_ref, frame, range(len(outer))
         )
-    total_ref[0] = next_ref[...]
-    total_ref[1] = first_ref[...]
-    for slot, place in enumerate(outer):
-        for tap in range(3):
-            target = place - tap
-            if 0 <= target <= rows:
-                both = jnp.dot(
-                    window_ref[1, slot], beside(weight1_ref.at[:, tap], 0, 1), preferred_element_type=F32
-                )
-                total_ref[0, target] += both[:, :channels]
-                total_ref[1, target] += both[:, channels:] + jnp.dot(
-                    window_ref[0, slot], weight1_ref[0, tap], preferred_element_type=F32
-                )
+    for target in (0, 1, rows):
+        taps = [(slot, place - target) for slot, place in enumerate(outer) if 0 <= place - target < 3]
+        total_ref[0, target] = next_ref[target]
+        total_ref[1, target] = first_ref[target]
+        both = side_by_side(window_ref, 1, taps, beside(weight1_ref, 0, 1))
+        total_ref[0, target] += both[:, :channels]
+        total_ref[1, target] += both[:, channels:] + side_by_side(
+            window_ref, 0, taps, weight1_ref[0]
+        )
     for slot in range(2):
+        strided_ref[slot, ABOVE:rows] = inner_ref[slot, ABOVE:rows]
         fill_second(
             lambda row: total_ref[slot, row],
-            gain2_ref[...], first_row, stage_ref, strided_ref, slot,
+            gain2_ref[...], first_row, stage_ref, strided_ref, slot, (0, 1, rows),
         )
     shape = out_ref.shape[1:]
     half = strided_ref.shape[2]
-    late = late_ref[...] + conv2_frame(strided_ref, 0, weight2_ref, 0)
+    late = late_ref[...] + conv2_frame(weight2_ref, (strided_ref, 0, 0))
     out_ref[1] = jnp.where(jnp.concatenate([keep, keep], axis=-1), late, 0.0).astype(BF16).reshape(shape)
-    early = conv2_frame(strided_ref, 0, weight2_ref, 2) + conv2_frame(strided_ref, 1, weight2_ref, 1)
+    early = conv2_frame(weight2_ref, (strided_ref, 0, 2), (strided_ref, 1, 1))
     for row in range(shape[0]):
         tail = chosen(
             distance, two_ref[row].astype(F32), four_ref[row].astype(F32), odd_ref[row].astype(F32)
@@ -359,38 +395,45 @@
     pair = swapped(pair, "row")
     far = relayed(near)
     pair, cross = after(near, pair, cross)
-    own_e, first, following, late = call(
-        own_kernel,
-        [flags, video_frames, pair, cross, gain1, weight1, bias1, gain2, weight2, bias2],
-        [
-            like((rows // 2, width, channels)), like(total, F32), like(total, F32),
-            like((rows // 2 * half, wide), F32),
-        ],
-        [window(4, rows + 3), stage, strided, VMEM((2,) + total, F32)],
-        flops=9 * one_tap + 3 * one_code,
+    own_e, strided3 = call(
+        send_kernel,
+        [flags, video_frames, pair, cross, gain1, weight1, bias1, gain2, weight2],
+        [like((rows // 2, width, channels)), like((1, rows + 1, half, 3 * channels))],
+        [window(3, rows + 3), stage, VMEM(total, F32)],
+        flops=3 * one_tap + one_code,
     )
     chosen_own = for_partner(own, near, after(own_e, far)[0])
     odd = swapped(chosen_own, "group")
     near_e = rotated(own_e, "group", 2)
     far_e = relayed(near_e)
+    first, following, late = call(
+        own_kernel,
+        [
+            flags, video_frames, pair, cross, gain1, weight1, bias1, gain2, weight2, bias2,
+            after(near_e, strided3)[0],
+        ],
+        [like(total, F32), like(total, F32), like((rows // 2 * half, wide), F32)],
+        [window(3, rows + 3), stage, strided, VMEM(total, F32)],
+        flops=WHILE_SWAPPED,
+    )
     odd_e = swapped(for_partner(own_e, near_e, far_e), "group")
     edge = like((2, ABOVE, width, channels))
     prior, prior_pair, prior_cross = call(
-        prior_kernel, [flags, near, far, odd], [pair_of, edge, edge], []
-    )
-    prior_cross = crossed_within(prior_cross)
+        prior_kernel, [flags, near, far, after(first, odd)[0]], [pair_of, edge, edge], []
+    )
+    prior_cross = crossed_late(prior_cross)
     prior_pair = swapped(prior_pair, "row")
-    first, following = call(
+    first, following, inner = call(
         inner_kernel,
-        [flags, prior, gain1, weight1, first, following],
-        [like(total, F32), like(total, F32)],
-        [window(2, rows)],
+        [flags, prior, gain1, weight1, gain2, first, following],
+        [like(total, F32), like(total, F32), like((2, rows + 1, half, 3 * channels))],
+        [window(2, rows), stage],
         flops=2 * one_tap,
     )
     return call(
         last_kernel,
         [flags, prior, prior_pair, prior_cross, gain1, weight1, gain2, weight2, bias2, first,
-         following, late, near_e, far_e, odd_e],
+         following, late, inner, near_e, far_e, odd_e],
         [like((frames // 2, rows // 2, half, wide))],
         [window(2, 3), stage, strided, VMEM((2,) + total, F32)],
         flops=one_tap + 3 * one_code,

time: 43.8 us -> 43.1 us (0.984); the launches traced: 43 us -> 42.8 us
  starting transfers between devices: 16.3 us -> 12.6 us
  Pallas kernels: 9.15 us -> 11.1 us
  waiting for transfers between devices: 14.8 us -> 16.4 us
    ppermute x2, starting transfers between devices: 8.47 us -> 4.71 us  [rotated(): lax.ppermute(value, axis, [(source, (source + steps) % count) for source...]
    pallas_call x7 -> x8, Pallas kernels: 9.15 us -> 11.1 us  [call(): pl.pallas_call(kernel, out_shape=outs, in_specs=[pl.BlockSpec(memory_spac...]
    ppermute x2, waiting for transfers between devices: 9.76 us -> 11.5 us  [rotated(): lax.ppermute(value, axis, [(source, (source + steps) % count) for source...]
    ppermute x5, starting transfers between devices: 4.68 us -> 5.17 us  [swapped(): lax.ppermute(value, axis, [(place, place ^ 1) for place in range(lax.axis...]
    ppermute x5, waiting for transfers between devices: 4.64 us -> 4.17 us  [swapped(): lax.ppermute(value, axis, [(place, place ^ 1) for place in range(lax.axis...]
  transfers between devices with their start and end apart: 11 -> 11, of which waited for: 7 -> 6; matrix products, arithmetic and copies ran while one was open for 0% -> 0% of each run, Pallas kernels for 15% -> 21%
where the time goes in v4:
time: 43.1 us; the launch traced here: 42.8 us
  waiting for transfers between devices  16.4 us (38%)
  starting transfers between devices  12.6 us (29%)
  Pallas kernels  11.1 us (26%)
  between operations  1.49 us (3%)
  local copies, waits for them, and re-layouts  1.21 us (3%)
    ppermute x2, waiting for transfers between devices, rotated(): lax.ppermute(value, axis, [(source, (source + steps) % count) for source...  11.5 us
    pallas_call x8, Pallas kernels, call(): pl.pallas_call(kernel, out_shape=outs, in_specs=[pl.BlockSpec(memory_spac...  11.1 us
    ppermute x5, starting transfers between devices, swapped(): lax.ppermute(value, axis, [(place, place ^ 1) for place in range(lax.axis...  5.17 us
    ppermute x2, starting transfers between devices, rotated(): lax.ppermute(value, axis, [(source, (source + steps) % count) for source...  4.71 us
    ppermute x5, waiting for transfers between devices, swapped(): lax.ppermute(value, axis, [(place, place ^ 1) for place in range(lax.axis...  4.17 us
    ppermute x1, starting transfers between devices, crossed(): return lax.ppermute(value, ('group', 'row'), pairs)  1.49 us
    ppermute x1, starting transfers between devices, crossed_late(): return lax.ppermute(value, ('group', 'row'), pairs)  1.2 us
    unnamed x16, local copies, waits for them, and re-layouts  1.16 us
  transfers between devices with their start and end apart: 11, of which 6 were waited for; matrix products, arithmetic and copies ran while one was open for 0% of the time, Pallas kernels for 21%

profile of v4, /device:TPU:0, one launch (start us, length us, event | category | flops | bytes accessed | tf_op | source)
XLA Modules:
  0.0 42.8 jit_solution(9414360382747641825)
XLA Ops:
  1.4 1.1 %copy-done.2 = bf16[4,4,192,128]{3,2,1,0:T(8,128)(2,1)S(1)} copy-done((bf16[4,4,192,128]{3,2,1,0:T(8,128)(2,1)S(1)}, bf16[4,4,192,128]{3,2,1,0:T(8,128)(2,1)}, u32[]{:S(2)}) %copy-start.2) | copy-done | bytes 786456
  2.6 0.2 shard_map.91
  2.7 3.1 %collective-permute-start = (bf16[8,192,128]{2,1,0:T(8,128)(2,1)S(1)}, bf16[8,192,128]{2,1,0:T(8,128)(2,1)S(1)}, u32[]{:S(2)}, u32[]{:S(2)}) collective-permute-start(bf16[8,192,128]{2,1,0:T(8,128)(2,1)S(1)} %bitcast.18), channel_id=1, source_target_pairs={{0,8},{4,12},{8,16},{12,20},{16,24},{20,28},{24,0},{28,4},{1,9},{5... | collective-permute-start | bytes 1179656 | tf_op jit(solution)/shard_map/ppermute | solution.py:21
  5.8 1.5 %collective-permute-start.3 = (f32[8,128]{1,0:T(8,128)S(1)}, f32[8,128]{1,0:T(8,128)S(1)}, u32[]{:S(2)}, u32[]{:S(2)}) collective-permute-start(f32[8,128]{1,0:T(8,128)S(1)} %broadcast_in_dim.15), channel_id=1, source_target_pairs={{0,4},{4,0},{8,12},{12,8},{16,20},{20,16},{24,28},{28,24},{1,5},{5... | collective-permute-start | bytes 12296 | tf_op jit(solution)/shard_map/ppermute | solution.py:38
  7.3 2.1 %collective-permute-done.3.wanted_ref = f32[8,128]{1,0:T(8,128)S(1)} collective-permute-done((f32[8,128]{1,0:T(8,128)S(1)}, f32[8,128]{1,0:T(8,128)S(1)}, u32[]{:S(2)}, u32[]{:S(2)}) %collective-permute-start.3) | collective-permute-done | bytes 4128 | tf_op jit(solution)/shard_map/ppermute | solution.py:38
  9.4 1.5 %collective-permute-start.4 = (bf16[4,2,192,128]{3,2,1,0:T(8,128)(2,1)S(1)}, bf16[4,2,192,128]{3,2,1,0:T(8,128)(2,1)S(1)}, u32[]{:S(2)}, u32[]{:S(2)}) collective-permute-start(bf16[4,2,192,128]{3,2,1,0:T(8,128)(2,1)S(1)} %get-tuple-element.28), channel_id=1, source_target_pairs={{0,4},{1,2},{2,1},{3,7},{4,0},{5,6},{6,5},{7,3},{8,12},{9,10},{10,... | collective-permute-start | bytes 1179656 | tf_op jit(solution)/shard_map/ppermute | solution.py:66
  10.9 6.0 %collective-permute-done.near_ref.two_ref = bf16[8,192,128]{2,1,0:T(8,128)(2,1)S(1)} collective-permute-done((bf16[8,192,128]{2,1,0:T(8,128)(2,1)S(1)}, bf16[8,192,128]{2,1,0:T(8,128)(2,1)S(1)}, u32[]{:S(2)}, u32[]{:S(2)}) %collective-permute-start) | collective-permute-done | bytes 393248 | tf_op jit(solution)/shard_map/ppermute | solution.py:21
  17.0 0.2 collective-permute-done.4.cross_ref
  17.2 0.0 copy-start.3
  17.3 0.0 copy-start.6
  17.3 3.0 %shard_map.92 = (bf16[2,192,128]{2,1,0:T(8,128)(2,1)S(1)}, bf16[1,5,96,384]{3,2,1,0:T(8,128)(2,1)S(1)}) custom-call(f32[8,128]{1,0:T(8,128)S(1)} %stack.7.flag_ref, bf16[4,4,192,128]{3,2,1,0:T(8,128)(2,1)S(1)} %copy-done.2, bf16[4,2,192,128]{3,2,1,0:T(8,128)(2,1)S(1)} %collective-permute-done.2.pair_ref, ...), custom_call_target="tpu_custom_call" | custom-call | flops 962592768 | bytes 4699648 | tf_op jit(solution)/shard_map/pallas_call | solution.py:338
  20.2 1.6 %collective-permute-start.5 = (bf16[2,192,128]{2,1,0:T(8,128)(2,1)S(1)}, bf16[2,192,128]{2,1,0:T(8,128)(2,1)S(1)}, u32[]{:S(2)}, u32[]{:S(2)}) collective-permute-start(bf16[2,192,128]{2,1,0:T(8,128)(2,1)S(1)} %get-tuple-element.31.own_ref), channel_id=1, source_target_pairs={{0,8},{4,12},{8,16},{12,20},{16,24},{20,28},{24,0},{28,4},{1,9},{5... | collective-permute-start | bytes 294920 | tf_op jit(solution)/shard_map/ppermute | solution.py:21
  21.9 0.2 shard_map.94
  22.0 1.6 %collective-permute-start.6 = (bf16[8,192,128]{2,1,0:T(8,128)(2,1)S(1)}, bf16[8,192,128]{2,1,0:T(8,128)(2,1)S(1)}, u32[]{:S(2)}, u32[]{:S(2)}) collective-permute-start(bf16[8,192,128]{2,1,0:T(8,128)(2,1)S(1)} %shard_map.94), channel_id=1, source_target_pairs={{0,4},{4,0},{8,12},{12,8},{16,20},{20,16},{24,28},{28,24},{1,5},{5... | collective-permute-start | bytes 1179656 | tf_op jit(solution)/shard_map/ppermute | solution.py:38
  23.6 5.5 %collective-permute-done.5.near_ref.two_ref = bf16[2,192,128]{2,1,0:T(8,128)(2,1)S(1)} collective-permute-done((bf16[2,192,128]{2,1,0:T(8,128)(2,1)S(1)}, bf16[2,192,128]{2,1,0:T(8,128)(2,1)S(1)}, u32[]{:S(2)}, u32[]{:S(2)}) %collective-permute-start.5) | collective-permute-done | bytes 98336 | tf_op jit(solution)/shard_map/ppermute | solution.py:21
  29.1 3.9 %shard_map.93 = (f32[5,192,128]{2,1,0:T(8,128)S(1)}, f32[5,192,128]{2,1,0:T(8,128)S(1)}, f32[192,256]{1,0:T(8,128)S(1)}) custom-call(f32[8,128]{1,0:T(8,128)S(1)} %stack.7.flag_ref, bf16[4,4,192,128]{3,2,1,0:T(8,128)(2,1)S(1)} %copy-done.3, bf16[4,2,192,128]{3,2,1,0:T(8,128)(2,1)S(1)} %collective-permute-done.2.pair_ref, ...), custom_call_target="tpu_custom_call" | custom-call | flops 4000000000 | bytes 5782016 | tf_op jit(solution)/shard_map/pallas_call | solution.py:338
  33.0 0.2 shard_map.95
  33.3 0.6 %collective-permute-start.7 = (bf16[2,2,192,128]{3,2,1,0:T(8,128)(2,1)S(1)}, bf16[2,2,192,128]{3,2,1,0:T(8,128)(2,1)S(1)}, u32[]{:S(2)}, u32[]{:S(2)}) collective-permute-start(bf16[2,2,192,128]{3,2,1,0:T(8,128)(2,1)S(1)} %get-tuple-element.38), channel_id=1, source_target_pairs={{0,1},{1,0},{2,3},{3,2},{4,5},{5,4},{6,7},{7,6},{8,9},{9,8},{10,11... | collective-permute-start | bytes 589832 | tf_op jit(solution)/shard_map/ppermute | solution.py:38
  33.8 1.2 %collective-permute-start.8 = (bf16[2,2,192,128]{3,2,1,0:T(8,128)(2,1)S(1)}, bf16[2,2,192,128]{3,2,1,0:T(8,128)(2,1)S(1)}, u32[]{:S(2)}, u32[]{:S(2)}) collective-permute-start(bf16[2,2,192,128]{3,2,1,0:T(8,128)(2,1)S(1)} %get-tuple-element.39), channel_id=1, source_target_pairs={{0,3},{1,2},{2,1},{3,0},{4,7},{5,6},{6,5},{7,4},{8,16},{9,10},{10,... | collective-permute-start | bytes 589832 | tf_op jit(solution)/shard_map/ppermute | solution.py:55
  35.1 1.6 %collective-permute-start.10 = (bf16[2,192,128]{2,1,0:T(8,128)(2,1)S(1)}, bf16[2,192,128]{2,1,0:T(8,128)(2,1)S(1)}, u32[]{:S(2)}, u32[]{:S(2)}) collective-permute-start(bf16[2,192,128]{2,1,0:T(8,128)(2,1)S(1)} %shard_map.97), channel_id=1, source_target_pairs={{0,4},{4,0},{8,12},{12,8},{16,20},{20,16},{24,28},{28,24},{1,5},{5... | collective-permute-start | bytes 294920 | tf_op jit(solution)/shard_map/ppermute | solution.py:38
  36.6 1.6 %shard_map.96 = (f32[5,192,128]{2,1,0:T(8,128)S(1)}, f32[5,192,128]{2,1,0:T(8,128)S(1)}, bf16[2,5,96,384]{3,2,1,0:T(8,128)(2,1)S(1)}) custom-call(f32[8,128]{1,0:T(8,128)S(1)} %stack.7.flag_ref, bf16[2,4,192,128]{3,2,1,0:T(8,128)(2,1)S(1)} %get-tuple-element.37.prior_ref, f32[1,128]{1,0:T(1,128)S(1)} %bitcast.22, bf16[3,3,384,128]{3,2,1,0:T(8,128)(2,1)S(1)} %bitcast.13, ...), custom_call_target="tpu_custom_call" | custom-call | flops 566231040 | bytes 3986432 | tf_op jit(solution)/shard_map/pallas_call | solution.py:338
  38.2 2.0 %collective-permute-done.10.odd_ref = bf16[2,192,128]{2,1,0:T(8,128)(2,1)S(1)} collective-permute-done((bf16[2,192,128]{2,1,0:T(8,128)(2,1)S(1)}, bf16[2,192,128]{2,1,0:T(8,128)(2,1)S(1)}, u32[]{:S(2)}, u32[]{:S(2)}) %collective-permute-start.10) | collective-permute-done | bytes 98336 | tf_op jit(solution)/shard_map/ppermute | solution.py:38
  40.3 0.5 %collective-permute-done.8.cross_ref = bf16[2,2,192,128]{3,2,1,0:T(8,128)(2,1)S(1)} collective-permute-done((bf16[2,2,192,128]{3,2,1,0:T(8,128)(2,1)S(1)}, bf16[2,2,192,128]{3,2,1,0:T(8,128)(2,1)S(1)}, u32[]{:S(2)}, u32[]{:S(2)}) %collective-permute-start.8) | collective-permute-done | bytes 196640 | tf_op jit(solution)/shard_map/ppermute | solution.py:55
  40.8 2.0 %shard_map.98 = bf16[2,2,96,256]{3,2,1,0:T(8,128)(2,1)} custom-call(f32[8,128]{1,0:T(8,128)S(1)} %stack.7.flag_ref, bf16[2,4,192,128]{3,2,1,0:T(8,128)(2,1)S(1)} %get-tuple-element.37.prior_ref, bf16[2,2,192,128]{3,2,1,0:T(8,128)(2,1)S(1)} %collective-permute-done.7.pair_ref, bf16[2,2,192,128]{3,2,1,0:T(8,128)(2,1)S(1)} %collective-permute-done.8.cross_ref, ...), custom_call_target="tpu_custom_call" | custom-call | flops 622854144 | bytes 5855232 | tf_op jit(solution)/shard_map/pallas_call | solution.py:338
  (31 shorter events, 0.1 us)
Async XLA Ops:
  1.4 1.1 %copy-start.2 = (bf16[4,4,192,128]{3,2,1,0:T(8,128)(2,1)S(1)}, bf16[4,4,192,128]{3,2,1,0:T(8,128)(2,1)}, u32[]{:S(2)}) copy-start(bf16[4,4,192,128]{3,2,1,0:T(8,128)(2,1)} %video_ref.5) | copy-start | bytes 2359300
  2.6 14.7 %copy-start = (bf16[3,3,3,128,128]{4,3,2,1,0:T(8,128)(2,1)S(1)}, bf16[3,3,3,128,128]{4,3,2,1,0:T(8,128)(2,1)}, u32[]{:S(2)}) copy-start(bf16[3,3,3,128,128]{4,3,2,1,0:T(8,128)(2,1)} %param.13) | copy-start | bytes 2654212
  2.6 14.7 %copy-start.1 = (bf16[3,3,3,128,256]{4,3,2,1,0:T(8,128)(2,1)S(1)}, bf16[3,3,3,128,256]{4,3,2,1,0:T(8,128)(2,1)}, u32[]{:S(2)}) copy-start(bf16[3,3,3,128,256]{4,3,2,1,0:T(8,128)(2,1)} %param.16) | copy-start | bytes 5308420
  2.6 14.7 %copy-start.4 = (f32[128]{0:T(128)S(1)}, f32[128]{0:T(128)}, u32[]{:S(2)}) copy-start(f32[128]{0:T(128)} %param.12) | copy-start | bytes 1540
  2.6 14.7 %copy-start.5 = (f32[128]{0:T(128)S(1)}, f32[128]{0:T(128)}, u32[]{:S(2)}) copy-start(f32[128]{0:T(128)} %param.15) | copy-start | bytes 1540
  2.6 14.7 %copy-start.7 = (f32[128]{0:T(128)S(1)}, f32[128]{0:T(128)}, u32[]{:S(2)}) copy-start(f32[128]{0:T(128)} %param.14) | copy-start | bytes 1540
  2.7 14.2 %collective-permute-start = (bf16[8,192,128]{2,1,0:T(8,128)(2,1)S(1)}, bf16[8,192,128]{2,1,0:T(8,128)(2,1)S(1)}, u32[]{:S(2)}, u32[]{:S(2)}) collective-permute-start(bf16[8,192,128]{2,1,0:T(8,128)(2,1)S(1)} %bitcast.18), channel_id=1, source_target_pairs={{0,8},{4,12},{8,16},{12,20},{16,24},{20,28},{24,0},{28,4},{1,9},{5... | collective-permute-start | bytes 1179656 | tf_op jit(solution)/shard_map/ppermute | solution.py:21
  5.8 3.6 %collective-permute-start.3 = (f32[8,128]{1,0:T(8,128)S(1)}, f32[8,128]{1,0:T(8,128)S(1)}, u32[]{:S(2)}, u32[]{:S(2)}) collective-permute-start(f32[8,128]{1,0:T(8,128)S(1)} %broadcast_in_dim.15), channel_id=1, source_target_pairs={{0,4},{4,0},{8,12},{12,8},{16,20},{20,16},{24,28},{28,24},{1,5},{5... | collective-permute-start | bytes 12296 | tf_op jit(solution)/shard_map/ppermute | solution.py:38
  7.3 9.7 %collective-permute-start.2 = (bf16[4,2,192,128]{3,2,1,0:T(8,128)(2,1)S(1)}, bf16[4,2,192,128]{3,2,1,0:T(8,128)(2,1)S(1)}, u32[]{:S(2)}, u32[]{:S(2)}) collective-permute-start(bf16[4,2,192,128]{3,2,1,0:T(8,128)(2,1)S(1)} %get-tuple-element.26), channel_id=1, source_target_pairs={{0,1},{1,0},{2,3},{3,2},{4,5},{5,4},{6,7},{7,6},{8,9},{9,8},{10,11... | collective-permute-start | bytes 1179656 | tf_op jit(solution)/shard_map/ppermute | solution.py:38
  9.4 7.8 %collective-permute-start.4 = (bf16[4,2,192,128]{3,2,1,0:T(8,128)(2,1)S(1)}, bf16[4,2,192,128]{3,2,1,0:T(8,128)(2,1)S(1)}, u32[]{:S(2)}, u32[]{:S(2)}) collective-permute-start(bf16[4,2,192,128]{3,2,1,0:T(8,128)(2,1)S(1)} %get-tuple-element.28), channel_id=1, source_target_pairs={{0,4},{1,2},{2,1},{3,7},{4,0},{5,6},{6,5},{7,3},{8,12},{9,10},{10,... | collective-permute-start | bytes 1179656 | tf_op jit(solution)/shard_map/ppermute | solution.py:66
  17.0 4.9 %collective-permute-start.1 = (bf16[8,192,128]{2,1,0:T(8,128)(2,1)S(1)}, bf16[8,192,128]{2,1,0:T(8,128)(2,1)S(1)}, u32[]{:S(2)}, u32[]{:S(2)}) collective-permute-start(bf16[8,192,128]{2,1,0:T(8,128)(2,1)S(1)} %collective-permute-done.near_ref.two_ref), channel_id=1, source_target_pairs={{0,1},{1,0},{2,3},{3,2},{4,5},{5,4},{6,7},{7,6},{8,16},{9,17},{10,... | collective-permute-start | bytes 1179656 | tf_op jit(solution)/shard_map/ppermute | solution.py:34
  17.2 11.9 %copy-start.3 = (bf16[4,4,192,128]{3,2,1,0:T(8,128)(2,1)S(1)}, bf16[4,4,192,128]{3,2,1,0:T(8,128)(2,1)}, u32[]{:S(2)}) copy-start(bf16[4,4,192,128]{3,2,1,0:T(8,128)(2,1)} %video_ref.5) | copy-start | bytes 2359300
  17.3 11.9 %copy-start.6 = (f32[256]{0:T(256)S(1)}, f32[256]{0:T(256)}, u32[]{:S(2)}) copy-start(f32[256]{0:T(256)} %param.17) | copy-start | bytes 3076
  20.2 8.9 %collective-permute-start.5 = (bf16[2,192,128]{2,1,0:T(8,128)(2,1)S(1)}, bf16[2,192,128]{2,1,0:T(8,128)(2,1)S(1)}, u32[]{:S(2)}, u32[]{:S(2)}) collective-permute-start(bf16[2,192,128]{2,1,0:T(8,128)(2,1)S(1)} %get-tuple-element.31.own_ref), channel_id=1, source_target_pairs={{0,8},{4,12},{8,16},{12,20},{16,24},{20,28},{24,0},{28,4},{1,9},{5... | collective-permute-start | bytes 294920 | tf_op jit(solution)/shard_map/ppermute | solution.py:21
  22.0 11.0 %collective-permute-start.6 = (bf16[8,192,128]{2,1,0:T(8,128)(2,1)S(1)}, bf16[8,192,128]{2,1,0:T(8,128)(2,1)S(1)}, u32[]{:S(2)}, u32[]{:S(2)}) collective-permute-start(bf16[8,192,128]{2,1,0:T(8,128)(2,1)S(1)} %shard_map.94), channel_id=1, source_target_pairs={{0,4},{4,0},{8,12},{12,8},{16,20},{20,16},{24,28},{28,24},{1,5},{5... | collective-permute-start | bytes 1179656 | tf_op jit(solution)/shard_map/ppermute | solution.py:38
  29.1 5.9 %collective-permute-start.9 = (bf16[2,192,128]{2,1,0:T(8,128)(2,1)S(1)}, bf16[2,192,128]{2,1,0:T(8,128)(2,1)S(1)}, u32[]{:S(2)}, u32[]{:S(2)}) collective-permute-start(bf16[2,192,128]{2,1,0:T(8,128)(2,1)S(1)} %collective-permute-done.5.near_ref.two_ref), channel_id=1, source_target_pairs={{0,1},{1,0},{2,3},{3,2},{4,5},{5,4},{6,7},{7,6},{8,16},{9,17},{10,... | collective-permute-start | bytes 294920 | tf_op jit(solution)/shard_map/ppermute | solution.py:34
  33.3 7.0 %collective-permute-start.7 = (bf16[2,2,192,128]{3,2,1,0:T(8,128)(2,1)S(1)}, bf16[2,2,192,128]{3,2,1,0:T(8,128)(2,1)S(1)}, u32[]{:S(2)}, u32[]{:S(2)}) collective-permute-start(bf16[2,2,192,128]{3,2,1,0:T(8,128)(2,1)S(1)} %get-tuple-element.38), channel_id=1, source_target_pairs={{0,1},{1,0},{2,3},{3,2},{4,5},{5,4},{6,7},{7,6},{8,9},{9,8},{10,11... | collective-permute-start | bytes 589832 | tf_op jit(solution)/shard_map/ppermute | solution.py:38
  33.8 6.9 %collective-permute-start.8 = (bf16[2,2,192,128]{3,2,1,0:T(8,128)(2,1)S(1)}, bf16[2,2,192,128]{3,2,1,0:T(8,128)(2,1)S(1)}, u32[]{:S(2)}, u32[]{:S(2)}) collective-permute-start(bf16[2,2,192,128]{3,2,1,0:T(8,128)(2,1)S(1)} %get-tuple-element.39), channel_id=1, source_target_pairs={{0,3},{1,2},{2,1},{3,0},{4,7},{5,6},{6,5},{7,4},{8,16},{9,10},{10,... | collective-permute-start | bytes 589832 | tf_op jit(solution)/shard_map/ppermute | solution.py:55
  35.1 5.2 %collective-permute-start.10 = (bf16[2,192,128]{2,1,0:T(8,128)(2,1)S(1)}, bf16[2,192,128]{2,1,0:T(8,128)(2,1)S(1)}, u32[]{:S(2)}, u32[]{:S(2)}) collective-permute-start(bf16[2,192,128]{2,1,0:T(8,128)(2,1)S(1)} %shard_map.97), channel_id=1, source_target_pairs={{0,4},{4,0},{8,12},{12,8},{16,20},{20,16},{24,28},{28,24},{1,5},{5... | collective-permute-start | bytes 294920 | tf_op jit(solution)/shard_map/ppermute | solution.py:38

commit v5 on v4

--- a/solution.py
+++ b/solution.py
@@ -11,6 +11,7 @@
 EVEN, TOP, FULL, DISTANCE, BOTTOM, EVEN_GROUP = range(6)
 PACK = 30_000_000_000
 WHILE_SWAPPED = 4_000_000_000
+WHILE_SENT = 2_000_000_000
 VMEM = pltpu.VMEM
 F32 = jnp.float32
 BF16 = jnp.bfloat16
@@ -191,33 +192,42 @@
             ]
 
 
+def second_kernel(
+    flag_ref, video_ref, pair_ref, cross_ref, gain1_ref, weight1_ref, bias1_ref,
+    gain2_ref, weight2_ref, bias2_ref, strided3_ref, later_ref, late_ref, window_ref,
+    stage_ref, strided_ref, total_ref,
+):
+    first_row = holds(flag_ref, TOP)
+    readers = [row_reader(flag_ref, video_ref, f, pair_ref, cross_ref) for f in range(4)]
+    fill_hidden(readers[0], gain1_ref[...], window_ref, 0, range(7))
+    total_ref[...] = (
+        conv1_rows(window_ref, 0, 5, weight1_ref[0])
+        + conv1_rows(later_ref, 0, 5, weight1_ref[1])
+        + conv1_rows(later_ref, 1, 5, weight1_ref[2])
+    ).reshape(total_ref.shape)
+    fill_second(
+        lambda row: total_ref[row] + readers[2](row + 1) + bias1_ref[...],
+        gain2_ref[...], first_row, stage_ref, strided_ref, 0, range(5),
+    )
+    late_ref[...] = (
+        conv2_frame(weight2_ref, (strided_ref, 0, 1), (strided3_ref, 0, 2)) + bias2_ref[...]
+    )
+
+
 def own_kernel(
-    flag_ref, video_ref, pair_ref, cross_ref, gain1_ref, weight1_ref, bias1_ref,
-    gain2_ref, weight2_ref, bias2_ref, strided3_ref, first_ref, next_ref, late_ref,
-    window_ref, stage_ref, strided_ref, total_ref,
-):
-    first_row = holds(flag_ref, TOP)
+    flag_ref, video_ref, pair_ref, cross_ref, weight1_ref, bias1_ref, window_ref, later_ref,
+    first_ref, next_ref,
+):
     channels = video_ref.shape[3]
-    readers = [row_reader(flag_ref, video_ref, f, pair_ref, cross_ref) for f in range(4)]
-    for frame in range(3):
-        fill_hidden(readers[frame], gain1_ref[...], window_ref, frame, range(7))
-    both = conv1_rows(window_ref, 0, 5, beside(weight1_ref, 0, 1))
-    both += conv1_rows(window_ref, 1, 5, beside(weight1_ref, 1, 2))
-    next_ref[...] = both[:, channels:].reshape(next_ref.shape)
-    total_ref[...] = (
-        both[:, :channels] + conv1_rows(window_ref, 2, 5, weight1_ref[2])
+    readers = [row_reader(flag_ref, video_ref, f, pair_ref, cross_ref) for f in range(2)]
+    both = conv1_rows(window_ref, 0, 5, beside(weight1_ref, 2, 1))
+    first_ref[...] = both[:, :channels].reshape(first_ref.shape)
+    next_ref[...] = (
+        both[:, channels:] + conv1_rows(later_ref, 0, 5, weight1_ref[2])
     ).reshape(next_ref.shape)
-    first_ref[...] = conv1_rows(window_ref, 0, 5, weight1_ref[2]).reshape(first_ref.shape)
     for row in range(5):
         next_ref[row] += readers[1](row + 1) + bias1_ref[...]
         first_ref[row] += readers[0](row + 1) + bias1_ref[...]
-    fill_second(
-        lambda row: total_ref[row] + readers[2](row + 1) + bias1_ref[...],
-        gain2_ref[...], first_row, stage_ref, strided_ref, 0, range(5),
-    )
-    late_ref[...] = (
-        conv2_frame(weight2_ref, (strided_ref, 0, 1), (strided3_ref, 0, 2)) + bias2_ref[...]
-    )
 
 
 def chosen(distance, two, four, odd):
@@ -226,24 +236,25 @@
     return jnp.where(distance == 0, 0.0, value)
 
 
-def partner_kernel(flag_ref, wanted_ref, own_ref, near_ref, far_ref, out_ref):
+def partner_kernel(start, flag_ref, wanted_ref, own_ref, near_ref, far_ref, out_ref):
     first, one = holds(flag_ref, EVEN_GROUP), wanted_ref[0:1] == 1
     for row in range(out_ref.shape[0]):
-        own, near, far = own_ref[row], near_ref[row], far_ref[row]
+        own, near, far = own_ref[start + row], near_ref[start + row], far_ref[row]
         out_ref[row] = jnp.where(
             first, jnp.where(one, own, near), jnp.where(one, near, far)
         )
 
 
 def prior_kernel(
-    flag_ref, two_ref, four_ref, odd_ref, prior_ref, pair_ref, cross_ref,
+    flag_ref, two_ref, four0_ref, four1_ref, odd0_ref, odd1_ref, prior_ref, pair_ref, cross_ref,
 ):
     even, distance = holds(flag_ref, EVEN), flag_ref[DISTANCE : DISTANCE + 1]
     frames, rows = prior_ref.shape[:2]
-    for frame in range(frames):
+    for frame, (four_ref, odd_ref) in enumerate(((four0_ref, odd0_ref), (four1_ref, odd1_ref))):
         for row in range(rows):
-            at = frame * rows + row
-            prior_ref[frame, row] = chosen(distance, two_ref[at], four_ref[at], odd_ref[at])
+            prior_ref[frame, row] = chosen(
+                distance, two_ref[frame * rows + row], four_ref[row], odd_ref[row]
+            )
     split_edges(even, prior_ref, frames, rows, pair_ref, cross_ref)
 
 
@@ -369,8 +380,9 @@
     def window(count, high):
         return VMEM((count, high, width, 3 * channels), BF16)
 
-    def for_partner(own, near, far):
-        return call(partner_kernel, [flags, wanted, own, near, far], [like(own.shape)], [])[0]
+    def for_partner(own, near, far, start=0):
+        kernel = functools.partial(partner_kernel, start)
+        return call(kernel, [flags, wanted, own, near, far], [like(far.shape)], [])[0]
 
     weight1 = conv1_weight.reshape(3, 3, 3 * channels, channels)
     weight2 = conv2_weight.reshape(3, 3, 3 * channels, wide)
@@ -393,33 +405,51 @@
     own = own.reshape(flat)
     near = rotated(own, "group", 2)
     pair = swapped(pair, "row")
-    far = relayed(near)
+    fars = [
+        relayed(lax.slice_in_dim(near, frame * rows, (frame + 1) * rows, axis=0))
+        for frame in range(2)
+    ]
     pair, cross = after(near, pair, cross)
-    own_e, strided3 = call(
+    def windows(count):
+        return like((count, rows + 3, width, 3 * channels))
+
+    own_e, strided3, later = call(
         send_kernel,
         [flags, video_frames, pair, cross, gain1, weight1, bias1, gain2, weight2],
-        [like((rows // 2, width, channels)), like((1, rows + 1, half, 3 * channels))],
-        [window(3, rows + 3), stage, VMEM(total, F32)],
+        [
+            like((rows // 2, width, channels)), like((1, rows + 1, half, 3 * channels)),
+            windows(3),
+        ],
+        [stage, VMEM(total, F32)],
         flops=3 * one_tap + one_code,
     )
-    chosen_own = for_partner(own, near, after(own_e, far)[0])
-    odd = swapped(chosen_own, "group")
+    chosen_first = for_partner(own, near, after(own_e, fars[0])[0])
+    chosen_own = for_partner(own, near, after(chosen_first, fars[1])[0], rows)
+    odds = [swapped(chosen_first, "group"), swapped(chosen_own, "group")]
     near_e = rotated(own_e, "group", 2)
-    far_e = relayed(near_e)
-    first, following, late = call(
-        own_kernel,
+    late, start = call(
+        second_kernel,
         [
             flags, video_frames, pair, cross, gain1, weight1, bias1, gain2, weight2, bias2,
-            after(near_e, strided3)[0],
+            after(chosen_own, strided3)[0], later,
         ],
-        [like(total, F32), like(total, F32), like((rows // 2 * half, wide), F32)],
-        [window(3, rows + 3), stage, strided, VMEM(total, F32)],
+        [like((rows // 2 * half, wide), F32), windows(1)],
+        [stage, strided, VMEM(total, F32)],
         flops=WHILE_SWAPPED,
+    )
+    near_e = after(late, near_e)[0]
+    far_e = relayed(near_e)
+    first, following = call(
+        own_kernel,
+        [flags, video_frames, pair, cross, weight1, bias1, after(near_e, start)[0], later],
+        [like(total, F32), like(total, F32)],
+        [],
+        flops=WHILE_SENT,
     )
     odd_e = swapped(for_partner(own_e, near_e, far_e), "group")
     edge = like((2, ABOVE, width, channels))
     prior, prior_pair, prior_cross = call(
-        prior_kernel, [flags, near, far, after(first, odd)[0]], [pair_of, edge, edge], []
+        prior_kernel, [flags, near] + fars + [odds[0], after(first, odds[1])[0]], [pair_of, edge, edge], []
     )
     prior_cross = crossed_late(prior_cross)
     prior_pair = swapped(prior_pair, "row")

time: 43.1 us -> 42.6 us (0.988)
  the two profiles are of different devices: /device:TPU:0 before, /device:TPU:8 now
where the time goes in v5:
time: 42.6 us; the launch traced here: 42.5 us
  starting transfers between devices  14.5 us (34%)
  waiting for transfers between devices  13.8 us (32%)
  Pallas kernels  11.4 us (27%)
  between operations  1.53 us (4%)
  local copies, waits for them, and re-layouts  1.23 us (3%)
    pallas_call x10, Pallas kernels, call(): pl.pallas_call(kernel, out_shape=outs, in_specs=[pl.BlockSpec(memory_spac...  11.4 us
    ppermute x6, starting transfers between devices, swapped(): lax.ppermute(value, axis, [(place, place ^ 1) for place in range(lax.axis...  5.28 us
    ppermute x3, waiting for transfers between devices, relayed(): return lax.ppermute(value, ('group', 'row'), pairs)  5.04 us
    ppermute x6, waiting for transfers between devices, swapped(): lax.ppermute(value, axis, [(place, place ^ 1) for place in range(lax.axis...  4.61 us
    ppermute x2, waiting for transfers between devices, rotated(): lax.ppermute(value, axis, [(source, (source + steps) % count) for source...  4.18 us
    ppermute x3, starting transfers between devices, relayed(): return lax.ppermute(value, ('group', 'row'), pairs)  3.94 us
    ppermute x2, starting transfers between devices, rotated(): lax.ppermute(value, axis, [(source, (source + steps) % count) for source...  2.11 us
    ppermute x1, starting transfers between devices, crossed_late(): return lax.ppermute(value, ('group', 'row'), pairs)  1.64 us
  transfers between devices with their start and end apart: 13, of which 6 were waited for; matrix products, arithmetic and copies ran while one was open for 0% of the time, Pallas kernels for 22%

profile of v5, /device:TPU:8, one launch (start us, length us, event | category | flops | bytes accessed | tf_op | source)
XLA Modules:
  0.0 42.5 jit_solution(16815750342886448316)
XLA Ops:
  1.4 1.1 %copy-done.2 = bf16[4,4,192,128]{3,2,1,0:T(8,128)(2,1)S(1)} copy-done((bf16[4,4,192,128]{3,2,1,0:T(8,128)(2,1)S(1)}, bf16[4,4,192,128]{3,2,1,0:T(8,128)(2,1)}, u32[]{:S(2)}) %copy-start.2) | copy-done | bytes 786456
  2.7 1.6 %collective-permute-start = (bf16[8,192,128]{2,1,0:T(8,128)(2,1)S(1)}, bf16[8,192,128]{2,1,0:T(8,128)(2,1)S(1)}, u32[]{:S(2)}, u32[]{:S(2)}) collective-permute-start(bf16[8,192,128]{2,1,0:T(8,128)(2,1)S(1)} %bitcast.19), channel_id=1, source_target_pairs={{0,8},{4,12},{8,16},{12,20},{16,24},{20,28},{24,0},{28,4},{1,9},{5... | collective-permute-start | bytes 1179656 | tf_op jit(solution)/shard_map/ppermute | solution.py:22
  4.4 1.5 %collective-permute-start.3 = (f32[8,128]{1,0:T(8,128)S(1)}, f32[8,128]{1,0:T(8,128)S(1)}, u32[]{:S(2)}, u32[]{:S(2)}) collective-permute-start(f32[8,128]{1,0:T(8,128)S(1)} %broadcast_in_dim.15), channel_id=1, source_target_pairs={{0,4},{4,0},{8,12},{12,8},{16,20},{20,16},{24,28},{28,24},{1,5},{5... | collective-permute-start | bytes 12296 | tf_op jit(solution)/shard_map/ppermute | solution.py:39
  5.9 2.1 %collective-permute-done.3.wanted_ref = f32[8,128]{1,0:T(8,128)S(1)} collective-permute-done((f32[8,128]{1,0:T(8,128)S(1)}, f32[8,128]{1,0:T(8,128)S(1)}, u32[]{:S(2)}, u32[]{:S(2)}) %collective-permute-start.3) | collective-permute-done | bytes 4128 | tf_op jit(solution)/shard_map/ppermute | solution.py:39
  8.0 1.5 %collective-permute-start.5 = (bf16[4,2,192,128]{3,2,1,0:T(8,128)(2,1)S(1)}, bf16[4,2,192,128]{3,2,1,0:T(8,128)(2,1)S(1)}, u32[]{:S(2)}, u32[]{:S(2)}) collective-permute-start(bf16[4,2,192,128]{3,2,1,0:T(8,128)(2,1)S(1)} %get-tuple-element.33), channel_id=1, source_target_pairs={{0,4},{1,2},{2,1},{3,7},{4,0},{5,6},{6,5},{7,3},{8,12},{9,10},{10,... | collective-permute-start | bytes 1179656 | tf_op jit(solution)/shard_map/ppermute | solution.py:67
  9.5 4.2 %collective-permute-done.near_ref.two_ref = bf16[8,192,128]{2,1,0:T(8,128)(2,1)S(1)} collective-permute-done((bf16[8,192,128]{2,1,0:T(8,128)(2,1)S(1)}, bf16[8,192,128]{2,1,0:T(8,128)(2,1)S(1)}, u32[]{:S(2)}, u32[]{:S(2)}) %collective-permute-start) | collective-permute-done | bytes 393248 | tf_op jit(solution)/shard_map/ppermute | solution.py:22
  13.7 1.6 %collective-permute-start.1 = (bf16[4,192,128]{2,1,0:T(8,128)(2,1)S(1)}, bf16[4,192,128]{2,1,0:T(8,128)(2,1)S(1)}, u32[]{:S(2)}, u32[]{:S(2)}) collective-permute-start(bf16[4,192,128]{2,1,0:T(8,128)(2,1)S(1)} %get-tuple-element.56), channel_id=1, source_target_pairs={{0,1},{1,0},{2,3},{3,2},{4,5},{5,4},{6,7},{7,6},{8,16},{9,17},{10,... | collective-permute-start | bytes 589832 | tf_op jit(solution)/shard_map/ppermute | solution.py:35
  15.3 1.6 %collective-permute-start.2 = (bf16[4,192,128]{2,1,0:T(8,128)(2,1)S(1)}, bf16[4,192,128]{2,1,0:T(8,128)(2,1)S(1)}, u32[]{:S(2)}, u32[]{:S(2)}) collective-permute-start(bf16[4,192,128]{2,1,0:T(8,128)(2,1)S(1)} %get-tuple-element.55), channel_id=1, source_target_pairs={{0,1},{1,0},{2,3},{3,2},{4,5},{5,4},{6,7},{7,6},{8,16},{9,17},{10,... | collective-permute-start | bytes 589832 | tf_op jit(solution)/shard_map/ppermute | solution.py:35
  17.0 3.0 %shard_map.92 = (bf16[2,192,128]{2,1,0:T(8,128)(2,1)S(1)}, bf16[1,5,96,384]{3,2,1,0:T(8,128)(2,1)S(1)}, bf16[3,7,192,384]{3,2,1,0:T(8,128)(2,1)S(1)}) custom-call(f32[8,128]{1,0:T(8,128)S(1)} %stack.7.flag_ref, bf16[4,4,192,128]{3,2,1,0:T(8,128)(2,1)S(1)} %copy-done.2, bf16[4,2,192,128]{3,2,1,0:T(8,128)(2,1)S(1)} %collective-permute-done.4.pair_ref, ...), custom_call_target="tpu_custom_call" | custom-call | flops 962592768 | bytes 7796224 | tf_op jit(solution)/shard_map/pallas_call | solution.py:349
  20.0 0.5 %collective-permute-start.7 = (bf16[2,192,128]{2,1,0:T(8,128)(2,1)S(1)}, bf16[2,192,128]{2,1,0:T(8,128)(2,1)S(1)}, u32[]{:S(2)}, u32[]{:S(2)}) collective-permute-start(bf16[2,192,128]{2,1,0:T(8,128)(2,1)S(1)} %get-tuple-element.36.own_ref), channel_id=1, source_target_pairs={{0,8},{4,12},{8,16},{12,20},{16,24},{20,28},{24,0},{28,4},{1,9},{5... | collective-permute-start | bytes 294920 | tf_op jit(solution)/shard_map/ppermute | solution.py:22
  20.4 2.0 %collective-permute-done.1.far_ref.four0_ref = bf16[4,192,128]{2,1,0:T(8,128)(2,1)S(1)} collective-permute-done((bf16[4,192,128]{2,1,0:T(8,128)(2,1)S(1)}, bf16[4,192,128]{2,1,0:T(8,128)(2,1)S(1)}, u32[]{:S(2)}, u32[]{:S(2)}) %collective-permute-start.1) | collective-permute-done | bytes 196640 | tf_op jit(solution)/shard_map/ppermute | solution.py:35
  22.5 1.6 %collective-permute-start.6 = (bf16[4,192,128]{2,1,0:T(8,128)(2,1)S(1)}, bf16[4,192,128]{2,1,0:T(8,128)(2,1)S(1)}, u32[]{:S(2)}, u32[]{:S(2)}) collective-permute-start(bf16[4,192,128]{2,1,0:T(8,128)(2,1)S(1)} %shard_map.93), channel_id=1, source_target_pairs={{0,4},{4,0},{8,12},{12,8},{16,20},{20,16},{24,28},{28,24},{1,5},{5... | collective-permute-start | bytes 589832 | tf_op jit(solution)/shard_map/ppermute | solution.py:39
  24.1 1.6 %collective-permute-done.2.far_ref.four1_ref = bf16[4,192,128]{2,1,0:T(8,128)(2,1)S(1)} collective-permute-done((bf16[4,192,128]{2,1,0:T(8,128)(2,1)S(1)}, bf16[4,192,128]{2,1,0:T(8,128)(2,1)S(1)}, u32[]{:S(2)}, u32[]{:S(2)}) %collective-permute-start.2) | collective-permute-done | bytes 196640 | tf_op jit(solution)/shard_map/ppermute | solution.py:35
  25.7 1.6 %collective-permute-start.8 = (bf16[4,192,128]{2,1,0:T(8,128)(2,1)S(1)}, bf16[4,192,128]{2,1,0:T(8,128)(2,1)S(1)}, u32[]{:S(2)}, u32[]{:S(2)}) collective-permute-start(bf16[4,192,128]{2,1,0:T(8,128)(2,1)S(1)} %shard_map.94), channel_id=1, source_target_pairs={{0,4},{4,0},{8,12},{12,8},{16,20},{20,16},{24,28},{28,24},{1,5},{5... | collective-permute-start | bytes 589832 | tf_op jit(solution)/shard_map/ppermute | solution.py:39
  27.3 2.8 %shard_map.95 = (f32[192,256]{1,0:T(8,128)S(1)}, bf16[1,7,192,384]{3,2,1,0:T(8,128)(2,1)S(1)}) custom-call(f32[8,128]{1,0:T(8,128)S(1)} %stack.7.flag_ref, bf16[4,4,192,128]{3,2,1,0:T(8,128)(2,1)S(1)} %copy-done.3, bf16[4,2,192,128]{3,2,1,0:T(8,128)(2,1)S(1)} %collective-permute-done.4.pair_ref, ...), custom_call_target="tpu_custom_call" | custom-call | flops 4000000000 | bytes 8927744 | tf_op jit(solution)/shard_map/pallas_call | solution.py:349
  30.1 0.7 %collective-permute-start.11 = (bf16[2,192,128]{2,1,0:T(8,128)(2,1)S(1)}, bf16[2,192,128]{2,1,0:T(8,128)(2,1)S(1)}, u32[]{:S(2)}, u32[]{:S(2)}) collective-permute-start(bf16[2,192,128]{2,1,0:T(8,128)(2,1)S(1)} %collective-permute-done.7.near_ref.two_ref), channel_id=1, source_target_pairs={{0,1},{1,0},{2,3},{3,2},{4,5},{5,4},{6,7},{7,6},{8,16},{9,17},{10,... | collective-permute-start | bytes 294920 | tf_op jit(solution)/shard_map/ppermute | solution.py:35
  30.9 1.4 %shard_map.96 = (f32[5,192,128]{2,1,0:T(8,128)S(1)}, f32[5,192,128]{2,1,0:T(8,128)S(1)}) custom-call(f32[8,128]{1,0:T(8,128)S(1)} %stack.7.flag_ref, bf16[4,4,192,128]{3,2,1,0:T(8,128)(2,1)S(1)} %copy-done.3, bf16[4,2,192,128]{3,2,1,0:T(8,128)(2,1)S(1)} %collective-permute-done.4.pair_ref, bf16[4,2,192,128]{3,2,1,0:T(8,128)(2,1)S(1)} %collective-permute-done.5.cross_ref, ...), custom_call_target="tpu_custom_call" | custom-call | flops 2000000000 | bytes 7574016 | tf_op jit(solution)/shard_map/pallas_call | solution.py:349
  32.3 0.2 shard_map.97
  32.6 1.6 %collective-permute-start.10 = (bf16[2,2,192,128]{3,2,1,0:T(8,128)(2,1)S(1)}, bf16[2,2,192,128]{3,2,1,0:T(8,128)(2,1)S(1)}, u32[]{:S(2)}, u32[]{:S(2)}) collective-permute-start(bf16[2,2,192,128]{3,2,1,0:T(8,128)(2,1)S(1)} %get-tuple-element.50), channel_id=1, source_target_pairs={{0,3},{1,2},{2,1},{3,0},{4,7},{5,6},{6,5},{7,4},{8,16},{9,10},{10,... | collective-permute-start | bytes 589832 | tf_op jit(solution)/shard_map/ppermute | solution.py:56
  34.2 1.5 %collective-permute-done.11.far_ref.four_ref = bf16[2,192,128]{2,1,0:T(8,128)(2,1)S(1)} collective-permute-done((bf16[2,192,128]{2,1,0:T(8,128)(2,1)S(1)}, bf16[2,192,128]{2,1,0:T(8,128)(2,1)S(1)}, u32[]{:S(2)}, u32[]{:S(2)}) %collective-permute-start.11) | collective-permute-done | bytes 98336 | tf_op jit(solution)/shard_map/ppermute | solution.py:35
  35.7 0.6 %collective-permute-start.12 = (bf16[2,192,128]{2,1,0:T(8,128)(2,1)S(1)}, bf16[2,192,128]{2,1,0:T(8,128)(2,1)S(1)}, u32[]{:S(2)}, u32[]{:S(2)}) collective-permute-start(bf16[2,192,128]{2,1,0:T(8,128)(2,1)S(1)} %shard_map.99), channel_id=1, source_target_pairs={{0,4},{4,0},{8,12},{12,8},{16,20},{20,16},{24,28},{28,24},{1,5},{5... | collective-permute-start | bytes 294920 | tf_op jit(solution)/shard_map/ppermute | solution.py:39
  36.3 1.6 %shard_map.98 = (f32[5,192,128]{2,1,0:T(8,128)S(1)}, f32[5,192,128]{2,1,0:T(8,128)S(1)}, bf16[2,5,96,384]{3,2,1,0:T(8,128)(2,1)S(1)}) custom-call(f32[8,128]{1,0:T(8,128)S(1)} %stack.7.flag_ref, bf16[2,4,192,128]{3,2,1,0:T(8,128)(2,1)S(1)} %get-tuple-element.48.prior_ref, f32[1,128]{1,0:T(1,128)S(1)} %bitcast.24, bf16[3,3,384,128]{3,2,1,0:T(8,128)(2,1)S(1)} %bitcast.14, ...), custom_call_target="tpu_custom_call" | custom-call | flops 566231040 | bytes 3986432 | tf_op jit(solution)/shard_map/pallas_call | solution.py:349
  37.9 2.5 %collective-permute-done.12.odd_ref = bf16[2,192,128]{2,1,0:T(8,128)(2,1)S(1)} collective-permute-done((bf16[2,192,128]{2,1,0:T(8,128)(2,1)S(1)}, bf16[2,192,128]{2,1,0:T(8,128)(2,1)S(1)}, u32[]{:S(2)}, u32[]{:S(2)}) %collective-permute-start.12) | collective-permute-done | bytes 98336 | tf_op jit(solution)/shard_map/ppermute | solution.py:39
  40.4 2.0 %shard_map.100 = bf16[2,2,96,256]{3,2,1,0:T(8,128)(2,1)} custom-call(f32[8,128]{1,0:T(8,128)S(1)} %stack.7.flag_ref, bf16[2,4,192,128]{3,2,1,0:T(8,128)(2,1)S(1)} %get-tuple-element.48.prior_ref, bf16[2,2,192,128]{3,2,1,0:T(8,128)(2,1)S(1)} %collective-permute-done.9.pair_ref, bf16[2,2,192,128]{3,2,1,0:T(8,128)(2,1)S(1)} %collective-permute-done.10.cross_ref, ...), custom_call_target="tpu_custom_call" | custom-call | flops 622854144 | bytes 5855232 | tf_op jit(solution)/shard_map/pallas_call | solution.py:349
  (38 shorter events, 0.6 us)
Async XLA Ops:
  1.4 1.1 %copy-start.2 = (bf16[4,4,192,128]{3,2,1,0:T(8,128)(2,1)S(1)}, bf16[4,4,192,128]{3,2,1,0:T(8,128)(2,1)}, u32[]{:S(2)}) copy-start(bf16[4,4,192,128]{3,2,1,0:T(8,128)(2,1)} %video_ref.7) | copy-start | bytes 2359300
  2.5 14.3 %copy-start = (bf16[3,3,3,128,128]{4,3,2,1,0:T(8,128)(2,1)S(1)}, bf16[3,3,3,128,128]{4,3,2,1,0:T(8,128)(2,1)}, u32[]{:S(2)}) copy-start(bf16[3,3,3,128,128]{4,3,2,1,0:T(8,128)(2,1)} %param.13) | copy-start | bytes 2654212
  2.5 14.4 %copy-start.1 = (bf16[3,3,3,128,256]{4,3,2,1,0:T(8,128)(2,1)S(1)}, bf16[3,3,3,128,256]{4,3,2,1,0:T(8,128)(2,1)}, u32[]{:S(2)}) copy-start(bf16[3,3,3,128,256]{4,3,2,1,0:T(8,128)(2,1)} %param.16) | copy-start | bytes 5308420
  2.5 14.4 %copy-start.4 = (f32[128]{0:T(128)S(1)}, f32[128]{0:T(128)}, u32[]{:S(2)}) copy-start(f32[128]{0:T(128)} %param.12) | copy-start | bytes 1540
  2.5 14.4 %copy-start.5 = (f32[128]{0:T(128)S(1)}, f32[128]{0:T(128)}, u32[]{:S(2)}) copy-start(f32[128]{0:T(128)} %param.15) | copy-start | bytes 1540
  2.6 14.4 %copy-start.7 = (f32[128]{0:T(128)S(1)}, f32[128]{0:T(128)}, u32[]{:S(2)}) copy-start(f32[128]{0:T(128)} %param.14) | copy-start | bytes 1540
  2.7 10.9 %collective-permute-start = (bf16[8,192,128]{2,1,0:T(8,128)(2,1)S(1)}, bf16[8,192,128]{2,1,0:T(8,128)(2,1)S(1)}, u32[]{:S(2)}, u32[]{:S(2)}) collective-permute-start(bf16[8,192,128]{2,1,0:T(8,128)(2,1)S(1)} %bitcast.19), channel_id=1, source_target_pairs={{0,8},{4,12},{8,16},{12,20},{16,24},{20,28},{24,0},{28,4},{1,9},{5... | collective-permute-start | bytes 1179656 | tf_op jit(solution)/shard_map/ppermute | solution.py:22
  4.4 3.6 %collective-permute-start.3 = (f32[8,128]{1,0:T(8,128)S(1)}, f32[8,128]{1,0:T(8,128)S(1)}, u32[]{:S(2)}, u32[]{:S(2)}) collective-permute-start(f32[8,128]{1,0:T(8,128)S(1)} %broadcast_in_dim.15), channel_id=1, source_target_pairs={{0,4},{4,0},{8,12},{12,8},{16,20},{20,16},{24,28},{28,24},{1,5},{5... | collective-permute-start | bytes 12296 | tf_op jit(solution)/shard_map/ppermute | solution.py:39
  5.9 11.0 %collective-permute-start.4 = (bf16[4,2,192,128]{3,2,1,0:T(8,128)(2,1)S(1)}, bf16[4,2,192,128]{3,2,1,0:T(8,128)(2,1)S(1)}, u32[]{:S(2)}, u32[]{:S(2)}) collective-permute-start(bf16[4,2,192,128]{3,2,1,0:T(8,128)(2,1)S(1)} %get-tuple-element.31), channel_id=1, source_target_pairs={{0,1},{1,0},{2,3},{3,2},{4,5},{5,4},{6,7},{7,6},{8,9},{9,8},{10,11... | collective-permute-start | bytes 1179656 | tf_op jit(solution)/shard_map/ppermute | solution.py:39
  8.0 8.9 %collective-permute-start.5 = (bf16[4,2,192,128]{3,2,1,0:T(8,128)(2,1)S(1)}, bf16[4,2,192,128]{3,2,1,0:T(8,128)(2,1)S(1)}, u32[]{:S(2)}, u32[]{:S(2)}) collective-permute-start(bf16[4,2,192,128]{3,2,1,0:T(8,128)(2,1)S(1)} %get-tuple-element.33), channel_id=1, source_target_pairs={{0,4},{1,2},{2,1},{3,7},{4,0},{5,6},{6,5},{7,3},{8,12},{9,10},{10,... | collective-permute-start | bytes 1179656 | tf_op jit(solution)/shard_map/ppermute | solution.py:67
  13.7 8.8 %collective-permute-start.1 = (bf16[4,192,128]{2,1,0:T(8,128)(2,1)S(1)}, bf16[4,192,128]{2,1,0:T(8,128)(2,1)S(1)}, u32[]{:S(2)}, u32[]{:S(2)}) collective-permute-start(bf16[4,192,128]{2,1,0:T(8,128)(2,1)S(1)} %get-tuple-element.56), channel_id=1, source_target_pairs={{0,1},{1,0},{2,3},{3,2},{4,5},{5,4},{6,7},{7,6},{8,16},{9,17},{10,... | collective-permute-start | bytes 589832 | tf_op jit(solution)/shard_map/ppermute | solution.py:35
  15.3 10.4 %collective-permute-start.2 = (bf16[4,192,128]{2,1,0:T(8,128)(2,1)S(1)}, bf16[4,192,128]{2,1,0:T(8,128)(2,1)S(1)}, u32[]{:S(2)}, u32[]{:S(2)}) collective-permute-start(bf16[4,192,128]{2,1,0:T(8,128)(2,1)S(1)} %get-tuple-element.55), channel_id=1, source_target_pairs={{0,1},{1,0},{2,3},{3,2},{4,5},{5,4},{6,7},{7,6},{8,16},{9,17},{10,... | collective-permute-start | bytes 589832 | tf_op jit(solution)/shard_map/ppermute | solution.py:35
  16.9 10.4 %copy-start.3 = (bf16[4,4,192,128]{3,2,1,0:T(8,128)(2,1)S(1)}, bf16[4,4,192,128]{3,2,1,0:T(8,128)(2,1)}, u32[]{:S(2)}) copy-start(bf16[4,4,192,128]{3,2,1,0:T(8,128)(2,1)} %video_ref.7) | copy-start | bytes 2359300
  16.9 10.4 %copy-start.6 = (f32[256]{0:T(256)S(1)}, f32[256]{0:T(256)}, u32[]{:S(2)}) copy-start(f32[256]{0:T(256)} %param.17) | copy-start | bytes 3076
  20.0 10.2 %collective-permute-start.7 = (bf16[2,192,128]{2,1,0:T(8,128)(2,1)S(1)}, bf16[2,192,128]{2,1,0:T(8,128)(2,1)S(1)}, u32[]{:S(2)}, u32[]{:S(2)}) collective-permute-start(bf16[2,192,128]{2,1,0:T(8,128)(2,1)S(1)} %get-tuple-element.36.own_ref), channel_id=1, source_target_pairs={{0,8},{4,12},{8,16},{12,20},{16,24},{20,28},{24,0},{28,4},{1,9},{5... | collective-permute-start | bytes 294920 | tf_op jit(solution)/shard_map/ppermute | solution.py:22
  22.5 9.7 %collective-permute-start.6 = (bf16[4,192,128]{2,1,0:T(8,128)(2,1)S(1)}, bf16[4,192,128]{2,1,0:T(8,128)(2,1)S(1)}, u32[]{:S(2)}, u32[]{:S(2)}) collective-permute-start(bf16[4,192,128]{2,1,0:T(8,128)(2,1)S(1)} %shard_map.93), channel_id=1, source_target_pairs={{0,4},{4,0},{8,12},{12,8},{16,20},{20,16},{24,28},{28,24},{1,5},{5... | collective-permute-start | bytes 589832 | tf_op jit(solution)/shard_map/ppermute | solution.py:39
  25.7 6.5 %collective-permute-start.8 = (bf16[4,192,128]{2,1,0:T(8,128)(2,1)S(1)}, bf16[4,192,128]{2,1,0:T(8,128)(2,1)S(1)}, u32[]{:S(2)}, u32[]{:S(2)}) collective-permute-start(bf16[4,192,128]{2,1,0:T(8,128)(2,1)S(1)} %shard_map.94), channel_id=1, source_target_pairs={{0,4},{4,0},{8,12},{12,8},{16,20},{20,16},{24,28},{28,24},{1,5},{5... | collective-permute-start | bytes 589832 | tf_op jit(solution)/shard_map/ppermute | solution.py:39
  30.1 5.6 %collective-permute-start.11 = (bf16[2,192,128]{2,1,0:T(8,128)(2,1)S(1)}, bf16[2,192,128]{2,1,0:T(8,128)(2,1)S(1)}, u32[]{:S(2)}, u32[]{:S(2)}) collective-permute-start(bf16[2,192,128]{2,1,0:T(8,128)(2,1)S(1)} %collective-permute-done.7.near_ref.two_ref), channel_id=1, source_target_pairs={{0,1},{1,0},{2,3},{3,2},{4,5},{5,4},{6,7},{7,6},{8,16},{9,17},{10,... | collective-permute-start | bytes 294920 | tf_op jit(solution)/shard_map/ppermute | solution.py:35
  32.5 7.9 %collective-permute-start.9 = (bf16[2,2,192,128]{3,2,1,0:T(8,128)(2,1)S(1)}, bf16[2,2,192,128]{3,2,1,0:T(8,128)(2,1)S(1)}, u32[]{:S(2)}, u32[]{:S(2)}) collective-permute-start(bf16[2,2,192,128]{3,2,1,0:T(8,128)(2,1)S(1)} %get-tuple-element.49), channel_id=1, source_target_pairs={{0,1},{1,0},{2,3},{3,2},{4,5},{5,4},{6,7},{7,6},{8,9},{9,8},{10,11... | collective-permute-start | bytes 589832 | tf_op jit(solution)/shard_map/ppermute | solution.py:39
  32.6 7.9 %collective-permute-start.10 = (bf16[2,2,192,128]{3,2,1,0:T(8,128)(2,1)S(1)}, bf16[2,2,192,128]{3,2,1,0:T(8,128)(2,1)S(1)}, u32[]{:S(2)}, u32[]{:S(2)}) collective-permute-start(bf16[2,2,192,128]{3,2,1,0:T(8,128)(2,1)S(1)} %get-tuple-element.50), channel_id=1, source_target_pairs={{0,3},{1,2},{2,1},{3,0},{4,7},{5,6},{6,5},{7,4},{8,16},{9,10},{10,... | collective-permute-start | bytes 589832 | tf_op jit(solution)/shard_map/ppermute | solution.py:56
  35.7 4.7 %collective-permute-start.12 = (bf16[2,192,128]{2,1,0:T(8,128)(2,1)S(1)}, bf16[2,192,128]{2,1,0:T(8,128)(2,1)S(1)}, u32[]{:S(2)}, u32[]{:S(2)}) collective-permute-start(bf16[2,192,128]{2,1,0:T(8,128)(2,1)S(1)} %shard_map.99), channel_id=1, source_target_pairs={{0,4},{4,0},{8,12},{12,8},{16,20},{20,16},{24,28},{28,24},{1,5},{5... | collective-permute-start | bytes 294920 | tf_op jit(solution)/shard_map/ppermute | solution.py:39

commit v6 on v5

--- a/solution.py
+++ b/solution.py
@@ -10,8 +10,8 @@
 ABOVE = 2
 EVEN, TOP, FULL, DISTANCE, BOTTOM, EVEN_GROUP = range(6)
 PACK = 30_000_000_000
-WHILE_SWAPPED = 4_000_000_000
-WHILE_SENT = 2_000_000_000
+WHILE_SWAPPED = 3_000_000_000
+WHILE_SENT = 200_000_000
 VMEM = pltpu.VMEM
 F32 = jnp.float32
 BF16 = jnp.bfloat16
@@ -426,22 +426,21 @@
     chosen_first = for_partner(own, near, after(own_e, fars[0])[0])
     chosen_own = for_partner(own, near, after(chosen_first, fars[1])[0], rows)
     odds = [swapped(chosen_first, "group"), swapped(chosen_own, "group")]
-    near_e = rotated(own_e, "group", 2)
+    near_e = after(chosen_own, rotated(own_e, "group", 2))[0]
     late, start = call(
         second_kernel,
         [
             flags, video_frames, pair, cross, gain1, weight1, bias1, gain2, weight2, bias2,
-            after(chosen_own, strided3)[0], later,
+            after(near_e, strided3)[0], later,
         ],
         [like((rows // 2 * half, wide), F32), windows(1)],
         [stage, strided, VMEM(total, F32)],
         flops=WHILE_SWAPPED,
     )
-    near_e = after(late, near_e)[0]
     far_e = relayed(near_e)
     first, following = call(
         own_kernel,
-        [flags, video_frames, pair, cross, weight1, bias1, after(near_e, start)[0], later],
+        [flags, video_frames, pair, cross, weight1, bias1, start, later],
         [like(total, F32), like(total, F32)],
         [],
         flops=WHILE_SENT,
@@ -449,7 +448,7 @@
     odd_e = swapped(for_partner(own_e, near_e, far_e), "group")
     edge = like((2, ABOVE, width, channels))
     prior, prior_pair, prior_cross = call(
-        prior_kernel, [flags, near] + fars + [odds[0], after(first, odds[1])[0]], [pair_of, edge, edge], []
+        prior_kernel, [flags, near] + fars + [odds[0], after(late, odds[1])[0]], [pair_of, edge, edge], []
     )
     prior_cross = crossed_late(prior_cross)
     prior_pair = swapped(prior_pair, "row")

time: 42.6 us -> 41.8 us (0.981)
  the two profiles are of different devices: /device:TPU:8 before, /device:TPU:0 now
where the time goes in v6:
time: 41.8 us; the launch traced here: 41.6 us
  starting transfers between devices  14.4 us (34%)
  waiting for transfers between devices  13 us (31%)
  Pallas kernels  11.5 us (28%)
  between operations  1.52 us (4%)
  local copies, waits for them, and re-layouts  1.23 us (3%)
    pallas_call x10, Pallas kernels, call(): pl.pallas_call(kernel, out_shape=outs, in_specs=[pl.BlockSpec(memory_spac...  11.5 us
    ppermute x2, waiting for transfers between devices, rotated(): lax.ppermute(value, axis, [(source, (source + steps) % count) for source...  9.82 us
    ppermute x2, starting transfers between devices, rotated(): lax.ppermute(value, axis, [(source, (source + steps) % count) for source...  5.49 us
    ppermute x6, starting transfers between devices, swapped(): lax.ppermute(value, axis, [(place, place ^ 1) for place in range(lax.axis...  5.39 us
    ppermute x6, waiting for transfers between devices, swapped(): lax.ppermute(value, axis, [(place, place ^ 1) for place in range(lax.axis...  2.88 us
    ppermute x1, starting transfers between devices, crossed(): return lax.ppermute(value, ('group', 'row'), pairs)  1.49 us
    ppermute x1, starting transfers between devices, crossed_late(): return lax.ppermute(value, ('group', 'row'), pairs)  1.45 us
    unnamed x16, local copies, waits for them, and re-layouts  1.16 us
  transfers between devices with their start and end apart: 13, of which 6 were waited for; matrix products, arithmetic and copies ran while one was open for 0% of the time, Pallas kernels for 22%

profile of v6, /device:TPU:0, one launch (start us, length us, event | category | flops | bytes accessed | tf_op | source)
XLA Modules:
  0.0 41.6 jit_solution(11981675753740404661)
XLA Ops:
  1.4 1.1 %copy-done.2 = bf16[4,4,192,128]{3,2,1,0:T(8,128)(2,1)S(1)} copy-done((bf16[4,4,192,128]{3,2,1,0:T(8,128)(2,1)S(1)}, bf16[4,4,192,128]{3,2,1,0:T(8,128)(2,1)}, u32[]{:S(2)}) %copy-start.2) | copy-done | bytes 786456
  2.6 0.2 shard_map.91
  2.7 3.1 %collective-permute-start = (bf16[8,192,128]{2,1,0:T(8,128)(2,1)S(1)}, bf16[8,192,128]{2,1,0:T(8,128)(2,1)S(1)}, u32[]{:S(2)}, u32[]{:S(2)}) collective-permute-start(bf16[8,192,128]{2,1,0:T(8,128)(2,1)S(1)} %bitcast.19), channel_id=1, source_target_pairs={{0,8},{4,12},{8,16},{12,20},{16,24},{20,28},{24,0},{28,4},{1,9},{5... | collective-permute-start | bytes 1179656 | tf_op jit(solution)/shard_map/ppermute | solution.py:22
  5.8 1.5 %collective-permute-start.3 = (f32[8,128]{1,0:T(8,128)S(1)}, f32[8,128]{1,0:T(8,128)S(1)}, u32[]{:S(2)}, u32[]{:S(2)}) collective-permute-start(f32[8,128]{1,0:T(8,128)S(1)} %broadcast_in_dim.15), channel_id=1, source_target_pairs={{0,4},{4,0},{8,12},{12,8},{16,20},{20,16},{24,28},{28,24},{1,5},{5... | collective-permute-start | bytes 12296 | tf_op jit(solution)/shard_map/ppermute | solution.py:39
  7.3 2.1 %collective-permute-done.3.wanted_ref = f32[8,128]{1,0:T(8,128)S(1)} collective-permute-done((f32[8,128]{1,0:T(8,128)S(1)}, f32[8,128]{1,0:T(8,128)S(1)}, u32[]{:S(2)}, u32[]{:S(2)}) %collective-permute-start.3) | collective-permute-done | bytes 4128 | tf_op jit(solution)/shard_map/ppermute | solution.py:39
  9.4 1.5 %collective-permute-start.5 = (bf16[4,2,192,128]{3,2,1,0:T(8,128)(2,1)S(1)}, bf16[4,2,192,128]{3,2,1,0:T(8,128)(2,1)S(1)}, u32[]{:S(2)}, u32[]{:S(2)}) collective-permute-start(bf16[4,2,192,128]{3,2,1,0:T(8,128)(2,1)S(1)} %get-tuple-element.32), channel_id=1, source_target_pairs={{0,4},{1,2},{2,1},{3,7},{4,0},{5,6},{6,5},{7,3},{8,12},{9,10},{10,... | collective-permute-start | bytes 1179656 | tf_op jit(solution)/shard_map/ppermute | solution.py:67
  10.9 6.0 %collective-permute-done.near_ref.two_ref = bf16[8,192,128]{2,1,0:T(8,128)(2,1)S(1)} collective-permute-done((bf16[8,192,128]{2,1,0:T(8,128)(2,1)S(1)}, bf16[8,192,128]{2,1,0:T(8,128)(2,1)S(1)}, u32[]{:S(2)}, u32[]{:S(2)}) %collective-permute-start) | collective-permute-done | bytes 393248 | tf_op jit(solution)/shard_map/ppermute | solution.py:22
  17.1 0.5 %collective-permute-start.2 = (bf16[4,192,128]{2,1,0:T(8,128)(2,1)S(1)}, bf16[4,192,128]{2,1,0:T(8,128)(2,1)S(1)}, u32[]{:S(2)}, u32[]{:S(2)}) collective-permute-start(bf16[4,192,128]{2,1,0:T(8,128)(2,1)S(1)} %get-tuple-element.53), channel_id=1, source_target_pairs={{0,1},{1,0},{2,3},{3,2},{4,5},{5,4},{6,7},{7,6},{8,16},{9,17},{10,... | collective-permute-start | bytes 589832 | tf_op jit(solution)/shard_map/ppermute | solution.py:35
  17.6 3.0 %shard_map.92 = (bf16[2,192,128]{2,1,0:T(8,128)(2,1)S(1)}, bf16[1,5,96,384]{3,2,1,0:T(8,128)(2,1)S(1)}, bf16[3,7,192,384]{3,2,1,0:T(8,128)(2,1)S(1)}) custom-call(f32[8,128]{1,0:T(8,128)S(1)} %stack.7.flag_ref, bf16[4,4,192,128]{3,2,1,0:T(8,128)(2,1)S(1)} %copy-done.2, bf16[4,2,192,128]{3,2,1,0:T(8,128)(2,1)S(1)} %collective-permute-done.4.pair_ref, ...), custom_call_target="tpu_custom_call" | custom-call | flops 962592768 | bytes 7796224 | tf_op jit(solution)/shard_map/pallas_call | solution.py:349
  20.7 2.4 %collective-permute-start.7 = (bf16[2,192,128]{2,1,0:T(8,128)(2,1)S(1)}, bf16[2,192,128]{2,1,0:T(8,128)(2,1)S(1)}, u32[]{:S(2)}, u32[]{:S(2)}) collective-permute-start(bf16[2,192,128]{2,1,0:T(8,128)(2,1)S(1)} %get-tuple-element.35.own_ref), channel_id=1, source_target_pairs={{0,8},{4,12},{8,16},{12,20},{16,24},{20,28},{24,0},{28,4},{1,9},{5... | collective-permute-start | bytes 294920 | tf_op jit(solution)/shard_map/ppermute | solution.py:22
  23.2 1.6 %collective-permute-start.6 = (bf16[4,192,128]{2,1,0:T(8,128)(2,1)S(1)}, bf16[4,192,128]{2,1,0:T(8,128)(2,1)S(1)}, u32[]{:S(2)}, u32[]{:S(2)}) collective-permute-start(bf16[4,192,128]{2,1,0:T(8,128)(2,1)S(1)} %shard_map.93), channel_id=1, source_target_pairs={{0,4},{4,0},{8,12},{12,8},{16,20},{20,16},{24,28},{28,24},{1,5},{5... | collective-permute-start | bytes 589832 | tf_op jit(solution)/shard_map/ppermute | solution.py:39
  24.8 0.6 %collective-permute-start.8 = (bf16[4,192,128]{2,1,0:T(8,128)(2,1)S(1)}, bf16[4,192,128]{2,1,0:T(8,128)(2,1)S(1)}, u32[]{:S(2)}, u32[]{:S(2)}) collective-permute-start(bf16[4,192,128]{2,1,0:T(8,128)(2,1)S(1)} %shard_map.94), channel_id=1, source_target_pairs={{0,4},{4,0},{8,12},{12,8},{16,20},{20,16},{24,28},{28,24},{1,5},{5... | collective-permute-start | bytes 589832 | tf_op jit(solution)/shard_map/ppermute | solution.py:39
  25.4 3.8 %collective-permute-done.7.near_ref.two_ref = bf16[2,192,128]{2,1,0:T(8,128)(2,1)S(1)} collective-permute-done((bf16[2,192,128]{2,1,0:T(8,128)(2,1)S(1)}, bf16[2,192,128]{2,1,0:T(8,128)(2,1)S(1)}, u32[]{:S(2)}, u32[]{:S(2)}) %collective-permute-start.7) | collective-permute-done | bytes 98336 | tf_op jit(solution)/shard_map/ppermute | solution.py:22
  29.2 2.8 %shard_map.95 = (f32[192,256]{1,0:T(8,128)S(1)}, bf16[1,7,192,384]{3,2,1,0:T(8,128)(2,1)S(1)}) custom-call(f32[8,128]{1,0:T(8,128)S(1)} %stack.7.flag_ref, bf16[4,4,192,128]{3,2,1,0:T(8,128)(2,1)S(1)} %copy-done.3, bf16[4,2,192,128]{3,2,1,0:T(8,128)(2,1)S(1)} %collective-permute-done.4.pair_ref, ...), custom_call_target="tpu_custom_call" | custom-call | flops 3000000000 | bytes 8927744 | tf_op jit(solution)/shard_map/pallas_call | solution.py:349
  32.0 0.4 collective-permute-done.8.odd1_ref
  32.4 0.2 shard_map.96
  32.7 0.2 collective-permute-start.9
  32.8 1.5 %collective-permute-start.10 = (bf16[2,2,192,128]{3,2,1,0:T(8,128)(2,1)S(1)}, bf16[2,2,192,128]{3,2,1,0:T(8,128)(2,1)S(1)}, u32[]{:S(2)}, u32[]{:S(2)}) collective-permute-start(bf16[2,2,192,128]{3,2,1,0:T(8,128)(2,1)S(1)} %get-tuple-element.46), channel_id=1, source_target_pairs={{0,3},{1,2},{2,1},{3,0},{4,7},{5,6},{6,5},{7,4},{8,16},{9,10},{10,... | collective-permute-start | bytes 589832 | tf_op jit(solution)/shard_map/ppermute | solution.py:56
  34.3 1.6 %collective-permute-start.12 = (bf16[2,192,128]{2,1,0:T(8,128)(2,1)S(1)}, bf16[2,192,128]{2,1,0:T(8,128)(2,1)S(1)}, u32[]{:S(2)}, u32[]{:S(2)}) collective-permute-start(bf16[2,192,128]{2,1,0:T(8,128)(2,1)S(1)} %shard_map.99), channel_id=1, source_target_pairs={{0,4},{4,0},{8,12},{12,8},{16,20},{20,16},{24,28},{28,24},{1,5},{5... | collective-permute-start | bytes 294920 | tf_op jit(solution)/shard_map/ppermute | solution.py:39
  35.9 1.4 %shard_map.97 = (f32[5,192,128]{2,1,0:T(8,128)S(1)}, f32[5,192,128]{2,1,0:T(8,128)S(1)}) custom-call(f32[8,128]{1,0:T(8,128)S(1)} %stack.7.flag_ref, bf16[4,4,192,128]{3,2,1,0:T(8,128)(2,1)S(1)} %copy-done.3, bf16[4,2,192,128]{3,2,1,0:T(8,128)(2,1)S(1)} %collective-permute-done.4.pair_ref, bf16[4,2,192,128]{3,2,1,0:T(8,128)(2,1)S(1)} %collective-permute-done.5.cross_ref, ...), custom_call_target="tpu_custom_call" | custom-call | flops 200000000 | bytes 7574016 | tf_op jit(solution)/shard_map/pallas_call | solution.py:349
  37.3 1.6 %shard_map.98 = (f32[5,192,128]{2,1,0:T(8,128)S(1)}, f32[5,192,128]{2,1,0:T(8,128)S(1)}, bf16[2,5,96,384]{3,2,1,0:T(8,128)(2,1)S(1)}) custom-call(f32[8,128]{1,0:T(8,128)S(1)} %stack.7.flag_ref, bf16[2,4,192,128]{3,2,1,0:T(8,128)(2,1)S(1)} %get-tuple-element.44.prior_ref, f32[1,128]{1,0:T(1,128)S(1)} %bitcast.24, bf16[3,3,384,128]{3,2,1,0:T(8,128)(2,1)S(1)} %bitcast.14, ...), custom_call_target="tpu_custom_call" | custom-call | flops 566231040 | bytes 3986432 | tf_op jit(solution)/shard_map/pallas_call | solution.py:349
  38.9 0.4 collective-permute-done.12.odd_ref
  39.3 0.3 collective-permute-done.10.cross_ref
  39.6 2.0 %shard_map.100 = bf16[2,2,96,256]{3,2,1,0:T(8,128)(2,1)} custom-call(f32[8,128]{1,0:T(8,128)S(1)} %stack.7.flag_ref, bf16[2,4,192,128]{3,2,1,0:T(8,128)(2,1)S(1)} %get-tuple-element.44.prior_ref, bf16[2,2,192,128]{3,2,1,0:T(8,128)(2,1)S(1)} %collective-permute-done.9.pair_ref, bf16[2,2,192,128]{3,2,1,0:T(8,128)(2,1)S(1)} %collective-permute-done.10.cross_ref, ...), custom_call_target="tpu_custom_call" | custom-call | flops 622854144 | bytes 5855232 | tf_op jit(solution)/shard_map/pallas_call | solution.py:349
  (38 shorter events, 0.4 us)
Async XLA Ops:
  1.4 1.1 %copy-start.2 = (bf16[4,4,192,128]{3,2,1,0:T(8,128)(2,1)S(1)}, bf16[4,4,192,128]{3,2,1,0:T(8,128)(2,1)}, u32[]{:S(2)}) copy-start(bf16[4,4,192,128]{3,2,1,0:T(8,128)(2,1)} %video_ref.7) | copy-start | bytes 2359300
  2.6 15.0 %copy-start = (bf16[3,3,3,128,128]{4,3,2,1,0:T(8,128)(2,1)S(1)}, bf16[3,3,3,128,128]{4,3,2,1,0:T(8,128)(2,1)}, u32[]{:S(2)}) copy-start(bf16[3,3,3,128,128]{4,3,2,1,0:T(8,128)(2,1)} %param.13) | copy-start | bytes 2654212
  2.6 15.0 %copy-start.1 = (bf16[3,3,3,128,256]{4,3,2,1,0:T(8,128)(2,1)S(1)}, bf16[3,3,3,128,256]{4,3,2,1,0:T(8,128)(2,1)}, u32[]{:S(2)}) copy-start(bf16[3,3,3,128,256]{4,3,2,1,0:T(8,128)(2,1)} %param.16) | copy-start | bytes 5308420
  2.6 15.0 %copy-start.4 = (f32[128]{0:T(128)S(1)}, f32[128]{0:T(128)}, u32[]{:S(2)}) copy-start(f32[128]{0:T(128)} %param.12) | copy-start | bytes 1540
  2.6 15.0 %copy-start.5 = (f32[128]{0:T(128)S(1)}, f32[128]{0:T(128)}, u32[]{:S(2)}) copy-start(f32[128]{0:T(128)} %param.15) | copy-start | bytes 1540
  2.6 15.0 %copy-start.6 = (f32[128]{0:T(128)S(1)}, f32[128]{0:T(128)}, u32[]{:S(2)}) copy-start(f32[128]{0:T(128)} %param.14) | copy-start | bytes 1540
  2.7 14.2 %collective-permute-start = (bf16[8,192,128]{2,1,0:T(8,128)(2,1)S(1)}, bf16[8,192,128]{2,1,0:T(8,128)(2,1)S(1)}, u32[]{:S(2)}, u32[]{:S(2)}) collective-permute-start(bf16[8,192,128]{2,1,0:T(8,128)(2,1)S(1)} %bitcast.19), channel_id=1, source_target_pairs={{0,8},{4,12},{8,16},{12,20},{16,24},{20,28},{24,0},{28,4},{1,9},{5... | collective-permute-start | bytes 1179656 | tf_op jit(solution)/shard_map/ppermute | solution.py:22
  5.8 3.6 %collective-permute-start.3 = (f32[8,128]{1,0:T(8,128)S(1)}, f32[8,128]{1,0:T(8,128)S(1)}, u32[]{:S(2)}, u32[]{:S(2)}) collective-permute-start(f32[8,128]{1,0:T(8,128)S(1)} %broadcast_in_dim.15), channel_id=1, source_target_pairs={{0,4},{4,0},{8,12},{12,8},{16,20},{20,16},{24,28},{28,24},{1,5},{5... | collective-permute-start | bytes 12296 | tf_op jit(solution)/shard_map/ppermute | solution.py:39
  7.3 10.2 %collective-permute-start.4 = (bf16[4,2,192,128]{3,2,1,0:T(8,128)(2,1)S(1)}, bf16[4,2,192,128]{3,2,1,0:T(8,128)(2,1)S(1)}, u32[]{:S(2)}, u32[]{:S(2)}) collective-permute-start(bf16[4,2,192,128]{3,2,1,0:T(8,128)(2,1)S(1)} %get-tuple-element.30), channel_id=1, source_target_pairs={{0,1},{1,0},{2,3},{3,2},{4,5},{5,4},{6,7},{7,6},{8,9},{9,8},{10,11... | collective-permute-start | bytes 1179656 | tf_op jit(solution)/shard_map/ppermute | solution.py:39
  9.4 8.1 %collective-permute-start.5 = (bf16[4,2,192,128]{3,2,1,0:T(8,128)(2,1)S(1)}, bf16[4,2,192,128]{3,2,1,0:T(8,128)(2,1)S(1)}, u32[]{:S(2)}, u32[]{:S(2)}) collective-permute-start(bf16[4,2,192,128]{3,2,1,0:T(8,128)(2,1)S(1)} %get-tuple-element.32), channel_id=1, source_target_pairs={{0,4},{1,2},{2,1},{3,7},{4,0},{5,6},{6,5},{7,3},{8,12},{9,10},{10,... | collective-permute-start | bytes 1179656 | tf_op jit(solution)/shard_map/ppermute | solution.py:67
  17.0 6.1 %collective-permute-start.1 = (bf16[4,192,128]{2,1,0:T(8,128)(2,1)S(1)}, bf16[4,192,128]{2,1,0:T(8,128)(2,1)S(1)}, u32[]{:S(2)}, u32[]{:S(2)}) collective-permute-start(bf16[4,192,128]{2,1,0:T(8,128)(2,1)S(1)} %get-tuple-element.54), channel_id=1, source_target_pairs={{0,1},{1,0},{2,3},{3,2},{4,5},{5,4},{6,7},{7,6},{8,16},{9,17},{10,... | collective-permute-start | bytes 589832 | tf_op jit(solution)/shard_map/ppermute | solution.py:35
  17.1 7.7 %collective-permute-start.2 = (bf16[4,192,128]{2,1,0:T(8,128)(2,1)S(1)}, bf16[4,192,128]{2,1,0:T(8,128)(2,1)S(1)}, u32[]{:S(2)}, u32[]{:S(2)}) collective-permute-start(bf16[4,192,128]{2,1,0:T(8,128)(2,1)S(1)} %get-tuple-element.53), channel_id=1, source_target_pairs={{0,1},{1,0},{2,3},{3,2},{4,5},{5,4},{6,7},{7,6},{8,16},{9,17},{10,... | collective-permute-start | bytes 589832 | tf_op jit(solution)/shard_map/ppermute | solution.py:35
  17.6 11.6 %copy-start.3 = (bf16[4,4,192,128]{3,2,1,0:T(8,128)(2,1)S(1)}, bf16[4,4,192,128]{3,2,1,0:T(8,128)(2,1)}, u32[]{:S(2)}) copy-start(bf16[4,4,192,128]{3,2,1,0:T(8,128)(2,1)} %video_ref.7) | copy-start | bytes 2359300
  17.6 11.6 %copy-start.7 = (f32[256]{0:T(256)S(1)}, f32[256]{0:T(256)}, u32[]{:S(2)}) copy-start(f32[256]{0:T(256)} %param.17) | copy-start | bytes 3076
  20.7 8.5 %collective-permute-start.7 = (bf16[2,192,128]{2,1,0:T(8,128)(2,1)S(1)}, bf16[2,192,128]{2,1,0:T(8,128)(2,1)S(1)}, u32[]{:S(2)}, u32[]{:S(2)}) collective-permute-start(bf16[2,192,128]{2,1,0:T(8,128)(2,1)S(1)} %get-tuple-element.35.own_ref), channel_id=1, source_target_pairs={{0,8},{4,12},{8,16},{12,20},{16,24},{20,28},{24,0},{28,4},{1,9},{5... | collective-permute-start | bytes 294920 | tf_op jit(solution)/shard_map/ppermute | solution.py:22
  23.2 9.3 %collective-permute-start.6 = (bf16[4,192,128]{2,1,0:T(8,128)(2,1)S(1)}, bf16[4,192,128]{2,1,0:T(8,128)(2,1)S(1)}, u32[]{:S(2)}, u32[]{:S(2)}) collective-permute-start(bf16[4,192,128]{2,1,0:T(8,128)(2,1)S(1)} %shard_map.93), channel_id=1, source_target_pairs={{0,4},{4,0},{8,12},{12,8},{16,20},{20,16},{24,28},{28,24},{1,5},{5... | collective-permute-start | bytes 589832 | tf_op jit(solution)/shard_map/ppermute | solution.py:39
  24.8 7.6 %collective-permute-start.8 = (bf16[4,192,128]{2,1,0:T(8,128)(2,1)S(1)}, bf16[4,192,128]{2,1,0:T(8,128)(2,1)S(1)}, u32[]{:S(2)}, u32[]{:S(2)}) collective-permute-start(bf16[4,192,128]{2,1,0:T(8,128)(2,1)S(1)} %shard_map.94), channel_id=1, source_target_pairs={{0,4},{4,0},{8,12},{12,8},{16,20},{20,16},{24,28},{28,24},{1,5},{5... | collective-permute-start | bytes 589832 | tf_op jit(solution)/shard_map/ppermute | solution.py:39
  29.2 5.1 %collective-permute-start.11 = (bf16[2,192,128]{2,1,0:T(8,128)(2,1)S(1)}, bf16[2,192,128]{2,1,0:T(8,128)(2,1)S(1)}, u32[]{:S(2)}, u32[]{:S(2)}) collective-permute-start(bf16[2,192,128]{2,1,0:T(8,128)(2,1)S(1)} %collective-permute-done.7.near_ref.two_ref), channel_id=1, source_target_pairs={{0,1},{1,0},{2,3},{3,2},{4,5},{5,4},{6,7},{7,6},{8,16},{9,17},{10,... | collective-permute-start | bytes 294920 | tf_op jit(solution)/shard_map/ppermute | solution.py:35
  32.7 6.6 %collective-permute-start.9 = (bf16[2,2,192,128]{3,2,1,0:T(8,128)(2,1)S(1)}, bf16[2,2,192,128]{3,2,1,0:T(8,128)(2,1)S(1)}, u32[]{:S(2)}, u32[]{:S(2)}) collective-permute-start(bf16[2,2,192,128]{3,2,1,0:T(8,128)(2,1)S(1)} %get-tuple-element.45), channel_id=1, source_target_pairs={{0,1},{1,0},{2,3},{3,2},{4,5},{5,4},{6,7},{7,6},{8,9},{9,8},{10,11... | collective-permute-start | bytes 589832 | tf_op jit(solution)/shard_map/ppermute | solution.py:39
  32.8 6.8 %collective-permute-start.10 = (bf16[2,2,192,128]{3,2,1,0:T(8,128)(2,1)S(1)}, bf16[2,2,192,128]{3,2,1,0:T(8,128)(2,1)S(1)}, u32[]{:S(2)}, u32[]{:S(2)}) collective-permute-start(bf16[2,2,192,128]{3,2,1,0:T(8,128)(2,1)S(1)} %get-tuple-element.46), channel_id=1, source_target_pairs={{0,3},{1,2},{2,1},{3,0},{4,7},{5,6},{6,5},{7,4},{8,16},{9,10},{10,... | collective-permute-start | bytes 589832 | tf_op jit(solution)/shard_map/ppermute | solution.py:56
  34.3 5.0 %collective-permute-start.12 = (bf16[2,192,128]{2,1,0:T(8,128)(2,1)S(1)}, bf16[2,192,128]{2,1,0:T(8,128)(2,1)S(1)}, u32[]{:S(2)}, u32[]{:S(2)}) collective-permute-start(bf16[2,192,128]{2,1,0:T(8,128)(2,1)S(1)} %shard_map.99), channel_id=1, source_target_pairs={{0,4},{4,0},{8,12},{12,8},{16,20},{20,16},{24,28},{28,24},{1,5},{5... | collective-permute-start | bytes 294920 | tf_op jit(solution)/shard_map/ppermute | solution.py:39

commit v7 on v6

--- a/solution.py
+++ b/solution.py
@@ -193,13 +193,12 @@
 
 
 def second_kernel(
-    flag_ref, video_ref, pair_ref, cross_ref, gain1_ref, weight1_ref, bias1_ref,
-    gain2_ref, weight2_ref, bias2_ref, strided3_ref, later_ref, late_ref, window_ref,
+    flag_ref, video_ref, pair_ref, cross_ref, weight1_ref, bias1_ref,
+    gain2_ref, weight2_ref, bias2_ref, strided3_ref, window_ref, later_ref, late_ref,
     stage_ref, strided_ref, total_ref,
 ):
     first_row = holds(flag_ref, TOP)
     readers = [row_reader(flag_ref, video_ref, f, pair_ref, cross_ref) for f in range(4)]
-    fill_hidden(readers[0], gain1_ref[...], window_ref, 0, range(7))
     total_ref[...] = (
         conv1_rows(window_ref, 0, 5, weight1_ref[0])
         + conv1_rows(later_ref, 0, 5, weight1_ref[1])
@@ -215,11 +214,12 @@
 
 
 def own_kernel(
-    flag_ref, video_ref, pair_ref, cross_ref, weight1_ref, bias1_ref, window_ref, later_ref,
-    first_ref, next_ref,
+    flag_ref, video_ref, pair_ref, cross_ref, gain1_ref, weight1_ref, bias1_ref, later_ref,
+    first_ref, next_ref, window_ref,
 ):
     channels = video_ref.shape[3]
     readers = [row_reader(flag_ref, video_ref, f, pair_ref, cross_ref) for f in range(2)]
+    fill_hidden(readers[0], gain1_ref[...], window_ref, 0, range(7))
     both = conv1_rows(window_ref, 0, 5, beside(weight1_ref, 2, 1))
     first_ref[...] = both[:, :channels].reshape(first_ref.shape)
     next_ref[...] = (
@@ -427,28 +427,30 @@
     chosen_own = for_partner(own, near, after(chosen_first, fars[1])[0], rows)
     odds = [swapped(chosen_first, "group"), swapped(chosen_own, "group")]
     near_e = after(chosen_own, rotated(own_e, "group", 2))[0]
-    late, start = call(
-        second_kernel,
+    far_e = relayed(near_e)
+    first, following, start = call(
+        own_kernel,
         [
-            flags, video_frames, pair, cross, gain1, weight1, bias1, gain2, weight2, bias2,
-            after(near_e, strided3)[0], later,
+            flags, video_frames, pair, cross, gain1, weight1, bias1, after(near_e, later)[0],
         ],
-        [like((rows // 2 * half, wide), F32), windows(1)],
-        [stage, strided, VMEM(total, F32)],
+        [like(total, F32), like(total, F32), windows(1)],
+        [],
         flops=WHILE_SWAPPED,
-    )
-    far_e = relayed(near_e)
-    first, following = call(
-        own_kernel,
-        [flags, video_frames, pair, cross, weight1, bias1, start, later],
-        [like(total, F32), like(total, F32)],
-        [],
-        flops=WHILE_SENT,
     )
     odd_e = swapped(for_partner(own_e, near_e, far_e), "group")
     edge = like((2, ABOVE, width, channels))
     prior, prior_pair, prior_cross = call(
-        prior_kernel, [flags, near] + fars + [odds[0], after(late, odds[1])[0]], [pair_of, edge, edge], []
+        prior_kernel, [flags, near] + fars + [odds[0], after(first, odds[1])[0]], [pair_of, edge, edge], []
+    )
+    (late,) = call(
+        second_kernel,
+        [
+            flags, video_frames, pair, cross, weight1, bias1, gain2, weight2, bias2,
+            after(prior, strided3)[0], start, later,
+        ],
+        [like((rows // 2 * half, wide), F32)],
+        [stage, strided, VMEM(total, F32)],
+        flops=WHILE_SENT,
     )
     prior_cross = crossed_late(prior_cross)
     prior_pair = swapped(prior_pair, "row")

time: 41.8 us -> 42.6 us (1.019)
  waiting for transfers between devices: 13 us -> 13.6 us
    ppermute x6, waiting for transfers between devices: 2.88 us -> 3.71 us  [swapped(): lax.ppermute(value, axis, [(place, place ^ 1) for place in range(lax.axis...]
  transfers between devices with their start and end apart: 13 -> 13, of which waited for: 6 -> 4; matrix products, arithmetic and copies ran while one was open for 0% -> 0% of each run, Pallas kernels for 22% -> 22%
where the time goes in v7:
time: 42.6 us; the launch traced here: 42.4 us
  starting transfers between devices  14.4 us (34%)
  waiting for transfers between devices  13.6 us (32%)
  Pallas kernels  11.7 us (27%)
  between operations  1.53 us (4%)
  local copies, waits for them, and re-layouts  1.23 us (3%)
    pallas_call x10, Pallas kernels, call(): pl.pallas_call(kernel, out_shape=outs, in_specs=[pl.BlockSpec(memory_spac...  11.7 us
    ppermute x2, waiting for transfers between devices, rotated(): lax.ppermute(value, axis, [(source, (source + steps) % count) for source...  9.84 us
    ppermute x2, starting transfers between devices, rotated(): lax.ppermute(value, axis, [(source, (source + steps) % count) for source...  5.49 us
    ppermute x6, starting transfers between devices, swapped(): lax.ppermute(value, axis, [(place, place ^ 1) for place in range(lax.axis...  5.28 us
    ppermute x6, waiting for transfers between devices, swapped(): lax.ppermute(value, axis, [(place, place ^ 1) for place in range(lax.axis...  3.71 us
    ppermute x1, starting transfers between devices, crossed_late(): return lax.ppermute(value, ('group', 'row'), pairs)  1.57 us
    ppermute x1, starting transfers between devices, crossed(): return lax.ppermute(value, ('group', 'row'), pairs)  1.49 us
    unnamed x16, local copies, waits for them, and re-layouts  1.16 us
  transfers between devices with their start and end apart: 13, of which 4 were waited for; matrix products, arithmetic and copies ran while one was open for 0% of the time, Pallas kernels for 22%

profile of v7, /device:TPU:0, one launch (start us, length us, event | category | flops | bytes accessed | tf_op | source)
XLA Modules:
  0.0 42.4 jit_solution(2349020991503910266)
XLA Ops:
  1.4 1.1 %copy-done.2 = bf16[4,4,192,128]{3,2,1,0:T(8,128)(2,1)S(1)} copy-done((bf16[4,4,192,128]{3,2,1,0:T(8,128)(2,1)S(1)}, bf16[4,4,192,128]{3,2,1,0:T(8,128)(2,1)}, u32[]{:S(2)}) %copy-start.2) | copy-done | bytes 786456
  2.6 0.2 shard_map.91
  2.7 3.1 %collective-permute-start = (bf16[8,192,128]{2,1,0:T(8,128)(2,1)S(1)}, bf16[8,192,128]{2,1,0:T(8,128)(2,1)S(1)}, u32[]{:S(2)}, u32[]{:S(2)}) collective-permute-start(bf16[8,192,128]{2,1,0:T(8,128)(2,1)S(1)} %bitcast.19), channel_id=1, source_target_pairs={{0,8},{4,12},{8,16},{12,20},{16,24},{20,28},{24,0},{28,4},{1,9},{5... | collective-permute-start | bytes 1179656 | tf_op jit(solution)/shard_map/ppermute | solution.py:22
  5.8 1.5 %collective-permute-start.3 = (f32[8,128]{1,0:T(8,128)S(1)}, f32[8,128]{1,0:T(8,128)S(1)}, u32[]{:S(2)}, u32[]{:S(2)}) collective-permute-start(f32[8,128]{1,0:T(8,128)S(1)} %broadcast_in_dim.15), channel_id=1, source_target_pairs={{0,4},{4,0},{8,12},{12,8},{16,20},{20,16},{24,28},{28,24},{1,5},{5... | collective-permute-start | bytes 12296 | tf_op jit(solution)/shard_map/ppermute | solution.py:39
  7.3 2.1 %collective-permute-done.3.wanted_ref = f32[8,128]{1,0:T(8,128)S(1)} collective-permute-done((f32[8,128]{1,0:T(8,128)S(1)}, f32[8,128]{1,0:T(8,128)S(1)}, u32[]{:S(2)}, u32[]{:S(2)}) %collective-permute-start.3) | collective-permute-done | bytes 4128 | tf_op jit(solution)/shard_map/ppermute | solution.py:39
  9.4 1.5 %collective-permute-start.5 = (bf16[4,2,192,128]{3,2,1,0:T(8,128)(2,1)S(1)}, bf16[4,2,192,128]{3,2,1,0:T(8,128)(2,1)S(1)}, u32[]{:S(2)}, u32[]{:S(2)}) collective-permute-start(bf16[4,2,192,128]{3,2,1,0:T(8,128)(2,1)S(1)} %get-tuple-element.32), channel_id=1, source_target_pairs={{0,4},{1,2},{2,1},{3,7},{4,0},{5,6},{6,5},{7,3},{8,12},{9,10},{10,... | collective-permute-start | bytes 1179656 | tf_op jit(solution)/shard_map/ppermute | solution.py:67
  10.9 6.0 %collective-permute-done.near_ref.two_ref = bf16[8,192,128]{2,1,0:T(8,128)(2,1)S(1)} collective-permute-done((bf16[8,192,128]{2,1,0:T(8,128)(2,1)S(1)}, bf16[8,192,128]{2,1,0:T(8,128)(2,1)S(1)}, u32[]{:S(2)}, u32[]{:S(2)}) %collective-permute-start) | collective-permute-done | bytes 393248 | tf_op jit(solution)/shard_map/ppermute | solution.py:22
  17.0 0.5 %collective-permute-start.2 = (bf16[4,192,128]{2,1,0:T(8,128)(2,1)S(1)}, bf16[4,192,128]{2,1,0:T(8,128)(2,1)S(1)}, u32[]{:S(2)}, u32[]{:S(2)}) collective-permute-start(bf16[4,192,128]{2,1,0:T(8,128)(2,1)S(1)} %get-tuple-element.53), channel_id=1, source_target_pairs={{0,1},{1,0},{2,3},{3,2},{4,5},{5,4},{6,7},{7,6},{8,16},{9,17},{10,... | collective-permute-start | bytes 589832 | tf_op jit(solution)/shard_map/ppermute | solution.py:35
  17.6 3.0 %shard_map.92 = (bf16[2,192,128]{2,1,0:T(8,128)(2,1)S(1)}, bf16[1,5,96,384]{3,2,1,0:T(8,128)(2,1)S(1)}, bf16[3,7,192,384]{3,2,1,0:T(8,128)(2,1)S(1)}) custom-call(f32[8,128]{1,0:T(8,128)S(1)} %stack.7.flag_ref, bf16[4,4,192,128]{3,2,1,0:T(8,128)(2,1)S(1)} %copy-done.2, bf16[4,2,192,128]{3,2,1,0:T(8,128)(2,1)S(1)} %collective-permute-done.4.pair_ref, ...), custom_call_target="tpu_custom_call" | custom-call | flops 962592768 | bytes 7796224 | tf_op jit(solution)/shard_map/pallas_call | solution.py:349
  20.6 2.4 %collective-permute-start.7 = (bf16[2,192,128]{2,1,0:T(8,128)(2,1)S(1)}, bf16[2,192,128]{2,1,0:T(8,128)(2,1)S(1)}, u32[]{:S(2)}, u32[]{:S(2)}) collective-permute-start(bf16[2,192,128]{2,1,0:T(8,128)(2,1)S(1)} %get-tuple-element.35.own_ref), channel_id=1, source_target_pairs={{0,8},{4,12},{8,16},{12,20},{16,24},{20,28},{24,0},{28,4},{1,9},{5... | collective-permute-start | bytes 294920 | tf_op jit(solution)/shard_map/ppermute | solution.py:22
  23.0 0.1 shard_map.93
  23.1 1.6 %collective-permute-start.6 = (bf16[4,192,128]{2,1,0:T(8,128)(2,1)S(1)}, bf16[4,192,128]{2,1,0:T(8,128)(2,1)S(1)}, u32[]{:S(2)}, u32[]{:S(2)}) collective-permute-start(bf16[4,192,128]{2,1,0:T(8,128)(2,1)S(1)} %shard_map.93), channel_id=1, source_target_pairs={{0,4},{4,0},{8,12},{12,8},{16,20},{20,16},{24,28},{28,24},{1,5},{5... | collective-permute-start | bytes 589832 | tf_op jit(solution)/shard_map/ppermute | solution.py:39
  24.7 0.1 shard_map.94
  24.8 0.6 %collective-permute-start.8 = (bf16[4,192,128]{2,1,0:T(8,128)(2,1)S(1)}, bf16[4,192,128]{2,1,0:T(8,128)(2,1)S(1)}, u32[]{:S(2)}, u32[]{:S(2)}) collective-permute-start(bf16[4,192,128]{2,1,0:T(8,128)(2,1)S(1)} %shard_map.94), channel_id=1, source_target_pairs={{0,4},{4,0},{8,12},{12,8},{16,20},{20,16},{24,28},{28,24},{1,5},{5... | collective-permute-start | bytes 589832 | tf_op jit(solution)/shard_map/ppermute | solution.py:39
  25.4 3.8 %collective-permute-done.7.near_ref.two_ref = bf16[2,192,128]{2,1,0:T(8,128)(2,1)S(1)} collective-permute-done((bf16[2,192,128]{2,1,0:T(8,128)(2,1)S(1)}, bf16[2,192,128]{2,1,0:T(8,128)(2,1)S(1)}, u32[]{:S(2)}, u32[]{:S(2)}) %collective-permute-start.7) | collective-permute-done | bytes 98336 | tf_op jit(solution)/shard_map/ppermute | solution.py:22
  29.2 1.6 %shard_map.95 = (f32[5,192,128]{2,1,0:T(8,128)S(1)}, f32[5,192,128]{2,1,0:T(8,128)S(1)}, bf16[1,7,192,384]{3,2,1,0:T(8,128)(2,1)S(1)}) custom-call(f32[8,128]{1,0:T(8,128)S(1)} %stack.7.flag_ref, bf16[4,4,192,128]{3,2,1,0:T(8,128)(2,1)S(1)} %copy-done.3, bf16[4,2,192,128]{3,2,1,0:T(8,128)(2,1)S(1)} %collective-permute-done.4.pair_ref, ...), custom_call_target="tpu_custom_call" | custom-call | flops 3000000000 | bytes 7574528 | tf_op jit(solution)/shard_map/pallas_call | solution.py:349
  30.8 1.6 %collective-permute-done.8.odd1_ref = bf16[4,192,128]{2,1,0:T(8,128)(2,1)S(1)} collective-permute-done((bf16[4,192,128]{2,1,0:T(8,128)(2,1)S(1)}, bf16[4,192,128]{2,1,0:T(8,128)(2,1)S(1)}, u32[]{:S(2)}, u32[]{:S(2)}) %collective-permute-start.8) | collective-permute-done | bytes 196640 | tf_op jit(solution)/shard_map/ppermute | solution.py:39
  32.4 0.2 shard_map.96
  32.6 0.1 collective-permute-start.9
  32.7 1.6 %collective-permute-start.10 = (bf16[2,2,192,128]{3,2,1,0:T(8,128)(2,1)S(1)}, bf16[2,2,192,128]{3,2,1,0:T(8,128)(2,1)S(1)}, u32[]{:S(2)}, u32[]{:S(2)}) collective-permute-start(bf16[2,2,192,128]{3,2,1,0:T(8,128)(2,1)S(1)} %get-tuple-element.45), channel_id=1, source_target_pairs={{0,3},{1,2},{2,1},{3,0},{4,7},{5,6},{6,5},{7,4},{8,16},{9,10},{10,... | collective-permute-start | bytes 589832 | tf_op jit(solution)/shard_map/ppermute | solution.py:56
  34.3 1.6 %collective-permute-start.12 = (bf16[2,192,128]{2,1,0:T(8,128)(2,1)S(1)}, bf16[2,192,128]{2,1,0:T(8,128)(2,1)S(1)}, u32[]{:S(2)}, u32[]{:S(2)}) collective-permute-start(bf16[2,192,128]{2,1,0:T(8,128)(2,1)S(1)} %shard_map.99), channel_id=1, source_target_pairs={{0,4},{4,0},{8,12},{12,8},{16,20},{20,16},{24,28},{28,24},{1,5},{5... | collective-permute-start | bytes 294920 | tf_op jit(solution)/shard_map/ppermute | solution.py:39
  35.9 2.8 %shard_map.98.late_ref = f32[192,256]{1,0:T(8,128)S(1)} custom-call(f32[8,128]{1,0:T(8,128)S(1)} %stack.7.flag_ref, bf16[4,4,192,128]{3,2,1,0:T(8,128)(2,1)S(1)} %copy-done.3, bf16[4,2,192,128]{3,2,1,0:T(8,128)(2,1)S(1)} %collective-permute-done.4.pair_ref, bf16[4,2,192,128]{3,2,1,0:T(8,128)(2,1)S(1)} %collective-permute-done.5.cross_ref, ...), custom_call_target="tpu_custom_call" | custom-call | flops 200000000 | bytes 8927232 | tf_op jit(solution)/shard_map/pallas_call | solution.py:349
  38.7 1.6 %shard_map.97 = (f32[5,192,128]{2,1,0:T(8,128)S(1)}, f32[5,192,128]{2,1,0:T(8,128)S(1)}, bf16[2,5,96,384]{3,2,1,0:T(8,128)(2,1)S(1)}) custom-call(f32[8,128]{1,0:T(8,128)S(1)} %stack.7.flag_ref, bf16[2,4,192,128]{3,2,1,0:T(8,128)(2,1)S(1)} %get-tuple-element.43.prior_ref, f32[1,128]{1,0:T(1,128)S(1)} %bitcast.28, bf16[3,3,384,128]{3,2,1,0:T(8,128)(2,1)S(1)} %bitcast.17, ...), custom_call_target="tpu_custom_call" | custom-call | flops 566231040 | bytes 3986432 | tf_op jit(solution)/shard_map/pallas_call | solution.py:349
  40.3 2.1 %shard_map.100 = bf16[2,2,96,256]{3,2,1,0:T(8,128)(2,1)} custom-call(f32[8,128]{1,0:T(8,128)S(1)} %stack.7.flag_ref, bf16[2,4,192,128]{3,2,1,0:T(8,128)(2,1)S(1)} %get-tuple-element.43.prior_ref, bf16[2,2,192,128]{3,2,1,0:T(8,128)(2,1)S(1)} %collective-permute-done.9.pair_ref, bf16[2,2,192,128]{3,2,1,0:T(8,128)(2,1)S(1)} %collective-permute-done.10.cross_ref, ...), custom_call_target="tpu_custom_call" | custom-call | flops 622854144 | bytes 5855232 | tf_op jit(solution)/shard_map/pallas_call | solution.py:349
  (38 shorter events, 0.2 us)
Async XLA Ops:
  1.4 1.1 %copy-start.2 = (bf16[4,4,192,128]{3,2,1,0:T(8,128)(2,1)S(1)}, bf16[4,4,192,128]{3,2,1,0:T(8,128)(2,1)}, u32[]{:S(2)}) copy-start(bf16[4,4,192,128]{3,2,1,0:T(8,128)(2,1)} %video_ref.7) | copy-start | bytes 2359300
  2.5 15.0 %copy-start = (bf16[3,3,3,128,256]{4,3,2,1,0:T(8,128)(2,1)S(1)}, bf16[3,3,3,128,256]{4,3,2,1,0:T(8,128)(2,1)}, u32[]{:S(2)}) copy-start(bf16[3,3,3,128,256]{4,3,2,1,0:T(8,128)(2,1)} %param.16) | copy-start | bytes 5308420
  2.5 15.0 %copy-start.1 = (bf16[3,3,3,128,128]{4,3,2,1,0:T(8,128)(2,1)S(1)}, bf16[3,3,3,128,128]{4,3,2,1,0:T(8,128)(2,1)}, u32[]{:S(2)}) copy-start(bf16[3,3,3,128,128]{4,3,2,1,0:T(8,128)(2,1)} %param.13) | copy-start | bytes 2654212
  2.5 15.0 %copy-start.4 = (f32[128]{0:T(128)S(1)}, f32[128]{0:T(128)}, u32[]{:S(2)}) copy-start(f32[128]{0:T(128)} %param.15) | copy-start | bytes 1540
  2.5 15.0 %copy-start.5 = (f32[128]{0:T(128)S(1)}, f32[128]{0:T(128)}, u32[]{:S(2)}) copy-start(f32[128]{0:T(128)} %param.12) | copy-start | bytes 1540
  2.6 15.0 %copy-start.7 = (f32[128]{0:T(128)S(1)}, f32[128]{0:T(128)}, u32[]{:S(2)}) copy-start(f32[128]{0:T(128)} %param.14) | copy-start | bytes 1540
  2.7 14.2 %collective-permute-start = (bf16[8,192,128]{2,1,0:T(8,128)(2,1)S(1)}, bf16[8,192,128]{2,1,0:T(8,128)(2,1)S(1)}, u32[]{:S(2)}, u32[]{:S(2)}) collective-permute-start(bf16[8,192,128]{2,1,0:T(8,128)(2,1)S(1)} %bitcast.19), channel_id=1, source_target_pairs={{0,8},{4,12},{8,16},{12,20},{16,24},{20,28},{24,0},{28,4},{1,9},{5... | collective-permute-start | bytes 1179656 | tf_op jit(solution)/shard_map/ppermute | solution.py:22
  5.8 3.6 %collective-permute-start.3 = (f32[8,128]{1,0:T(8,128)S(1)}, f32[8,128]{1,0:T(8,128)S(1)}, u32[]{:S(2)}, u32[]{:S(2)}) collective-permute-start(f32[8,128]{1,0:T(8,128)S(1)} %broadcast_in_dim.15), channel_id=1, source_target_pairs={{0,4},{4,0},{8,12},{12,8},{16,20},{20,16},{24,28},{28,24},{1,5},{5... | collective-permute-start | bytes 12296 | tf_op jit(solution)/shard_map/ppermute | solution.py:39
  7.3 10.2 %collective-permute-start.4 = (bf16[4,2,192,128]{3,2,1,0:T(8,128)(2,1)S(1)}, bf16[4,2,192,128]{3,2,1,0:T(8,128)(2,1)S(1)}, u32[]{:S(2)}, u32[]{:S(2)}) collective-permute-start(bf16[4,2,192,128]{3,2,1,0:T(8,128)(2,1)S(1)} %get-tuple-element.30), channel_id=1, source_target_pairs={{0,1},{1,0},{2,3},{3,2},{4,5},{5,4},{6,7},{7,6},{8,9},{9,8},{10,11... | collective-permute-start | bytes 1179656 | tf_op jit(solution)/shard_map/ppermute | solution.py:39
  9.4 8.1 %collective-permute-start.5 = (bf16[4,2,192,128]{3,2,1,0:T(8,128)(2,1)S(1)}, bf16[4,2,192,128]{3,2,1,0:T(8,128)(2,1)S(1)}, u32[]{:S(2)}, u32[]{:S(2)}) collective-permute-start(bf16[4,2,192,128]{3,2,1,0:T(8,128)(2,1)S(1)} %get-tuple-element.32), channel_id=1, source_target_pairs={{0,4},{1,2},{2,1},{3,7},{4,0},{5,6},{6,5},{7,3},{8,12},{9,10},{10,... | collective-permute-start | bytes 1179656 | tf_op jit(solution)/shard_map/ppermute | solution.py:67
  17.0 6.1 %collective-permute-start.1 = (bf16[4,192,128]{2,1,0:T(8,128)(2,1)S(1)}, bf16[4,192,128]{2,1,0:T(8,128)(2,1)S(1)}, u32[]{:S(2)}, u32[]{:S(2)}) collective-permute-start(bf16[4,192,128]{2,1,0:T(8,128)(2,1)S(1)} %get-tuple-element.54), channel_id=1, source_target_pairs={{0,1},{1,0},{2,3},{3,2},{4,5},{5,4},{6,7},{7,6},{8,16},{9,17},{10,... | collective-permute-start | bytes 589832 | tf_op jit(solution)/shard_map/ppermute | solution.py:35
  17.0 7.6 %collective-permute-start.2 = (bf16[4,192,128]{2,1,0:T(8,128)(2,1)S(1)}, bf16[4,192,128]{2,1,0:T(8,128)(2,1)S(1)}, u32[]{:S(2)}, u32[]{:S(2)}) collective-permute-start(bf16[4,192,128]{2,1,0:T(8,128)(2,1)S(1)} %get-tuple-element.53), channel_id=1, source_target_pairs={{0,1},{1,0},{2,3},{3,2},{4,5},{5,4},{6,7},{7,6},{8,16},{9,17},{10,... | collective-permute-start | bytes 589832 | tf_op jit(solution)/shard_map/ppermute | solution.py:35
  17.6 11.6 %copy-start.3 = (bf16[4,4,192,128]{3,2,1,0:T(8,128)(2,1)S(1)}, bf16[4,4,192,128]{3,2,1,0:T(8,128)(2,1)}, u32[]{:S(2)}) copy-start(bf16[4,4,192,128]{3,2,1,0:T(8,128)(2,1)} %video_ref.7) | copy-start | bytes 2359300
  20.6 8.5 %collective-permute-start.7 = (bf16[2,192,128]{2,1,0:T(8,128)(2,1)S(1)}, bf16[2,192,128]{2,1,0:T(8,128)(2,1)S(1)}, u32[]{:S(2)}, u32[]{:S(2)}) collective-permute-start(bf16[2,192,128]{2,1,0:T(8,128)(2,1)S(1)} %get-tuple-element.35.own_ref), channel_id=1, source_target_pairs={{0,8},{4,12},{8,16},{12,20},{16,24},{20,28},{24,0},{28,4},{1,9},{5... | collective-permute-start | bytes 294920 | tf_op jit(solution)/shard_map/ppermute | solution.py:22
  23.1 9.3 %collective-permute-start.6 = (bf16[4,192,128]{2,1,0:T(8,128)(2,1)S(1)}, bf16[4,192,128]{2,1,0:T(8,128)(2,1)S(1)}, u32[]{:S(2)}, u32[]{:S(2)}) collective-permute-start(bf16[4,192,128]{2,1,0:T(8,128)(2,1)S(1)} %shard_map.93), channel_id=1, source_target_pairs={{0,4},{4,0},{8,12},{12,8},{16,20},{20,16},{24,28},{28,24},{1,5},{5... | collective-permute-start | bytes 589832 | tf_op jit(solution)/shard_map/ppermute | solution.py:39
  24.8 7.6 %collective-permute-start.8 = (bf16[4,192,128]{2,1,0:T(8,128)(2,1)S(1)}, bf16[4,192,128]{2,1,0:T(8,128)(2,1)S(1)}, u32[]{:S(2)}, u32[]{:S(2)}) collective-permute-start(bf16[4,192,128]{2,1,0:T(8,128)(2,1)S(1)} %shard_map.94), channel_id=1, source_target_pairs={{0,4},{4,0},{8,12},{12,8},{16,20},{20,16},{24,28},{28,24},{1,5},{5... | collective-permute-start | bytes 589832 | tf_op jit(solution)/shard_map/ppermute | solution.py:39
  29.2 5.1 %collective-permute-start.11 = (bf16[2,192,128]{2,1,0:T(8,128)(2,1)S(1)}, bf16[2,192,128]{2,1,0:T(8,128)(2,1)S(1)}, u32[]{:S(2)}, u32[]{:S(2)}) collective-permute-start(bf16[2,192,128]{2,1,0:T(8,128)(2,1)S(1)} %collective-permute-done.7.near_ref.two_ref), channel_id=1, source_target_pairs={{0,1},{1,0},{2,3},{3,2},{4,5},{5,4},{6,7},{7,6},{8,16},{9,17},{10,... | collective-permute-start | bytes 294920 | tf_op jit(solution)/shard_map/ppermute | solution.py:35
  29.2 6.7 %copy-start.6 = (f32[256]{0:T(256)S(1)}, f32[256]{0:T(256)}, u32[]{:S(2)}) copy-start(f32[256]{0:T(256)} %param.17) | copy-start | bytes 3076
  32.6 7.7 %collective-permute-start.9 = (bf16[2,2,192,128]{3,2,1,0:T(8,128)(2,1)S(1)}, bf16[2,2,192,128]{3,2,1,0:T(8,128)(2,1)S(1)}, u32[]{:S(2)}, u32[]{:S(2)}) collective-permute-start(bf16[2,2,192,128]{3,2,1,0:T(8,128)(2,1)S(1)} %get-tuple-element.44), channel_id=1, source_target_pairs={{0,1},{1,0},{2,3},{3,2},{4,5},{5,4},{6,7},{7,6},{8,9},{9,8},{10,11... | collective-permute-start | bytes 589832 | tf_op jit(solution)/shard_map/ppermute | solution.py:39
  32.7 7.6 %collective-permute-start.10 = (bf16[2,2,192,128]{3,2,1,0:T(8,128)(2,1)S(1)}, bf16[2,2,192,128]{3,2,1,0:T(8,128)(2,1)S(1)}, u32[]{:S(2)}, u32[]{:S(2)}) collective-permute-start(bf16[2,2,192,128]{3,2,1,0:T(8,128)(2,1)S(1)} %get-tuple-element.45), channel_id=1, source_target_pairs={{0,3},{1,2},{2,1},{3,0},{4,7},{5,6},{6,5},{7,4},{8,16},{9,10},{10,... | collective-permute-start | bytes 589832 | tf_op jit(solution)/shard_map/ppermute | solution.py:56
  34.3 6.0 %collective-permute-start.12 = (bf16[2,192,128]{2,1,0:T(8,128)(2,1)S(1)}, bf16[2,192,128]{2,1,0:T(8,128)(2,1)S(1)}, u32[]{:S(2)}, u32[]{:S(2)}) collective-permute-start(bf16[2,192,128]{2,1,0:T(8,128)(2,1)S(1)} %shard_map.99), channel_id=1, source_target_pairs={{0,4},{4,0},{8,12},{12,8},{16,20},{20,16},{24,28},{28,24},{1,5},{5... | collective-permute-start | bytes 294920 | tf_op jit(solution)/shard_map/ppermute | solution.py:39

commit v8 on v6

--- a/solution.py
+++ b/solution.py
@@ -148,10 +148,11 @@
     return read
 
 
-def pack_kernel(flag_ref, video_ref, own_ref, pair_ref, cross_ref):
+def pack_kernel(flag_ref, video_ref, own0_ref, own1_ref, pair_ref, cross_ref):
     even = holds(flag_ref, EVEN)
     frames, rows = video_ref.shape[:2]
-    own_ref[...] = video_ref[frames - 2 :]
+    own0_ref[...] = video_ref[frames - 2]
+    own1_ref[...] = video_ref[frames - 1]
     split_edges(even, video_ref, frames, rows, pair_ref, cross_ref)
 
 
@@ -246,14 +247,15 @@
 
 
 def prior_kernel(
-    flag_ref, two_ref, four0_ref, four1_ref, odd0_ref, odd1_ref, prior_ref, pair_ref, cross_ref,
+    flag_ref, two0_ref, two1_ref, four0_ref, four1_ref, odd0_ref, odd1_ref, prior_ref, pair_ref, cross_ref,
 ):
     even, distance = holds(flag_ref, EVEN), flag_ref[DISTANCE : DISTANCE + 1]
     frames, rows = prior_ref.shape[:2]
-    for frame, (four_ref, odd_ref) in enumerate(((four0_ref, odd0_ref), (four1_ref, odd1_ref))):
+    sources = ((two0_ref, four0_ref, odd0_ref), (two1_ref, four1_ref, odd1_ref))
+    for frame, (two_ref, four_ref, odd_ref) in enumerate(sources):
         for row in range(rows):
             prior_ref[frame, row] = chosen(
-                distance, two_ref[frame * rows + row], four_ref[row], odd_ref[row]
+                distance, two_ref[row], four_ref[row], odd_ref[row]
             )
     split_edges(even, prior_ref, frames, rows, pair_ref, cross_ref)
 
@@ -389,7 +391,7 @@
     gain1, bias1 = norm1_gain[None], conv1_bias[None]
     gain2, bias2 = norm2_gain[None], conv2_bias[None]
     pair_of = like((2, rows, width, channels))
-    flat = (2 * rows, width, channels)
+    frame_of = like((rows, width, channels))
     total = (rows + 1, width, channels)
     stage = VMEM((rows + 1, width + 16, channels), F32)
     strided = VMEM((2, rows + 1, half, 3 * channels), BF16)
@@ -397,19 +399,15 @@
     one_code = 2 * (rows // 2) * half * 9 * channels * wide
 
     edge = like((frames, ABOVE, width, channels))
-    own, pair, cross = call(
-        pack_kernel, [flags, video_frames], [pair_of, edge, edge], [], flops=PACK
+    own0, own1, pair, cross = call(
+        pack_kernel, [flags, video_frames], [frame_of, frame_of, edge, edge], [], flops=PACK
     )
     wanted = swapped(jnp.full((8, channels), distance, F32), "group")
-    cross = crossed(after(wanted, cross)[0])
-    own = own.reshape(flat)
-    near = rotated(own, "group", 2)
+    cross = crossed(cross)
+    nears = [rotated(own0, "group", 2), rotated(own1, "group", 2)]
     pair = swapped(pair, "row")
-    fars = [
-        relayed(lax.slice_in_dim(near, frame * rows, (frame + 1) * rows, axis=0))
-        for frame in range(2)
-    ]
-    pair, cross = after(near, pair, cross)
+    fars = [relayed(near) for near in nears]
+    pair, cross = after(nears[1], pair, cross)
     def windows(count):
         return like((count, rows + 3, width, 3 * channels))
 
@@ -423,8 +421,8 @@
         [stage, VMEM(total, F32)],
         flops=3 * one_tap + one_code,
     )
-    chosen_first = for_partner(own, near, after(own_e, fars[0])[0])
-    chosen_own = for_partner(own, near, after(chosen_first, fars[1])[0], rows)
+    chosen_first = for_partner(own0, nears[0], after(own_e, fars[0])[0])
+    chosen_own = for_partner(own1, nears[1], after(chosen_first, fars[1])[0])
     odds = [swapped(chosen_first, "group"), swapped(chosen_own, "group")]
     near_e = after(chosen_own, rotated(own_e, "group", 2))[0]
     late, start = call(
@@ -448,7 +446,7 @@
     odd_e = swapped(for_partner(own_e, near_e, far_e), "group")
     edge = like((2, ABOVE, width, channels))
     prior, prior_pair, prior_cross = call(
-        prior_kernel, [flags, near] + fars + [odds[0], after(late, odds[1])[0]], [pair_of, edge, edge], []
+        prior_kernel, [flags] + nears + fars + [odds[0], after(late, odds[1])[0]], [pair_of, edge, edge], []
     )
     prior_cross = crossed_late(prior_cross)
     prior_pair = swapped(prior_pair, "row")

time: 41.8 us -> 46.2 us (1.11)
  waiting for transfers between devices: 13 us -> 19.2 us
  starting transfers between devices: 14.4 us -> 12.6 us
    ppermute x6, waiting for transfers between devices: 2.88 us -> 7.94 us  [swapped(): lax.ppermute(value, axis, [(place, place ^ 1) for place in range(lax.axis...]
    ppermute x6, starting transfers between devices: 5.39 us -> 4.27 us  [swapped(): lax.ppermute(value, axis, [(place, place ^ 1) for place in range(lax.axis...]
    ppermute x1, starting transfers between devices: 1.49 us -> 2.56 us  [crossed(): return lax.ppermute(value, ('group', 'row'), pairs)]
    ppermute x2 -> x3, starting transfers between devices: 5.49 us -> 4.55 us  [rotated(): lax.ppermute(value, axis, [(source, (source + steps) % count) for source...]
    ppermute x2 -> x3, waiting for transfers between devices: 9.82 us -> 10.6 us  [rotated(): lax.ppermute(value, axis, [(source, (source + steps) % count) for source...]
    ppermute x3, starting transfers between devices: 0.55 us -> 0.01 us  [relayed(): return lax.ppermute(value, ('group', 'row'), pairs)]
  transfers between devices with their start and end apart: 13 -> 14, of which waited for: 6 -> 6; matrix products, arithmetic and copies ran while one was open for 0% -> 0% of each run, Pallas kernels for 22% -> 20%
where the time goes in v8:
time: 46.2 us; the launch traced here: 46 us
  waiting for transfers between devices  19.2 us (42%)
  starting transfers between devices  12.6 us (27%)
  Pallas kernels  11.5 us (25%)
  between operations  1.53 us (3%)
  local copies, waits for them, and re-layouts  1.21 us (3%)
    pallas_call x10, Pallas kernels, call(): pl.pallas_call(kernel, out_shape=outs, in_specs=[pl.BlockSpec(memory_spac...  11.5 us
    ppermute x3, waiting for transfers between devices, rotated(): lax.ppermute(value, axis, [(source, (source + steps) % count) for source...  10.6 us
    ppermute x6, waiting for transfers between devices, swapped(): lax.ppermute(value, axis, [(place, place ^ 1) for place in range(lax.axis...  7.94 us
    ppermute x3, starting transfers between devices, rotated(): lax.ppermute(value, axis, [(source, (source + steps) % count) for source...  4.55 us
    ppermute x6, starting transfers between devices, swapped(): lax.ppermute(value, axis, [(place, place ^ 1) for place in range(lax.axis...  4.27 us
    ppermute x1, starting transfers between devices, crossed(): return lax.ppermute(value, ('group', 'row'), pairs)  2.56 us
    ppermute x1, starting transfers between devices, crossed_late(): return lax.ppermute(value, ('group', 'row'), pairs)  1.16 us
    unnamed x16, local copies, waits for them, and re-layouts  1.16 us
  transfers between devices with their start and end apart: 14, of which 6 were waited for; matrix products, arithmetic and copies ran while one was open for 0% of the time, Pallas kernels for 20%

profile of v8, /device:TPU:0, one launch (start us, length us, event | category | flops | bytes accessed | tf_op | source)
XLA Modules:
  0.0 46.0 jit_solution(18093213575108723942)
XLA Ops:
  1.4 1.1 %copy-done.2 = bf16[4,4,192,128]{3,2,1,0:T(8,128)(2,1)S(1)} copy-done((bf16[4,4,192,128]{3,2,1,0:T(8,128)(2,1)S(1)}, bf16[4,4,192,128]{3,2,1,0:T(8,128)(2,1)}, u32[]{:S(2)}) %copy-start.2) | copy-done | bytes 786456
  2.6 0.2 shard_map.91
  2.8 0.5 %collective-permute-start.5 = (bf16[4,2,192,128]{3,2,1,0:T(8,128)(2,1)S(1)}, bf16[4,2,192,128]{3,2,1,0:T(8,128)(2,1)S(1)}, u32[]{:S(2)}, u32[]{:S(2)}) collective-permute-start(bf16[4,2,192,128]{3,2,1,0:T(8,128)(2,1)S(1)} %get-tuple-element.31), channel_id=1, source_target_pairs={{0,1},{1,0},{2,3},{3,2},{4,5},{5,4},{6,7},{7,6},{8,9},{9,8},{10,11... | collective-permute-start | bytes 1179656 | tf_op jit(solution)/shard_map/ppermute | solution.py:39
  3.3 2.6 %collective-permute-start.6 = (bf16[4,2,192,128]{3,2,1,0:T(8,128)(2,1)S(1)}, bf16[4,2,192,128]{3,2,1,0:T(8,128)(2,1)S(1)}, u32[]{:S(2)}, u32[]{:S(2)}) collective-permute-start(bf16[4,2,192,128]{3,2,1,0:T(8,128)(2,1)S(1)} %get-tuple-element.32), channel_id=1, source_target_pairs={{0,4},{1,2},{2,1},{3,7},{4,0},{5,6},{6,5},{7,3},{8,12},{9,10},{10,... | collective-permute-start | bytes 1179656 | tf_op jit(solution)/shard_map/ppermute | solution.py:67
  5.9 1.6 %collective-permute-start = (bf16[4,192,128]{2,1,0:T(8,128)(2,1)S(1)}, bf16[4,192,128]{2,1,0:T(8,128)(2,1)S(1)}, u32[]{:S(2)}, u32[]{:S(2)}) collective-permute-start(bf16[4,192,128]{2,1,0:T(8,128)(2,1)S(1)} %get-tuple-element.29.own_ref), channel_id=1, source_target_pairs={{0,8},{4,12},{8,16},{12,20},{16,24},{20,28},{24,0},{28,4},{1,9},{5... | collective-permute-start | bytes 589832 | tf_op jit(solution)/shard_map/ppermute | solution.py:22
  7.4 1.6 %collective-permute-start.1 = (bf16[4,192,128]{2,1,0:T(8,128)(2,1)S(1)}, bf16[4,192,128]{2,1,0:T(8,128)(2,1)S(1)}, u32[]{:S(2)}, u32[]{:S(2)}) collective-permute-start(bf16[4,192,128]{2,1,0:T(8,128)(2,1)S(1)} %get-tuple-element.30.own_ref), channel_id=1, source_target_pairs={{0,8},{4,12},{8,16},{12,20},{16,24},{20,28},{24,0},{28,4},{1,9},{5... | collective-permute-start | bytes 589832 | tf_op jit(solution)/shard_map/ppermute | solution.py:22
  9.0 6.4 %collective-permute-done.near_ref.two0_ref = bf16[4,192,128]{2,1,0:T(8,128)(2,1)S(1)} collective-permute-done((bf16[4,192,128]{2,1,0:T(8,128)(2,1)S(1)}, bf16[4,192,128]{2,1,0:T(8,128)(2,1)S(1)}, u32[]{:S(2)}, u32[]{:S(2)}) %collective-permute-start) | collective-permute-done | bytes 196640 | tf_op jit(solution)/shard_map/ppermute | solution.py:22
  15.4 4.2 %collective-permute-done.1.near_ref.two1_ref = bf16[4,192,128]{2,1,0:T(8,128)(2,1)S(1)} collective-permute-done((bf16[4,192,128]{2,1,0:T(8,128)(2,1)S(1)}, bf16[4,192,128]{2,1,0:T(8,128)(2,1)S(1)}, u32[]{:S(2)}, u32[]{:S(2)}) %collective-permute-start.1) | collective-permute-done | bytes 196640 | tf_op jit(solution)/shard_map/ppermute | solution.py:22
  19.7 3.0 %shard_map.92 = (bf16[2,192,128]{2,1,0:T(8,128)(2,1)S(1)}, bf16[1,5,96,384]{3,2,1,0:T(8,128)(2,1)S(1)}, bf16[3,7,192,384]{3,2,1,0:T(8,128)(2,1)S(1)}) custom-call(f32[8,128]{1,0:T(8,128)S(1)} %stack.7.flag_ref, bf16[4,4,192,128]{3,2,1,0:T(8,128)(2,1)S(1)} %copy-done.2, bf16[4,2,192,128]{3,2,1,0:T(8,128)(2,1)S(1)} %collective-permute-done.5.pair_ref, ...), custom_call_target="tpu_custom_call" | custom-call | flops 962592768 | bytes 7796224 | tf_op jit(solution)/shard_map/pallas_call | solution.py:351
  22.7 1.4 %collective-permute-start.8 = (bf16[2,192,128]{2,1,0:T(8,128)(2,1)S(1)}, bf16[2,192,128]{2,1,0:T(8,128)(2,1)S(1)}, u32[]{:S(2)}, u32[]{:S(2)}) collective-permute-start(bf16[2,192,128]{2,1,0:T(8,128)(2,1)S(1)} %get-tuple-element.35.own_ref), channel_id=1, source_target_pairs={{0,8},{4,12},{8,16},{12,20},{16,24},{20,28},{24,0},{28,4},{1,9},{5... | collective-permute-start | bytes 294920 | tf_op jit(solution)/shard_map/ppermute | solution.py:22
  24.1 0.4 collective-permute-start.4
  24.6 3.2 %collective-permute-done.4.wanted_ref = f32[8,128]{1,0:T(8,128)S(1)} collective-permute-done((f32[8,128]{1,0:T(8,128)S(1)}, f32[8,128]{1,0:T(8,128)S(1)}, u32[]{:S(2)}, u32[]{:S(2)}) %collective-permute-start.4) | collective-permute-done | bytes 4128 | tf_op jit(solution)/shard_map/ppermute | solution.py:39
  27.8 0.5 %collective-permute-start.7 = (bf16[4,192,128]{2,1,0:T(8,128)(2,1)S(1)}, bf16[4,192,128]{2,1,0:T(8,128)(2,1)S(1)}, u32[]{:S(2)}, u32[]{:S(2)}) collective-permute-start(bf16[4,192,128]{2,1,0:T(8,128)(2,1)S(1)} %shard_map.93), channel_id=1, source_target_pairs={{0,4},{4,0},{8,12},{12,8},{16,20},{20,16},{24,28},{28,24},{1,5},{5... | collective-permute-start | bytes 589832 | tf_op jit(solution)/shard_map/ppermute | solution.py:39
  28.4 1.6 %collective-permute-start.9 = (bf16[4,192,128]{2,1,0:T(8,128)(2,1)S(1)}, bf16[4,192,128]{2,1,0:T(8,128)(2,1)S(1)}, u32[]{:S(2)}, u32[]{:S(2)}) collective-permute-start(bf16[4,192,128]{2,1,0:T(8,128)(2,1)S(1)} %shard_map.94), channel_id=1, source_target_pairs={{0,4},{4,0},{8,12},{12,8},{16,20},{20,16},{24,28},{28,24},{1,5},{5... | collective-permute-start | bytes 589832 | tf_op jit(solution)/shard_map/ppermute | solution.py:39
  30.1 2.8 %shard_map.95 = (f32[192,256]{1,0:T(8,128)S(1)}, bf16[1,7,192,384]{3,2,1,0:T(8,128)(2,1)S(1)}) custom-call(f32[8,128]{1,0:T(8,128)S(1)} %stack.7.flag_ref, bf16[4,4,192,128]{3,2,1,0:T(8,128)(2,1)S(1)} %copy-done.3, bf16[4,2,192,128]{3,2,1,0:T(8,128)(2,1)S(1)} %collective-permute-done.5.pair_ref, ...), custom_call_target="tpu_custom_call" | custom-call | flops 3000000000 | bytes 8927744 | tf_op jit(solution)/shard_map/pallas_call | solution.py:351
  32.9 4.1 %collective-permute-done.9.odd1_ref = bf16[4,192,128]{2,1,0:T(8,128)(2,1)S(1)} collective-permute-done((bf16[4,192,128]{2,1,0:T(8,128)(2,1)S(1)}, bf16[4,192,128]{2,1,0:T(8,128)(2,1)S(1)}, u32[]{:S(2)}, u32[]{:S(2)}) %collective-permute-start.9) | collective-permute-done | bytes 196640 | tf_op jit(solution)/shard_map/ppermute | solution.py:39
  37.0 0.2 shard_map.96
  37.3 1.2 %collective-permute-start.11 = (bf16[2,2,192,128]{3,2,1,0:T(8,128)(2,1)S(1)}, bf16[2,2,192,128]{3,2,1,0:T(8,128)(2,1)S(1)}, u32[]{:S(2)}, u32[]{:S(2)}) collective-permute-start(bf16[2,2,192,128]{3,2,1,0:T(8,128)(2,1)S(1)} %get-tuple-element.46), channel_id=1, source_target_pairs={{0,3},{1,2},{2,1},{3,0},{4,7},{5,6},{6,5},{7,4},{8,16},{9,10},{10,... | collective-permute-start | bytes 589832 | tf_op jit(solution)/shard_map/ppermute | solution.py:56
  38.5 1.1 %collective-permute-start.13 = (bf16[2,192,128]{2,1,0:T(8,128)(2,1)S(1)}, bf16[2,192,128]{2,1,0:T(8,128)(2,1)S(1)}, u32[]{:S(2)}, u32[]{:S(2)}) collective-permute-start(bf16[2,192,128]{2,1,0:T(8,128)(2,1)S(1)} %shard_map.99), channel_id=1, source_target_pairs={{0,4},{4,0},{8,12},{12,8},{16,20},{20,16},{24,28},{28,24},{1,5},{5... | collective-permute-start | bytes 294920 | tf_op jit(solution)/shard_map/ppermute | solution.py:39
  39.6 1.4 %shard_map.97 = (f32[5,192,128]{2,1,0:T(8,128)S(1)}, f32[5,192,128]{2,1,0:T(8,128)S(1)}) custom-call(f32[8,128]{1,0:T(8,128)S(1)} %stack.7.flag_ref, bf16[4,4,192,128]{3,2,1,0:T(8,128)(2,1)S(1)} %copy-done.3, bf16[4,2,192,128]{3,2,1,0:T(8,128)(2,1)S(1)} %collective-permute-done.5.pair_ref, bf16[4,2,192,128]{3,2,1,0:T(8,128)(2,1)S(1)} %collective-permute-done.6.cross_ref, ...), custom_call_target="tpu_custom_call" | custom-call | flops 200000000 | bytes 7574016 | tf_op jit(solution)/shard_map/pallas_call | solution.py:351
  41.0 1.6 %shard_map.98 = (f32[5,192,128]{2,1,0:T(8,128)S(1)}, f32[5,192,128]{2,1,0:T(8,128)S(1)}, bf16[2,5,96,384]{3,2,1,0:T(8,128)(2,1)S(1)}) custom-call(f32[8,128]{1,0:T(8,128)S(1)} %stack.7.flag_ref, bf16[2,4,192,128]{3,2,1,0:T(8,128)(2,1)S(1)} %get-tuple-element.44.prior_ref, f32[1,128]{1,0:T(1,128)S(1)} %bitcast.20, bf16[3,3,384,128]{3,2,1,0:T(8,128)(2,1)S(1)} %bitcast.13, ...), custom_call_target="tpu_custom_call" | custom-call | flops 566231040 | bytes 3986432 | tf_op jit(solution)/shard_map/pallas_call | solution.py:351
  42.6 0.7 %collective-permute-done.13.odd_ref = bf16[2,192,128]{2,1,0:T(8,128)(2,1)S(1)} collective-permute-done((bf16[2,192,128]{2,1,0:T(8,128)(2,1)S(1)}, bf16[2,192,128]{2,1,0:T(8,128)(2,1)S(1)}, u32[]{:S(2)}, u32[]{:S(2)}) %collective-permute-start.13) | collective-permute-done | bytes 98336 | tf_op jit(solution)/shard_map/ppermute | solution.py:39
  43.3 0.7 %collective-permute-done.11.cross_ref = bf16[2,2,192,128]{3,2,1,0:T(8,128)(2,1)S(1)} collective-permute-done((bf16[2,2,192,128]{3,2,1,0:T(8,128)(2,1)S(1)}, bf16[2,2,192,128]{3,2,1,0:T(8,128)(2,1)S(1)}, u32[]{:S(2)}, u32[]{:S(2)}) %collective-permute-start.11) | collective-permute-done | bytes 196640 | tf_op jit(solution)/shard_map/ppermute | solution.py:56
  44.0 2.0 %shard_map.100 = bf16[2,2,96,256]{3,2,1,0:T(8,128)(2,1)} custom-call(f32[8,128]{1,0:T(8,128)S(1)} %stack.7.flag_ref, bf16[2,4,192,128]{3,2,1,0:T(8,128)(2,1)S(1)} %get-tuple-element.44.prior_ref, bf16[2,2,192,128]{3,2,1,0:T(8,128)(2,1)S(1)} %collective-permute-done.10.pair_ref, bf16[2,2,192,128]{3,2,1,0:T(8,128)(2,1)S(1)} %collective-permute-done.11.cross_ref, ...), custom_call_target="tpu_custom_call" | custom-call | flops 622854144 | bytes 5855232 | tf_op jit(solution)/shard_map/pallas_call | solution.py:351
  (39 shorter events, 0.4 us)
Async XLA Ops:
  1.4 1.1 %copy-start.2 = (bf16[4,4,192,128]{3,2,1,0:T(8,128)(2,1)S(1)}, bf16[4,4,192,128]{3,2,1,0:T(8,128)(2,1)}, u32[]{:S(2)}) copy-start(bf16[4,4,192,128]{3,2,1,0:T(8,128)(2,1)} %video_ref.7) | copy-start | bytes 2359300
  2.6 17.1 %copy-start = (bf16[3,3,3,128,128]{4,3,2,1,0:T(8,128)(2,1)S(1)}, bf16[3,3,3,128,128]{4,3,2,1,0:T(8,128)(2,1)}, u32[]{:S(2)}) copy-start(bf16[3,3,3,128,128]{4,3,2,1,0:T(8,128)(2,1)} %param.13) | copy-start | bytes 2654212
  2.6 17.1 %copy-start.1 = (bf16[3,3,3,128,256]{4,3,2,1,0:T(8,128)(2,1)S(1)}, bf16[3,3,3,128,256]{4,3,2,1,0:T(8,128)(2,1)}, u32[]{:S(2)}) copy-start(bf16[3,3,3,128,256]{4,3,2,1,0:T(8,128)(2,1)} %param.16) | copy-start | bytes 5308420
  2.6 17.1 %copy-start.4 = (f32[128]{0:T(128)S(1)}, f32[128]{0:T(128)}, u32[]{:S(2)}) copy-start(f32[128]{0:T(128)} %param.12) | copy-start | bytes 1540
  2.6 17.1 %copy-start.5 = (f32[128]{0:T(128)S(1)}, f32[128]{0:T(128)}, u32[]{:S(2)}) copy-start(f32[128]{0:T(128)} %param.15) | copy-start | bytes 1540
  2.6 17.1 %copy-start.6 = (f32[128]{0:T(128)S(1)}, f32[128]{0:T(128)}, u32[]{:S(2)}) copy-start(f32[128]{0:T(128)} %param.14) | copy-start | bytes 1540
  2.7 27.3 %copy-start.3 = (bf16[4,4,192,128]{3,2,1,0:T(8,128)(2,1)S(1)}, bf16[4,4,192,128]{3,2,1,0:T(8,128)(2,1)}, u32[]{:S(2)}) copy-start(bf16[4,4,192,128]{3,2,1,0:T(8,128)(2,1)} %video_ref.7) | copy-start | bytes 2359300
  2.8 27.3 %copy-start.7 = (f32[256]{0:T(256)S(1)}, f32[256]{0:T(256)}, u32[]{:S(2)}) copy-start(f32[256]{0:T(256)} %param.17) | copy-start | bytes 3076
  2.8 16.8 %collective-permute-start.5 = (bf16[4,2,192,128]{3,2,1,0:T(8,128)(2,1)S(1)}, bf16[4,2,192,128]{3,2,1,0:T(8,128)(2,1)S(1)}, u32[]{:S(2)}, u32[]{:S(2)}) collective-permute-start(bf16[4,2,192,128]{3,2,1,0:T(8,128)(2,1)S(1)} %get-tuple-element.31), channel_id=1, source_target_pairs={{0,1},{1,0},{2,3},{3,2},{4,5},{5,4},{6,7},{7,6},{8,9},{9,8},{10,11... | collective-permute-start | bytes 1179656 | tf_op jit(solution)/shard_map/ppermute | solution.py:39
  3.3 16.3 %collective-permute-start.6 = (bf16[4,2,192,128]{3,2,1,0:T(8,128)(2,1)S(1)}, bf16[4,2,192,128]{3,2,1,0:T(8,128)(2,1)S(1)}, u32[]{:S(2)}, u32[]{:S(2)}) collective-permute-start(bf16[4,2,192,128]{3,2,1,0:T(8,128)(2,1)S(1)} %get-tuple-element.32), channel_id=1, source_target_pairs={{0,4},{1,2},{2,1},{3,7},{4,0},{5,6},{6,5},{7,3},{8,12},{9,10},{10,... | collective-permute-start | bytes 1179656 | tf_op jit(solution)/shard_map/ppermute | solution.py:67
  5.9 9.5 %collective-permute-start = (bf16[4,192,128]{2,1,0:T(8,128)(2,1)S(1)}, bf16[4,192,128]{2,1,0:T(8,128)(2,1)S(1)}, u32[]{:S(2)}, u32[]{:S(2)}) collective-permute-start(bf16[4,192,128]{2,1,0:T(8,128)(2,1)S(1)} %get-tuple-element.29.own_ref), channel_id=1, source_target_pairs={{0,8},{4,12},{8,16},{12,20},{16,24},{20,28},{24,0},{28,4},{1,9},{5... | collective-permute-start | bytes 589832 | tf_op jit(solution)/shard_map/ppermute | solution.py:22
  7.4 12.2 %collective-permute-start.1 = (bf16[4,192,128]{2,1,0:T(8,128)(2,1)S(1)}, bf16[4,192,128]{2,1,0:T(8,128)(2,1)S(1)}, u32[]{:S(2)}, u32[]{:S(2)}) collective-permute-start(bf16[4,192,128]{2,1,0:T(8,128)(2,1)S(1)} %get-tuple-element.30.own_ref), channel_id=1, source_target_pairs={{0,8},{4,12},{8,16},{12,20},{16,24},{20,28},{24,0},{28,4},{1,9},{5... | collective-permute-start | bytes 589832 | tf_op jit(solution)/shard_map/ppermute | solution.py:22
  15.4 9.2 %collective-permute-start.2 = (bf16[4,192,128]{2,1,0:T(8,128)(2,1)S(1)}, bf16[4,192,128]{2,1,0:T(8,128)(2,1)S(1)}, u32[]{:S(2)}, u32[]{:S(2)}) collective-permute-start(bf16[4,192,128]{2,1,0:T(8,128)(2,1)S(1)} %collective-permute-done.near_ref.two0_ref), channel_id=1, source_target_pairs={{0,1},{1,0},{2,3},{3,2},{4,5},{5,4},{6,7},{7,6},{8,16},{9,17},{10,... | collective-permute-start | bytes 589832 | tf_op jit(solution)/shard_map/ppermute | solution.py:35
  19.6 8.7 %collective-permute-start.3 = (bf16[4,192,128]{2,1,0:T(8,128)(2,1)S(1)}, bf16[4,192,128]{2,1,0:T(8,128)(2,1)S(1)}, u32[]{:S(2)}, u32[]{:S(2)}) collective-permute-start(bf16[4,192,128]{2,1,0:T(8,128)(2,1)S(1)} %collective-permute-done.1.near_ref.two1_ref), channel_id=1, source_target_pairs={{0,1},{1,0},{2,3},{3,2},{4,5},{5,4},{6,7},{7,6},{8,16},{9,17},{10,... | collective-permute-start | bytes 589832 | tf_op jit(solution)/shard_map/ppermute | solution.py:35
  22.7 7.3 %collective-permute-start.8 = (bf16[2,192,128]{2,1,0:T(8,128)(2,1)S(1)}, bf16[2,192,128]{2,1,0:T(8,128)(2,1)S(1)}, u32[]{:S(2)}, u32[]{:S(2)}) collective-permute-start(bf16[2,192,128]{2,1,0:T(8,128)(2,1)S(1)} %get-tuple-element.35.own_ref), channel_id=1, source_target_pairs={{0,8},{4,12},{8,16},{12,20},{16,24},{20,28},{24,0},{28,4},{1,9},{5... | collective-permute-start | bytes 294920 | tf_op jit(solution)/shard_map/ppermute | solution.py:22
  24.1 3.6 %collective-permute-start.4 = (f32[8,128]{1,0:T(8,128)S(1)}, f32[8,128]{1,0:T(8,128)S(1)}, u32[]{:S(2)}, u32[]{:S(2)}) collective-permute-start(f32[8,128]{1,0:T(8,128)S(1)} %broadcast_in_dim.15), channel_id=1, source_target_pairs={{0,4},{4,0},{8,12},{12,8},{16,20},{20,16},{24,28},{28,24},{1,5},{5... | collective-permute-start | bytes 12296 | tf_op jit(solution)/shard_map/ppermute | solution.py:39
  27.8 9.2 %collective-permute-start.7 = (bf16[4,192,128]{2,1,0:T(8,128)(2,1)S(1)}, bf16[4,192,128]{2,1,0:T(8,128)(2,1)S(1)}, u32[]{:S(2)}, u32[]{:S(2)}) collective-permute-start(bf16[4,192,128]{2,1,0:T(8,128)(2,1)S(1)} %shard_map.93), channel_id=1, source_target_pairs={{0,4},{4,0},{8,12},{12,8},{16,20},{20,16},{24,28},{28,24},{1,5},{5... | collective-permute-start | bytes 589832 | tf_op jit(solution)/shard_map/ppermute | solution.py:39
  28.4 8.6 %collective-permute-start.9 = (bf16[4,192,128]{2,1,0:T(8,128)(2,1)S(1)}, bf16[4,192,128]{2,1,0:T(8,128)(2,1)S(1)}, u32[]{:S(2)}, u32[]{:S(2)}) collective-permute-start(bf16[4,192,128]{2,1,0:T(8,128)(2,1)S(1)} %shard_map.94), channel_id=1, source_target_pairs={{0,4},{4,0},{8,12},{12,8},{16,20},{20,16},{24,28},{28,24},{1,5},{5... | collective-permute-start | bytes 589832 | tf_op jit(solution)/shard_map/ppermute | solution.py:39
  30.0 8.4 %collective-permute-start.12 = (bf16[2,192,128]{2,1,0:T(8,128)(2,1)S(1)}, bf16[2,192,128]{2,1,0:T(8,128)(2,1)S(1)}, u32[]{:S(2)}, u32[]{:S(2)}) collective-permute-start(bf16[2,192,128]{2,1,0:T(8,128)(2,1)S(1)} %collective-permute-done.8.near_ref.two_ref), channel_id=1, source_target_pairs={{0,1},{1,0},{2,3},{3,2},{4,5},{5,4},{6,7},{7,6},{8,16},{9,17},{10,... | collective-permute-start | bytes 294920 | tf_op jit(solution)/shard_map/ppermute | solution.py:35
  37.2 6.1 %collective-permute-start.10 = (bf16[2,2,192,128]{3,2,1,0:T(8,128)(2,1)S(1)}, bf16[2,2,192,128]{3,2,1,0:T(8,128)(2,1)S(1)}, u32[]{:S(2)}, u32[]{:S(2)}) collective-permute-start(bf16[2,2,192,128]{3,2,1,0:T(8,128)(2,1)S(1)} %get-tuple-element.45), channel_id=1, source_target_pairs={{0,1},{1,0},{2,3},{3,2},{4,5},{5,4},{6,7},{7,6},{8,9},{9,8},{10,11... | collective-permute-start | bytes 589832 | tf_op jit(solution)/shard_map/ppermute | solution.py:39
  37.3 6.7 %collective-permute-start.11 = (bf16[2,2,192,128]{3,2,1,0:T(8,128)(2,1)S(1)}, bf16[2,2,192,128]{3,2,1,0:T(8,128)(2,1)S(1)}, u32[]{:S(2)}, u32[]{:S(2)}) collective-permute-start(bf16[2,2,192,128]{3,2,1,0:T(8,128)(2,1)S(1)} %get-tuple-element.46), channel_id=1, source_target_pairs={{0,3},{1,2},{2,1},{3,0},{4,7},{5,6},{6,5},{7,4},{8,16},{9,10},{10,... | collective-permute-start | bytes 589832 | tf_op jit(solution)/shard_map/ppermute | solution.py:56
  38.5 4.8 %collective-permute-start.13 = (bf16[2,192,128]{2,1,0:T(8,128)(2,1)S(1)}, bf16[2,192,128]{2,1,0:T(8,128)(2,1)S(1)}, u32[]{:S(2)}, u32[]{:S(2)}) collective-permute-start(bf16[2,192,128]{2,1,0:T(8,128)(2,1)S(1)} %shard_map.99), channel_id=1, source_target_pairs={{0,4},{4,0},{8,12},{12,8},{16,20},{20,16},{24,28},{28,24},{1,5},{5... | collective-permute-start | bytes 294920 | tf_op jit(solution)/shard_map/ppermute | solution.py:39
